TPU v7x, 32 devices: a whole 2x2x4 slice. The times are simulated.
32 devices in a mesh: ctx: 8 (over y, x, core), tp: 4 (over z).
Axes of the slice: x: 2, y: 2, z: 4, core: 2. Of those that a mesh axis runs over, the one named last changes fastest.
Arguments:
- block_in: bfloat16 [4096, 2048], P(('ctx', 'tp')), may hold values from -6 to 6
- out_grad: bfloat16 [4096, 2048], P(('ctx', 'tp')), may hold values from -6 to 6
- pair_slot: int32 [8], replicated, may hold values from 0 to 7, each once
- gain_attn: bfloat16 [2048], P('ctx'), may hold values from 0.099609375 to 1.8984375
- wq: bfloat16 [2048, 2048], P('ctx', 'tp'), may hold values from -0.125 to 0.125
- wk: bfloat16 [2048, 512], P('ctx', 'tp'), may hold values from -0.125 to 0.125
- wv: bfloat16 [2048, 512], P('ctx', 'tp'), may hold values from -0.125 to 0.125
- wo: bfloat16 [2048, 2048], P('ctx', 'tp'), may hold values from -2 to 2
- gain_mlp: bfloat16 [2048], P('ctx'), may hold values from 0.099609375 to 1.8984375
- w_gate: bfloat16 [2048, 8192], P('ctx', 'tp'), may hold values from -0.125 to 0.125
- w_up: bfloat16 [2048, 8192], P('ctx', 'tp'), may hold values from -0.125 to 0.125
- w_down: bfloat16 [2048, 8192], P('ctx', 'tp'), may hold values from -0.0625 to 0.0625
Outputs:
- block_out: bfloat16 [4096, 2048], P(('ctx', 'tp'))
- input_grad: float32 [4096, 2048], P(('ctx', 'tp'))
- grad_gain_attn: float32 [2048], P('ctx')
- grad_wq: float32 [2048, 2048], P('ctx', 'tp')
- grad_wk: float32 [2048, 512], P('ctx', 'tp')
- grad_wv: float32 [2048, 512], P('ctx', 'tp')
- grad_wo: float32 [2048, 2048], P('ctx', 'tp')
- grad_gain_mlp: float32 [2048], P('ctx')
- grad_w_gate: float32 [2048, 8192], P('ctx', 'tp')
- grad_w_up: float32 [2048, 8192], P('ctx', 'tp')
- grad_w_down: float32 [2048, 8192], P('ctx', 'tp')
Inputs may be any that keep to these rules, and one draw needn't show every extreme that they name: `pair_slot`: each of 0 to 7 appears once.
All inputs are finite; a program needn't handle non-finite values.
Results may differ from a plain program's by a relative error of at most 0.024.
Values may be sent and summed in bfloat16 or wider, within the bound.
No kernel may reach another device: no remote copies, remote signals or barrier semaphores. Data moves between devices by JAX's collectives and lax.ppermute only.
A program may use at most 256 MiB of HBM per device.

v0:
```python
import math

import jax
import jax.numpy as jnp
from jax import lax
from jax.sharding import PartitionSpec as P

HEAD_SIZE = 64


eps_norm = 1e-05
big_negative = -1e30


def block_positions(pair_slot, block_len):
    pair_count = pair_slot.shape[0]
    offsets = jnp.arange(2 * block_len, dtype=jnp.int32)
    lower_half = offsets < block_len
    block_index = jnp.where(
        lower_half[None, :], pair_slot[:, None], 2 * pair_count - 1 - pair_slot[:, None]
    )
    return (block_index * block_len + (offsets % block_len)[None, :]).reshape(-1)


def inverse_freqs(head_dim):
    exponent = jnp.arange(0, head_dim, 2).astype(jnp.float32) / head_dim
    base_freq = 500000.0 ** (-exponent)
    wavelength = 2.0 * math.pi / base_freq
    smooth = (8192.0 / wavelength - 1.0) / 3.0
    blended = (1.0 - smooth) * base_freq / 32.0 + smooth * base_freq
    scaled = jnp.where(wavelength > 8192.0, base_freq / 32.0, base_freq)
    middle = (wavelength >= 2048.0) & (wavelength <= 8192.0)
    return jnp.where(middle, blended, scaled)


def rope_tables(positions, head_dim):
    angles = positions.astype(jnp.float32)[:, None] * inverse_freqs(head_dim)[None, :]
    doubled = jnp.concatenate([angles, angles], axis=1)
    return (jnp.cos(doubled), jnp.sin(doubled))


def apply_rotation(values, cosine_table, sine_table):
    half_dim = values.shape[-1] // 2
    turned = jnp.concatenate([-values[..., half_dim:], values[..., :half_dim]], axis=-1)
    return values * cosine_table[:, None, :] + turned * sine_table[:, None, :]


def rotate_back(gradient, cosine_table, sine_table):
    half_dim = gradient.shape[-1] // 2
    sined = gradient * sine_table[:, None, :]
    return gradient * cosine_table[:, None, :] + jnp.concatenate(
        [sined[..., half_dim:], -sined[..., :half_dim]], axis=-1
    )


def rms_scale(values):
    return lax.rsqrt(jnp.mean(values * values, axis=-1, keepdims=True) + eps_norm)


def norm_back(gradient, normed, factor):
    return factor * (gradient - normed * jnp.mean(gradient * normed, axis=-1, keepdims=True))


def times_t(left, right):
    return lax.dot_general(
        left, right, (((1,), (1,)), ((), ())), preferred_element_type=jnp.float32
    )


def inner_rows(left, right):
    return lax.dot_general(
        left, right, (((0,), (0,)), ((), ())), preferred_element_type=jnp.float32
    )


def tile_scores(heads_of_query, key_tile, pos_tile, pos_rows):
    score_scale = HEAD_SIZE ** (-0.5)
    scores = (
        jnp.einsum("qgrd,kgd->grqk", heads_of_query, key_tile, preferred_element_type=jnp.float32)
        * score_scale
    )
    visible = pos_tile[None, :] <= pos_rows[:, None]
    return (scores, visible)


def tile_count(pos_rows, tile_len):
    return pos_rows[-1] // tile_len + 1


def block_forward(heads_of_query, pos_rows, key_tiles, value_tiles, pos_tiles):
    rows, heads_kv, repeat_heads, _ = heads_of_query.shape
    count = tile_count(pos_rows, key_tiles.shape[1])

    def stat_step(index, running):
        run_max, run_sum = running
        scores, visible = tile_scores(heads_of_query, key_tiles[index], pos_tiles[index], pos_rows)
        scores = jnp.where(visible, scores, big_negative)
        new_max = jnp.maximum(run_max, jnp.max(scores, axis=-1))
        weights = jnp.where(visible, jnp.exp(scores - new_max[..., None]), 0.0)
        run_sum = run_sum * jnp.exp(run_max - new_max) + jnp.sum(weights, axis=-1)
        return (new_max, run_sum)

    start_max = jnp.full((heads_kv, repeat_heads, rows), big_negative, jnp.float32)
    start_sum = jnp.zeros((heads_kv, repeat_heads, rows), jnp.float32)
    row_max, row_sum = lax.fori_loop(0, count, stat_step, (start_max, start_sum))
    log_total = row_max + jnp.log(row_sum)

    def value_step(index, accum):
        scores, visible = tile_scores(heads_of_query, key_tiles[index], pos_tiles[index], pos_rows)
        weights = jnp.where(visible, jnp.exp(scores - log_total[..., None]), 0.0).astype(
            jnp.bfloat16
        )
        return accum + jnp.einsum(
            "grqk,kgd->qgrd", weights, value_tiles[index], preferred_element_type=jnp.float32
        )

    start_out = jnp.zeros((rows, heads_kv, repeat_heads, HEAD_SIZE), jnp.float32)
    attended = lax.fori_loop(0, count, value_step, start_out)
    return (attended, log_total)


def sequence_order(keys_all, values_all, pos_all, tile_len, heads_kv):
    seq_len = pos_all.shape[0]
    order = jnp.zeros((seq_len,), jnp.int32).at[pos_all].set(jnp.arange(seq_len, dtype=jnp.int32))
    key_tiles = keys_all[order].reshape(-1, tile_len, heads_kv, HEAD_SIZE)
    value_tiles = values_all[order].reshape(-1, tile_len, heads_kv, HEAD_SIZE)
    pos_tiles = jnp.arange(seq_len, dtype=jnp.int32).reshape(-1, tile_len)
    return (key_tiles, value_tiles, pos_tiles)


def attention_forward(queries, key_tiles, value_tiles, pos_tiles, pos_rows, heads_kv):
    group_rows = queries.shape[0]
    half_rows = group_rows // 2
    heads_of_query = queries.reshape(group_rows, heads_kv, -1, HEAD_SIZE)
    low_out, low_total = block_forward(
        heads_of_query[:half_rows], pos_rows[:half_rows], key_tiles, value_tiles, pos_tiles
    )
    high_out, high_total = block_forward(
        heads_of_query[half_rows:], pos_rows[half_rows:], key_tiles, value_tiles, pos_tiles
    )
    attended = jnp.concatenate([low_out, high_out], axis=0)
    log_total = jnp.concatenate([low_total, high_total], axis=-1)
    return (attended.reshape(group_rows, -1), log_total)


def block_backward(
    heads_of_query,
    grad_heads,
    row_dot,
    log_total,
    pos_rows,
    key_tiles,
    value_tiles,
    pos_tiles,
    buffers,
):
    score_scale = HEAD_SIZE ** (-0.5)
    tile_len = key_tiles.shape[1]
    count = tile_count(pos_rows, tile_len)

    def back_step(index, carry):
        grad_query, key_buffer, value_buffer = carry
        key_tile = key_tiles[index]
        scores, visible = tile_scores(heads_of_query, key_tile, pos_tiles[index], pos_rows)
        weights = jnp.where(visible, jnp.exp(scores - log_total[..., None]), 0.0)
        grad_weights = jnp.einsum(
            "qgrd,kgd->grqk", grad_heads, value_tiles[index], preferred_element_type=jnp.float32
        )
        grad_scores = (weights * (grad_weights - row_dot[..., None])).astype(jnp.bfloat16)
        grad_value = jnp.einsum(
            "grqk,qgrd->kgd",
            weights.astype(jnp.bfloat16),
            grad_heads,
            preferred_element_type=jnp.float32,
        )
        grad_key = (
            jnp.einsum(
                "grqk,qgrd->kgd", grad_scores, heads_of_query, preferred_element_type=jnp.float32
            )
            * score_scale
        )
        grad_query = grad_query + jnp.einsum(
            "grqk,kgd->qgrd", grad_scores, key_tile, preferred_element_type=jnp.float32
        )
        key_buffer = key_buffer.at[index].add(grad_key)
        value_buffer = value_buffer.at[index].add(grad_value)
        return (grad_query, key_buffer, value_buffer)

    start_grad = jnp.zeros(heads_of_query.shape, jnp.float32)
    return lax.fori_loop(0, count, back_step, (start_grad, buffers[0], buffers[1]))


def attention_backward(
    queries,
    key_tiles,
    value_tiles,
    pos_tiles,
    grad_attended,
    row_dot,
    log_total,
    pos_rows,
    pos_all,
    heads_kv,
):
    group_rows = queries.shape[0]
    half_rows = group_rows // 2
    score_scale = HEAD_SIZE ** (-0.5)
    heads_of_query = queries.reshape(group_rows, heads_kv, -1, HEAD_SIZE)
    grad_heads = grad_attended.reshape(group_rows, heads_kv, -1, HEAD_SIZE)
    buffers = (jnp.zeros(key_tiles.shape, jnp.float32), jnp.zeros(value_tiles.shape, jnp.float32))
    low_query, key_buffer, value_buffer = block_backward(
        heads_of_query[:half_rows],
        grad_heads[:half_rows],
        row_dot[..., :half_rows],
        log_total[..., :half_rows],
        pos_rows[:half_rows],
        key_tiles,
        value_tiles,
        pos_tiles,
        buffers,
    )
    high_query, key_buffer, value_buffer = block_backward(
        heads_of_query[half_rows:],
        grad_heads[half_rows:],
        row_dot[..., half_rows:],
        log_total[..., half_rows:],
        pos_rows[half_rows:],
        key_tiles,
        value_tiles,
        pos_tiles,
        (key_buffer, value_buffer),
    )
    grad_query = jnp.concatenate([low_query, high_query], axis=0)
    width_kv = heads_kv * HEAD_SIZE
    seq_len = pos_all.shape[0]
    grad_key = key_buffer.reshape(seq_len, width_kv)[pos_all]
    grad_value = value_buffer.reshape(seq_len, width_kv)[pos_all]
    return (grad_query.reshape(group_rows, -1) * score_scale, grad_key, grad_value)


def on_device(
    block_in, out_grad, pair_slot, gain_attn, wq, wk, wv, wo, gain_mlp, w_gate, w_up, w_down
):
    local_rows = block_in.shape[0]
    group_rows = local_rows * lax.axis_size("tp")
    block_len = group_rows // 2
    tile_len = 2 * group_rows
    gathered = (
        lax.all_gather(gain_attn, "ctx", axis=0, tiled=True),
        lax.all_gather(wq, "ctx", axis=0, tiled=True),
        lax.all_gather(wk, "ctx", axis=0, tiled=True),
        lax.all_gather(wv, "ctx", axis=0, tiled=True),
        lax.all_gather(wo, "ctx", axis=0, tiled=True),
        lax.all_gather(gain_mlp, "ctx", axis=0, tiled=True),
        lax.all_gather(w_gate, "ctx", axis=0, tiled=True),
        lax.all_gather(w_up, "ctx", axis=0, tiled=True),
        lax.all_gather(w_down, "ctx", axis=0, tiled=True),
    )
    g_attn = gathered[0].astype(jnp.float32)
    q_w, k_w, v_w, o_w = (gathered[1], gathered[2], gathered[3], gathered[4])
    g_mlp = gathered[5].astype(jnp.float32)
    gate_w, up_w, down_w = (gathered[6], gathered[7], gathered[8])
    heads_kv = k_w.shape[1] // HEAD_SIZE
    pos_all = block_positions(pair_slot, block_len)
    pos_rows = lax.dynamic_slice_in_dim(pos_all, lax.axis_index("ctx") * group_rows, group_rows)
    cosine_table, sine_table = rope_tables(pos_rows, HEAD_SIZE)
    inputs = block_in.astype(jnp.float32)
    factor_attn = rms_scale(inputs)
    normed_attn = inputs * factor_attn
    attn_in = lax.all_gather((normed_attn * g_attn).astype(jnp.bfloat16), "tp", axis=0, tiled=True)
    query_raw = jnp.dot(attn_in, q_w, preferred_element_type=jnp.float32)
    key_unrotated = jnp.dot(attn_in, k_w, preferred_element_type=jnp.float32)
    values = jnp.dot(attn_in, v_w, preferred_element_type=jnp.float32).astype(jnp.bfloat16)
    queries = (
        apply_rotation(query_raw.reshape(group_rows, -1, HEAD_SIZE), cosine_table, sine_table)
        .reshape(group_rows, -1)
        .astype(jnp.bfloat16)
    )
    rows_of_key = (
        apply_rotation(key_unrotated.reshape(group_rows, -1, HEAD_SIZE), cosine_table, sine_table)
        .reshape(group_rows, -1)
        .astype(jnp.bfloat16)
    )
    keys_all, values_all = (
        lax.all_gather(rows_of_key, "ctx", axis=0, tiled=True),
        lax.all_gather(values, "ctx", axis=0, tiled=True),
    )
    key_tiles, value_tiles, pos_tiles = sequence_order(
        keys_all, values_all, pos_all, tile_len, heads_kv
    )
    attended_exact, log_total = attention_forward(
        queries, key_tiles, value_tiles, pos_tiles, pos_rows, heads_kv
    )
    attended = attended_exact.astype(jnp.bfloat16)
    residual = inputs + lax.psum_scatter(
        times_t(attended, o_w).astype(jnp.bfloat16), "tp", scatter_dimension=0, tiled=True
    ).astype(jnp.float32)
    factor_mlp = rms_scale(residual)
    normed_mlp = residual * factor_mlp
    mlp_in = lax.all_gather((normed_mlp * g_mlp).astype(jnp.bfloat16), "tp", axis=0, tiled=True)
    gate_proj = jnp.dot(mlp_in, gate_w, preferred_element_type=jnp.float32)
    up_proj = jnp.dot(mlp_in, up_w, preferred_element_type=jnp.float32)
    sigmoid_gate = jax.nn.sigmoid(gate_proj)
    silu_gate = gate_proj * sigmoid_gate
    hidden = (silu_gate * up_proj).astype(jnp.bfloat16)
    mlp_out = lax.psum_scatter(
        times_t(hidden, down_w).astype(jnp.bfloat16), "tp", scatter_dimension=0, tiled=True
    ).astype(jnp.float32)
    block_out = (residual + mlp_out).astype(jnp.bfloat16)
    grad_rows = lax.all_gather(out_grad, "tp", axis=0, tiled=True)
    grad_down = inner_rows(grad_rows, hidden)
    grad_hidden = jnp.dot(grad_rows, down_w, preferred_element_type=jnp.float32)
    grad_gate = (
        grad_hidden * up_proj * sigmoid_gate * (1.0 + gate_proj * (1.0 - sigmoid_gate))
    ).astype(jnp.bfloat16)
    grad_up = (grad_hidden * silu_gate).astype(jnp.bfloat16)
    grad_gate_w = inner_rows(mlp_in, grad_gate)
    grad_up_w = inner_rows(mlp_in, grad_up)
    grad_mlp_in = lax.psum_scatter(
        (times_t(grad_gate, gate_w) + times_t(grad_up, up_w)).astype(jnp.bfloat16),
        "tp",
        scatter_dimension=0,
        tiled=True,
    ).astype(jnp.float32)
    gain_mlp_part = jnp.sum(grad_mlp_in * normed_mlp, axis=0)
    grad_residual = out_grad.astype(jnp.float32) + norm_back(
        grad_mlp_in * g_mlp, normed_mlp, factor_mlp
    )
    branch_rows = lax.all_gather(grad_residual.astype(jnp.bfloat16), "tp", axis=0, tiled=True)
    grad_o_w = inner_rows(branch_rows, attended)
    grad_attended = jnp.dot(branch_rows, o_w, preferred_element_type=jnp.float32).astype(
        jnp.bfloat16
    )
    row_dot = jnp.sum(
        (grad_attended.astype(jnp.float32) * attended_exact).reshape(
            group_rows, heads_kv, -1, HEAD_SIZE
        ),
        axis=-1,
    )
    row_dot = jnp.transpose(row_dot, (1, 2, 0))
    grad_query_rot, grad_key_part, grad_value_part = attention_backward(
        queries,
        key_tiles,
        value_tiles,
        pos_tiles,
        grad_attended,
        row_dot,
        log_total,
        pos_rows,
        pos_all,
        heads_kv,
    )
    grad_key_rot, grad_value_sum = (
        lax.psum_scatter(
            grad_key_part.astype(jnp.bfloat16), "ctx", scatter_dimension=0, tiled=True
        ).astype(jnp.float32),
        lax.psum_scatter(
            grad_value_part.astype(jnp.bfloat16), "ctx", scatter_dimension=0, tiled=True
        ).astype(jnp.float32),
    )
    grad_queries = (
        rotate_back(grad_query_rot.reshape(group_rows, -1, HEAD_SIZE), cosine_table, sine_table)
        .reshape(group_rows, -1)
        .astype(jnp.bfloat16)
    )
    grad_keys = (
        rotate_back(grad_key_rot.reshape(group_rows, -1, HEAD_SIZE), cosine_table, sine_table)
        .reshape(group_rows, -1)
        .astype(jnp.bfloat16)
    )
    grad_values = grad_value_sum.astype(jnp.bfloat16)
    grad_q_w = inner_rows(attn_in, grad_queries)
    grad_k_w = inner_rows(attn_in, grad_keys)
    grad_v_w = inner_rows(attn_in, grad_values)
    grad_attn_part = (
        times_t(grad_queries, q_w) + times_t(grad_keys, k_w) + times_t(grad_values, v_w)
    )
    grad_attn_in = lax.psum_scatter(
        grad_attn_part.astype(jnp.bfloat16), "tp", scatter_dimension=0, tiled=True
    ).astype(jnp.float32)
    gain_attn_part = jnp.sum(grad_attn_in * normed_attn, axis=0)
    input_grad = grad_residual + norm_back(grad_attn_in * g_attn, normed_attn, factor_attn)
    all_sums = (
        lax.psum_scatter(
            gain_attn_part.astype(jnp.bfloat16), "ctx", scatter_dimension=0, tiled=True
        ).astype(jnp.float32),
        lax.psum_scatter(
            grad_q_w.astype(jnp.bfloat16), "ctx", scatter_dimension=0, tiled=True
        ).astype(jnp.float32),
        lax.psum_scatter(
            grad_k_w.astype(jnp.bfloat16), "ctx", scatter_dimension=0, tiled=True
        ).astype(jnp.float32),
        lax.psum_scatter(
            grad_v_w.astype(jnp.bfloat16), "ctx", scatter_dimension=0, tiled=True
        ).astype(jnp.float32),
        lax.psum_scatter(
            grad_o_w.astype(jnp.bfloat16), "ctx", scatter_dimension=0, tiled=True
        ).astype(jnp.float32),
        lax.psum_scatter(
            gain_mlp_part.astype(jnp.bfloat16), "ctx", scatter_dimension=0, tiled=True
        ).astype(jnp.float32),
        lax.psum_scatter(
            grad_gate_w.astype(jnp.bfloat16), "ctx", scatter_dimension=0, tiled=True
        ).astype(jnp.float32),
        lax.psum_scatter(
            grad_up_w.astype(jnp.bfloat16), "ctx", scatter_dimension=0, tiled=True
        ).astype(jnp.float32),
        lax.psum_scatter(
            grad_down.astype(jnp.bfloat16), "ctx", scatter_dimension=0, tiled=True
        ).astype(jnp.float32),
    )
    gain_attn_sum, sum_q_w, sum_k_w, sum_v_w, sum_o_w = (
        all_sums[0],
        all_sums[1],
        all_sums[2],
        all_sums[3],
        all_sums[4],
    )
    gain_mlp_sum, sum_gate_w, sum_up_w, sum_down_w = (
        all_sums[5],
        all_sums[6],
        all_sums[7],
        all_sums[8],
    )
    total_attn_gain, total_mlp_gain = lax.psum((gain_attn_sum, gain_mlp_sum), "tp")
    return (
        block_out,
        input_grad,
        total_attn_gain,
        sum_q_w,
        sum_k_w,
        sum_v_w,
        sum_o_w,
        total_mlp_gain,
        sum_gate_w,
        sum_up_w,
        sum_down_w,
    )


def solution(mesh):
    placed = (
        P(("ctx", "tp"), None),
        P(("ctx", "tp"), None),
        P(),
        P("ctx"),
        P("ctx", "tp"),
        P("ctx", "tp"),
        P("ctx", "tp"),
        P("ctx", "tp"),
        P("ctx"),
        P("ctx", "tp"),
        P("ctx", "tp"),
        P("ctx", "tp"),
    )
    return jax.shard_map(
        on_device,
        mesh=mesh,
        in_specs=placed,
        out_specs=(
            P(("ctx", "tp"), None),
            P(("ctx", "tp"), None),
            P("ctx"),
            P("ctx", "tp"),
            P("ctx", "tp"),
            P("ctx", "tp"),
            P("ctx", "tp"),
            P("ctx"),
            P("ctx", "tp"),
            P("ctx", "tp"),
            P("ctx", "tp"),
        ),
        check_vma=False,
    )
```

profile of v0, /device:TPU:2, one launch (start us, length us, event | category | flops | bytes accessed | tf_op | source)
XLA Modules:
  0.0 1308.4 jit_solution(12839793133745210811)
XLA Ops:
  7.9 8.9 all-gather
  22.5 9.2 all_gather.49
  32.6 33.9 %all-gather.14.cloned.1.call-done = bf16[512,2048]{1,0:T(8,128)(2,1)} async-done(((bf16[128,2048]{1,0:T(8,128)(2,1)}), bf16[512,2048]{1,0:T(8,128)(2,1)}) %all-gather.14.cloned.1.call-update) | async-done | bytes 2097168 | tf_op jit(solution)/shard_map/all_gather | solution.py:270
  69.9 11.2 all_gather.47
  89.0 15.5 %scatter_custom_fusion = s32[4096]{0:T(1024)S(1)} fusion(s32[4096]{0:T(1024)S(1)} %bitcast.564, s32[4096]{0:T(1024)S(1)} %iota.46, s32[]{:T(128)} %constant.232.clone.1), kind=kCustom, calls=%fused_computation.220 | custom fusion | bytes 16388 | tf_op jit(solution)/shard_map/scatter | solution.py:124
  108.2 12.9 all-gather.18.cloned.1.call-done
  122.7 12.1 gather_fusion.1
  141.4 7.5 while.76
  149.0 12.4 gather_fusion
  163.2 5.9 copy.83
  169.1 7.4 while.77
  176.6 11.3 while.78
  187.9 10.9 while.79
  204.6 9.3 all-gather.1
  213.9 36.3 %reduce-scatter.14.cloned.1.call-done = bf16[128,2048]{1,0:T(8,128)(2,1)} async-done(((bf16[512,2048]{1,0:T(8,128)(2,1)}), bf16[128,2048]{1,0:T(8,128)(2,1)}) %reduce-scatter.14.cloned.1.call-update) | async-done | bytes 524304 | tf_op jit(solution)/shard_map/reduce_scatter | solution.py:295
  256.7 42.3 %all-gather.24.cloned.1.call-done = bf16[512,2048]{1,0:T(8,128)(2,1)} async-done(((bf16[128,2048]{1,0:T(8,128)(2,1)}), bf16[512,2048]{1,0:T(8,128)(2,1)}) %all-gather.24.cloned.1.call-update) | async-done | bytes 2097168 | tf_op jit(solution)/shard_map/all_gather | solution.py:300
  299.0 55.2 %all-gather.26.cloned.1.call-done = bf16[2048,2048]{1,0:T(8,128)(2,1)} async-done(((bf16[256,2048]{1,0:T(8,128)(2,1)}), bf16[2048,2048]{1,0:T(8,128)(2,1)}) %all-gather.26.cloned.1.call-update) | async-done | bytes 8388624 | tf_op jit(solution)/shard_map/all_gather | solution.py:255
  354.2 10.6 fusion.182
  364.8 45.9 %all-gather.28.cloned.1.call-done = bf16[2048,2048]{1,0:T(8,128)(2,1)} async-done(((bf16[256,2048]{1,0:T(8,128)(2,1)}), bf16[2048,2048]{1,0:T(8,128)(2,1)}) %all-gather.28.cloned.1.call-update) | async-done | bytes 8388624 | tf_op jit(solution)/shard_map/all_gather | solution.py:256
  410.6 10.5 fusion.183
  421.1 37.0 %all-gather.32.cloned.1.call-done = bf16[512,2048]{1,0:T(8,128)(2,1)} async-done(((bf16[128,2048]{1,0:T(8,128)(2,1)}), bf16[512,2048]{1,0:T(8,128)(2,1)}) %all-gather.32.cloned.1.call-update) | async-done | bytes 2097168 | tf_op jit(solution)/shard_map/all_gather | solution.py:310
  458.1 55.2 %all-gather.30.cloned.1.call-done = bf16[2048,2048]{1,0:T(8,128)(2,1)} async-done(((bf16[256,2048]{1,0:T(8,128)(2,1)}), bf16[2048,2048]{1,0:T(8,128)(2,1)}) %all-gather.30.cloned.1.call-update) | async-done | bytes 8388624 | tf_op jit(solution)/shard_map/all_gather | solution.py:257
  513.3 14.2 %multiply_convert_fusion = (bf16[512,2048]{1,0:T(8,128)(2,1)}, bf16[512,2048]{1,0:T(8,128)(2,1)S(1)}, bf16[512,2048]{1,0:T(8,128)(2,1)}) fusion(f32[512,2048]{1,0:T(8,128)} %fusion.182, f32[512,2048]{1,0:T(8,128)} %fusion.183, bf16[512,2048]{1,0:T(8,128)(2,1)} %all-gather.32.cloned.1.call-done, bf16[2048,2048]{1,0:T(8,128)(2,1)} %all-gather.30.cloned.1.call-done), kind=kOutput, calls=%fused_computation.138 | convolution fusion | flops 4310695936 | bytes 25165824 | tf_op jit(solution)/shard_map/dot_general | solution.py:312
  527.5 8.3 fusion.184
  535.8 7.5 add_convert_fusion.1
  543.3 44.0 %reduce-scatter.18.cloned.1.call-done = bf16[128,2048]{1,0:T(8,128)(2,1)} async-done(((bf16[512,2048]{1,0:T(8,128)(2,1)}), bf16[128,2048]{1,0:T(8,128)(2,1)}) %reduce-scatter.18.cloned.1.call-update) | async-done | bytes 524304 | tf_op jit(solution)/shard_map/reduce_scatter | solution.py:319
  591.9 45.3 %all-gather.34.cloned.1.call-done = bf16[512,2048]{1,0:T(8,128)(2,1)} async-done(((bf16[128,2048]{1,0:T(8,128)(2,1)}), bf16[512,2048]{1,0:T(8,128)(2,1)}) %all-gather.34.cloned.1.call-update) | async-done | bytes 2097168 | tf_op jit(solution)/shard_map/all_gather | solution.py:329
  645.1 28.9 %while.80 = (s32[]{:T(128)}, f32[256,2,4,64]{0,3,2,1:T(8,128)S(1)}, f32[4,1024,2,64]{1,3,2,0:T(8,128)}, f32[4,1024,2,64]{1,3,2,0:T(8,128)}, s32[]{:T(128)}, /*in...) while((s32[]{:T(128)}, f32[256,2,4,64]{0,3,2,1:T(8,128)S(1)}, ...), condition=%wide.region_22.23_spmd, body=%wide.region_20.22_spmd.sunk | while | flops 1364197376 | bytes 44604684 | solution.py:190
  674.8 42.7 %while.81 = (s32[]{:T(128)}, f32[256,2,4,64]{0,3,2,1:T(8,128)S(1)}, f32[4,1024,2,64]{1,3,2,0:T(8,128)}, f32[4,1024,2,64]{1,3,2,0:T(8,128)}, s32[]{:T(128)}, /*in...) while((s32[]{:T(128)}, f32[256,2,4,64]{0,3,2,1:T(8,128)S(1)}, ...), condition=%wide.region_25.26_spmd, body=%wide.region_23.25_spmd.sunk | while | flops 1364197376 | bytes 44604684 | solution.py:190
  717.5 6.6 copy.120
  728.0 12.1 gather_fusion.2
  747.7 15.0 %gather_fusion.3 = bf16[4096,128]{1,0:T(8,128)(2,1)} fusion(bf16[4096,128]{1,0:T(8,128)(2,1)S(1)} %reshape.520, s32[4096]{0:T(1024)S(1)} %broadcast_clamp_fusion), kind=kCustom, calls=%fused_computation.3 | custom fusion | bytes 2113536 | tf_op jit(solution)/shard_map/gather | solution.py:237
  762.8 13.6 %reduce-scatter.20.cloned.1.call-done = bf16[512,128]{0,1:T(8,128)(2,1)} async-done(((bf16[4096,128]{0,1:T(8,128)(2,1)}), bf16[512,128]{0,1:T(8,128)(2,1)}) %reduce-scatter.20.cloned.1.call-update) | async-done | bytes 131088 | tf_op jit(solution)/shard_map/reduce_scatter | solution.py:354
  779.9 36.1 %reduce-scatter.22.cloned.1.call-done = bf16[512,128]{1,0:T(8,128)(2,1)} async-done(((bf16[4096,128]{1,0:T(8,128)(2,1)}), bf16[512,128]{1,0:T(8,128)(2,1)}) %reduce-scatter.22.cloned.1.call-update) | async-done | bytes 131088 | tf_op jit(solution)/shard_map/reduce_scatter | solution.py:357
  828.1 10.1 convolution_convert_fusion.1
  839.8 8.4 convolution_convert_fusion
  849.8 8.4 convert_bitcast_fusion
  864.5 9.3 convolution_convert_fusion.4
  876.6 14.4 %reduce-scatter.30.cloned.1.call-done = bf16[256,128]{1,0:T(8,128)(2,1)} async-done(((bf16[2048,128]{1,0:T(8,128)(2,1)}), bf16[256,128]{1,0:T(8,128)(2,1)}) %reduce-scatter.30.cloned.1.call-update) | async-done | bytes 65552 | tf_op jit(solution)/shard_map/reduce_scatter | solution.py:393
  892.5 43.4 %reduce-scatter.32.cloned.1.call-done = bf16[256,512]{1,0:T(8,128)(2,1)} async-done(((bf16[2048,512]{1,0:T(8,128)(2,1)}), bf16[256,512]{1,0:T(8,128)(2,1)}) %reduce-scatter.32.cloned.1.call-update) | async-done | bytes 262160 | tf_op jit(solution)/shard_map/reduce_scatter | solution.py:396
  937.8 43.7 %reduce-scatter.26.cloned.1.call-done = bf16[256,512]{1,0:T(8,128)(2,1)} async-done(((bf16[2048,512]{1,0:T(8,128)(2,1)}), bf16[256,512]{1,0:T(8,128)(2,1)}) %reduce-scatter.26.cloned.1.call-update) | async-done | bytes 262160 | tf_op jit(solution)/shard_map/reduce_scatter | solution.py:387
  983.2 72.8 %reduce-scatter.34.cloned.1.call-done = bf16[256,2048]{1,0:T(8,128)(2,1)} async-done(((bf16[2048,2048]{1,0:T(8,128)(2,1)}), bf16[256,2048]{1,0:T(8,128)(2,1)}) %reduce-scatter.34.cloned.1.call-update) | async-done | bytes 1048592 | tf_op jit(solution)/shard_map/reduce_scatter | solution.py:402
  1058.8 72.4 %reduce-scatter.36.cloned.1.call-done = bf16[256,2048]{1,0:T(8,128)(2,1)} async-done(((bf16[2048,2048]{1,0:T(8,128)(2,1)}), bf16[256,2048]{1,0:T(8,128)(2,1)}) %reduce-scatter.36.cloned.1.call-update) | async-done | bytes 1048592 | tf_op jit(solution)/shard_map/reduce_scatter | solution.py:405
  1134.0 72.0 %reduce-scatter.38.cloned.1.call-done = bf16[256,2048]{0,1:T(8,128)(2,1)} async-done(((bf16[2048,2048]{0,1:T(8,128)(2,1)}), bf16[256,2048]{0,1:T(8,128)(2,1)}) %reduce-scatter.38.cloned.1.call-update) | async-done | bytes 1048592 | tf_op jit(solution)/shard_map/reduce_scatter | solution.py:408
  1208.5 43.8 %reduce-scatter.24.cloned.1.call-done = bf16[128,2048]{1,0:T(8,128)(2,1)} async-done(((bf16[512,2048]{1,0:T(8,128)(2,1)}), bf16[128,2048]{1,0:T(8,128)(2,1)}) %reduce-scatter.24.cloned.1.call-update) | async-done | bytes 524304 | tf_op jit(solution)/shard_map/reduce_scatter | solution.py:378
  1253.8 11.1 all-reduce.3
  1265.0 11.1 all-reduce.2
  1276.1 21.9 %reduce-scatter.16.cloned.1.call-done = bf16[128,2048]{1,0:T(8,128)(2,1)} async-done(((bf16[512,2048]{1,0:T(8,128)(2,1)}), bf16[128,2048]{1,0:T(8,128)(2,1)}) %reduce-scatter.16.cloned.1.call-update) | async-done | bytes 524304 | tf_op jit(solution)/shard_map/reduce_scatter | solution.py:306
  (350 shorter events, 216.1 us)
Async XLA Ops:
  7.2 59.3 %all-gather.14.cloned.1.call-start = ((), (), s32[]{:S(2)}) async-start(), calls=%async_computation.13 | async-start | bytes 2621440 | tf_op jit(solution)/shard_map/all_gather | solution.py:270
  16.8 53.1 %copy-start.35 = (bf16[256,128]{1,0:T(8,128)(2,1)S(1)}, bf16[256,128]{1,0:T(8,128)(2,1)}, u32[]{:S(2)}) copy-start(bf16[256,128]{1,0:T(8,128)(2,1)} %param.38) | copy-start | bytes 196612
  20.1 84.5 %all-gather.20.cloned.1.call-start = ((), (), s32[]{:S(2)}) async-start(), calls=%async_computation.16 | async-start | bytes 2359296 | tf_op jit(solution)/shard_map/all_gather | solution.py:250
  20.9 100.2 %all-gather.18.cloned.1.call-start = ((), (), s32[]{:S(2)}) async-start(), calls=%async_computation.15 | async-start | bytes 1179648 | tf_op jit(solution)/shard_map/all_gather | solution.py:285
  31.6 50.8 %copy-start.13 = (bf16[2048,128]{1,0:T(8,128)(2,1)}, bf16[2048,128]{1,0:T(8,128)(2,1)S(1)}, u32[]{:S(2)}) copy-start(bf16[2048,128]{1,0:T(8,128)(2,1)S(1)} %all_gather.49) | copy-start | bytes 1572868
  32.6 75.1 %copy-start.22 = (f32[512,64]{0,1:T(8,128)}, f32[512,64]{0,1:T(8,128)S(1)}, u32[]{:S(2)}) copy-start(f32[512,64]{0,1:T(8,128)S(1)} %get-tuple-element.760) | copy-start | bytes 393220
  32.6 75.3 %copy-start.20 = (f32[512,64]{0,1:T(8,128)}, f32[512,64]{0,1:T(8,128)S(1)}, u32[]{:S(2)}) copy-start(f32[512,64]{0,1:T(8,128)S(1)} %get-tuple-element.761) | copy-start | bytes 393220
  69.9 79.1 %all-gather.16.cloned.1.call-start = ((), (), s32[]{:S(2)}) async-start(), calls=%async_computation.14 | async-start | bytes 1179648 | tf_op jit(solution)/shard_map/all_gather | solution.py:286
  81.1 26.5 %copy-start.15 = (bf16[2048,128]{1,0:T(8,128)(2,1)}, bf16[2048,128]{1,0:T(8,128)(2,1)S(1)}, u32[]{:S(2)}) copy-start(bf16[2048,128]{1,0:T(8,128)(2,1)S(1)} %all_gather.47) | copy-start | bytes 1572868
  82.5 117.5 %all-gather.22.cloned.1.call-start = ((), (), s32[]{:S(2)}) async-start(), calls=%async_computation.17 | async-start | bytes 2359296 | tf_op jit(solution)/shard_map/all_gather | solution.py:253
  83.1 167.1 %reduce-scatter.14.cloned.1.call-start = ((), (), s32[]{:S(2)}) async-start(), calls=%async_computation.18 | async-start | bytes 2621440 | tf_op jit(solution)/shard_map/reduce_scatter | solution.py:295
  200.0 50.2 %copy-start.2 = (bf16[128,2048]{1,0:T(8,128)(2,1)S(1)}, bf16[128,2048]{1,0:T(8,128)(2,1)}, u32[]{:S(2)}) copy-start(bf16[128,2048]{1,0:T(8,128)(2,1)} %param.32) | copy-start | bytes 1572868
  204.5 94.5 %all-gather.24.cloned.1.call-start = ((), (), s32[]{:S(2)}) async-start(), calls=%async_computation.19 | async-start | bytes 2621440 | tf_op jit(solution)/shard_map/all_gather | solution.py:300
  213.8 375.6 %copy-start.31 = (f32[8,1,256]{2,1,0:T(1,128)}, f32[8,1,256]{2,1,0:T(1,128)S(1)}, u32[]{:S(2)}) copy-start(f32[8,1,256]{2,1,0:T(1,128)S(1)} %convert_element_type.229) | copy-start | bytes 24580
  251.5 338.0 %copy-start.40 = (f32[128]{0:T(128)}, f32[128]{0:T(128)S(1)}, u32[]{:S(2)}) copy-start(f32[128]{0:T(128)S(1)} %add_rsqrt_fusion) | copy-start | bytes 1540
  253.6 100.6 %all-gather.26.cloned.1.call-start = ((), (), s32[]{:S(2)}) async-start(), calls=%async_computation.20 | async-start | bytes 9437184 | tf_op jit(solution)/shard_map/all_gather | solution.py:255
  254.3 156.3 %all-gather.28.cloned.1.call-start = ((), (), s32[]{:S(2)}) async-start(), calls=%async_computation.21 | async-start | bytes 9437184 | tf_op jit(solution)/shard_map/all_gather | solution.py:256
  255.1 203.0 %all-gather.32.cloned.1.call-start = ((), (), s32[]{:S(2)}) async-start(), calls=%async_computation.24 | async-start | bytes 2621440 | tf_op jit(solution)/shard_map/all_gather | solution.py:310
  255.7 257.6 %all-gather.30.cloned.1.call-start = ((), (), s32[]{:S(2)}) async-start(), calls=%async_computation.22 | async-start | bytes 9437184 | tf_op jit(solution)/shard_map/all_gather | solution.py:257
  256.4 330.9 %reduce-scatter.18.cloned.1.call-start = ((), (), s32[]{:S(2)}) async-start(), calls=%async_computation.25 | async-start | bytes 2621440 | tf_op jit(solution)/shard_map/reduce_scatter | solution.py:319
  535.8 51.5 %copy-start.8 = (bf16[128,2048]{1,0:T(8,128)(2,1)S(1)}, bf16[128,2048]{1,0:T(8,128)(2,1)}, u32[]{:S(2)}) copy-start(bf16[128,2048]{1,0:T(8,128)(2,1)} %reduce-scatter.14.cloned.1.call-done) | copy-start | bytes 1572868
  535.8 53.7 %copy-start.10 = (bf16[128,2048]{1,0:T(8,128)(2,1)S(1)}, bf16[128,2048]{1,0:T(8,128)(2,1)}, u32[]{:S(2)}) copy-start(bf16[128,2048]{1,0:T(8,128)(2,1)} %param.33) | copy-start | bytes 1572868
  543.3 48.6 %copy-start.37 = (s32[4096,1]{0,1:T(1,128)S(1)}, s32[4096,1]{0,1:T(1,128)}, u32[]{:S(2)}) copy-start(s32[4096,1]{0,1:T(1,128)} %copy-done.36) | copy-start | bytes 49156
  543.3 93.9 %all-gather.34.cloned.1.call-start = ((), (), s32[]{:S(2)}) async-start(), calls=%async_computation.26 | async-start | bytes 2621440 | tf_op jit(solution)/shard_map/all_gather | solution.py:329
  591.8 184.5 %reduce-scatter.20.cloned.1.call-start = ((), (), s32[]{:S(2)}) async-start(), calls=%async_computation.27 | async-start | bytes 1179648 | tf_op jit(solution)/shard_map/reduce_scatter | solution.py:354
  741.5 74.5 %reduce-scatter.22.cloned.1.call-start = ((), (), s32[]{:S(2)}) async-start(), calls=%async_computation.28 | async-start | bytes 1179648 | tf_op jit(solution)/shard_map/reduce_scatter | solution.py:357
  747.6 28.7 %copy-start.23 = (f32[512,64]{0,1:T(8,128)S(1)}, f32[512,64]{0,1:T(8,128)}, u32[]{:S(2)}) copy-start(f32[512,64]{0,1:T(8,128)} %copy-done.22) | copy-start | bytes 393220
  747.6 29.7 %copy-start.21 = (f32[512,64]{0,1:T(8,128)S(1)}, f32[512,64]{0,1:T(8,128)}, u32[]{:S(2)}) copy-start(f32[512,64]{0,1:T(8,128)} %copy-done.20) | copy-start | bytes 393220
  747.6 30.6 %copy-start.1 = (bf16[512,2048]{1,0:T(8,128)(2,1)S(1)}, bf16[512,2048]{1,0:T(8,128)(2,1)}, u32[]{:S(2)}) copy-start(bf16[512,2048]{1,0:T(8,128)(2,1)} %all-gather.14.cloned.1.call-done) | copy-start | bytes 6291460
  762.7 112.4 %reduce-scatter.28.cloned.1.call-start = ((), (), s32[]{:S(2)}) async-start(), calls=%async_computation.31 | async-start | bytes 589824 | tf_op jit(solution)/shard_map/reduce_scatter | solution.py:390
  779.9 111.1 %reduce-scatter.30.cloned.1.call-start = ((), (), s32[]{:S(2)}) async-start(), calls=%async_computation.32 | async-start | bytes 589824 | tf_op jit(solution)/shard_map/reduce_scatter | solution.py:393
  818.5 117.5 %reduce-scatter.32.cloned.1.call-start = ((), (), s32[]{:S(2)}) async-start(), calls=%async_computation.33 | async-start | bytes 2359296 | tf_op jit(solution)/shard_map/reduce_scatter | solution.py:396
  822.9 158.5 %reduce-scatter.26.cloned.1.call-start = ((), (), s32[]{:S(2)}) async-start(), calls=%async_computation.30 | async-start | bytes 2359296 | tf_op jit(solution)/shard_map/reduce_scatter | solution.py:387
  828.1 228.0 %reduce-scatter.34.cloned.1.call-start = ((), (), s32[]{:S(2)}) async-start(), calls=%async_computation.34 | async-start | bytes 9437184 | tf_op jit(solution)/shard_map/reduce_scatter | solution.py:402
  838.3 292.9 %reduce-scatter.36.cloned.1.call-start = ((), (), s32[]{:S(2)}) async-start(), calls=%async_computation.35 | async-start | bytes 9437184 | tf_op jit(solution)/shard_map/reduce_scatter | solution.py:405
  848.3 357.7 %reduce-scatter.38.cloned.1.call-start = ((), (), s32[]{:S(2)}) async-start(), calls=%async_computation.36 | async-start | bytes 9437184 | tf_op jit(solution)/shard_map/reduce_scatter | solution.py:408
  858.3 394.1 %reduce-scatter.24.cloned.1.call-start = ((), (), s32[]{:S(2)}) async-start(), calls=%async_computation.29 | async-start | bytes 2621440 | tf_op jit(solution)/shard_map/reduce_scatter | solution.py:378
  864.5 433.5 %reduce-scatter.16.cloned.1.call-start = ((), (), s32[]{:S(2)}) async-start(), calls=%async_computation.23 | async-start | bytes 2621440 | tf_op jit(solution)/shard_map/reduce_scatter | solution.py:306
  983.2 269.1 %copy-start.3 = (bf16[128,2048]{1,0:T(8,128)(2,1)S(1)}, bf16[128,2048]{1,0:T(8,128)(2,1)}, u32[]{:S(2)}) copy-start(bf16[128,2048]{1,0:T(8,128)(2,1)} %param.32) | copy-start | bytes 1572868
  983.2 269.1 %copy-start.34 = (f32[8,1,256]{2,1,0:T(1,128)S(1)}, f32[8,1,256]{2,1,0:T(1,128)}, u32[]{:S(2)}) copy-start(f32[8,1,256]{2,1,0:T(1,128)} %copy-done.33) | copy-start | bytes 24580
  983.2 269.1 %copy-start.43 = (f32[128]{0:T(128)S(1)}, f32[128]{0:T(128)}, u32[]{:S(2)}) copy-start(f32[128]{0:T(128)} %copy-done.42) | copy-start | bytes 1540
  1058.8 195.0 %copy-start.39 = (bf16[2048]{0:T(1024)(128)(2,1)S(1)}, bf16[2048]{0:T(1024)(128)(2,1)}, u32[]{:S(2)}) copy-start(bf16[2048]{0:T(1024)(128)(2,1)} %get-tuple-element.608) | copy-start | bytes 12292
  1058.8 239.1 %copy-start.9 = (bf16[128,2048]{1,0:T(8,128)(2,1)S(1)}, bf16[128,2048]{1,0:T(8,128)(2,1)}, u32[]{:S(2)}) copy-start(bf16[128,2048]{1,0:T(8,128)(2,1)} %reduce-scatter.14.cloned.1.call-done) | copy-start | bytes 1572868
  1058.8 239.1 %copy-start.11 = (bf16[128,2048]{1,0:T(8,128)(2,1)S(1)}, bf16[128,2048]{1,0:T(8,128)(2,1)}, u32[]{:S(2)}) copy-start(bf16[128,2048]{1,0:T(8,128)(2,1)} %param.33) | copy-start | bytes 1572868
  1058.8 239.2 %copy-start.12 = (bf16[128,2048]{1,0:T(8,128)(2,1)S(1)}, bf16[128,2048]{1,0:T(8,128)(2,1)}, u32[]{:S(2)}) copy-start(bf16[128,2048]{1,0:T(8,128)(2,1)} %reduce-scatter.18.cloned.1.call-done) | copy-start | bytes 1572868
  1058.8 239.1 %copy-start.32 = (f32[8,1,256]{2,1,0:T(1,128)S(1)}, f32[8,1,256]{2,1,0:T(1,128)}, u32[]{:S(2)}) copy-start(f32[8,1,256]{2,1,0:T(1,128)} %copy-done.31) | copy-start | bytes 24580
  1058.8 239.1 %copy-start.41 = (f32[128]{0:T(128)S(1)}, f32[128]{0:T(128)}, u32[]{:S(2)}) copy-start(f32[128]{0:T(128)} %copy-done.40) | copy-start | bytes 1540
  1058.8 239.1 %copy-start.45 = (f32[128]{0:T(128)S(1)}, f32[128]{0:T(128)}, u32[]{:S(2)}) copy-start(f32[128]{0:T(128)} %copy-done.44) | copy-start | bytes 1540
  (32 other events, 143.8 us)
Sparse Core Ops, SparseCore 0:
  20.2 46.2 all-gather.13
  68.4 26.6 all-gather.19
  97.5 23.5 all-gather.17
  123.4 23.4 all-gather.15
  148.7 27.9 all-gather.21
  204.6 45.5 reduce-scatter.13
  253.7 45.2 all-gather.23
  301.0 53.0 all-gather.25
  356.2 54.3 all-gather.27
  412.1 45.9 all-gather.31
  460.2 53.0 all-gather.29
  543.4 43.8 reduce-scatter.17
  591.9 45.2 all-gather.33
  741.6 34.6 reduce-scatter.19
  779.9 36.0 reduce-scatter.21
  819.5 34.0 reduce-scatter.27
  856.8 34.1 reduce-scatter.29
  894.7 41.1 reduce-scatter.31
  940.2 41.2 reduce-scatter.25
  984.7 71.2 reduce-scatter.33
  1059.9 71.2 reduce-scatter.35
  1134.7 71.2 reduce-scatter.37
  1208.4 43.9 reduce-scatter.23
  1254.5 43.4 reduce-scatter.15
where the time goes:
time: 1320 us; the launch traced here: 1310 us
  waiting for transfers between devices  846 us (64%)
  matrix products  207 us (16%)
  local copies, waits for them, and re-layouts  118 us (9%)
  blocking collectives  60.7 us (5%)
  other arithmetic  51.7 us (4%)
  between operations  21.7 us (2%)
    reduce_scatter x1, waiting for transfers between devices, on_device(): lax.psum_scatter(grad_gate_w.astype(jnp.bfloat16), 'ctx', scatter_dimensi...  72.8 us
    reduce_scatter x1, waiting for transfers between devices, on_device(): lax.psum_scatter(grad_up_w.astype(jnp.bfloat16), 'ctx', scatter_dimension...  72.4 us
    reduce_scatter x1, waiting for transfers between devices, on_device(): lax.psum_scatter(grad_down.astype(jnp.bfloat16), 'ctx', scatter_dimension...  72 us
    all_gather x1, waiting for transfers between devices, on_device(): lax.all_gather(w_down, 'ctx', axis=0, tiled=True)  55.2 us
    all_gather x1, waiting for transfers between devices, on_device(): lax.all_gather(w_gate, 'ctx', axis=0, tiled=True)  55.2 us
    all_gather x1, waiting for transfers between devices, on_device(): lax.all_gather(w_up, 'ctx', axis=0, tiled=True)  45.9 us
    all_gather x1, waiting for transfers between devices, on_device(): lax.all_gather(grad_residual.astype(jnp.bfloat16), 'tp', axis=0, tiled=True)  45.3 us
    reduce_scatter x1, waiting for transfers between devices, on_device(): lax.psum_scatter((times_t(grad_gate, gate_w) + times_t(grad_up, up_w)).as...  44 us
  transfers between devices with their start and end apart: 24, of which 20 were waited for; matrix products, arithmetic and copies ran while one was open for 17% of the time, Pallas kernels for 0%

commit v1 on v0

v1 whole, which is shorter than its diff:
```python
import functools
import math

import jax
import jax.numpy as jnp
from jax import lax
from jax.experimental import pallas as pl
from jax.experimental.pallas import tpu as pltpu
from jax.sharding import PartitionSpec as P

HEAD_SIZE = 64
LANES = 128
KERNEL_VMEM = 56 * 1024 * 1024

eps_norm = 1e-05
big_negative = -1e30

in_smem = pl.BlockSpec(memory_space=pltpu.SMEM)
in_vmem = pl.BlockSpec(memory_space=pltpu.VMEM)


def kernel_params():
    return pltpu.CompilerParams(vmem_limit_bytes=KERNEL_VMEM)


def cost(flops, moved):
    return pl.CostEstimate(flops=int(flops), bytes_accessed=int(moved), transcendentals=0)


def bit_order(bits):
    return [1, 2, 0] + list(range(3, bits)) if bits >= 3 else list(range(bits))


def block_key(position, bits):
    key = 0
    for place, bit in enumerate(bit_order(bits)):
        key = key | (((position >> place) & 1) << bit)
    return key


def key_position(key, bits):
    position = 0
    for place, bit in enumerate(bit_order(bits)):
        position = position | (((key >> bit) & 1) << place)
    return position


def swap(array, bit, bits):
    return lax.ppermute(array, "ctx", [(i, i ^ (1 << bit)) for i in range(1 << bits)])


def gather_ctx(own, bits, axis=0):
    first, second = bit_order(bits)[:2]
    middle = own.shape[axis] // 2
    by_first = swap(own, first, bits)
    by_second = swap(own, second, bits)
    lower = lax.slice_in_dim(by_first, 0, middle, axis=axis)
    upper = lax.slice_in_dim(by_second, middle, 2 * middle, axis=axis)
    both_lower = swap(lower, second, bits)
    both_upper = swap(upper, first, bits)
    parts = [jnp.concatenate([own, by_first, by_second, both_lower, both_upper], axis=axis)]
    for bit in bit_order(bits)[2:]:
        parts = parts + [swap(part, bit, bits) for part in parts]
    return parts


def scatter_pieces(parts, bits):
    for bit in reversed(bit_order(bits)[2:]):
        kept = len(parts) // 2
        received = [swap(part, bit, bits) for part in parts[kept:]]
        parts = [
            (mine.astype(jnp.float32) + other.astype(jnp.float32)).astype(jnp.bfloat16)
            for mine, other in zip(parts[:kept], received)
        ]
    first, second = bit_order(bits)[:2]
    own, at_first, at_second, at_both = jnp.split(parts[0], 4, axis=0)
    middle = own.shape[0] // 2
    lower = swap(at_both[:middle], second, bits)
    upper = swap(at_both[middle:], first, bits)
    to_first = jnp.concatenate([at_first[:middle] + lower, at_first[middle:]], axis=0)
    to_second = jnp.concatenate([at_second[:middle], at_second[middle:] + upper], axis=0)
    return own, swap(to_first, first, bits), swap(to_second, second, bits)


def scatter_ctx(parts, bits):
    own, by_first, by_second = scatter_pieces(parts, bits)
    return own.astype(jnp.float32) + by_first.astype(jnp.float32) + by_second.astype(jnp.float32)


def to_relative(array, me, bits):
    width = array.shape[1] // (1 << bits)
    return jnp.concatenate(
        [
            lax.dynamic_slice_in_dim(array, (me ^ block_key(p, bits)) * width, width, 1)
            for p in range(1 << bits)
        ],
        axis=1,
    )


def to_absolute(array, me, bits):
    width = array.shape[1] // (1 << bits)
    return jnp.concatenate(
        [
            lax.dynamic_slice_in_dim(array, key_position(me ^ c, bits) * width, width, 1)
            for c in range(1 << bits)
        ],
        axis=1,
    )


def block_positions(pair_slot, block_len):
    pair_count = pair_slot.shape[0]
    offsets = jnp.arange(2 * block_len, dtype=jnp.int32)
    lower_half = offsets < block_len
    block_index = jnp.where(
        lower_half[None, :], pair_slot[:, None], 2 * pair_count - 1 - pair_slot[:, None]
    )
    return (block_index * block_len + (offsets % block_len)[None, :]).reshape(-1)


def inverse_freqs(head_dim):
    exponent = jnp.arange(0, head_dim, 2).astype(jnp.float32) / head_dim
    base_freq = 500000.0 ** (-exponent)
    wavelength = 2.0 * math.pi / base_freq
    smooth = (8192.0 / wavelength - 1.0) / 3.0
    blended = (1.0 - smooth) * base_freq / 32.0 + smooth * base_freq
    scaled = jnp.where(wavelength > 8192.0, base_freq / 32.0, base_freq)
    middle = (wavelength >= 2048.0) & (wavelength <= 8192.0)
    return jnp.where(middle, blended, scaled)


def rope_tables(positions):
    angles = positions.astype(jnp.float32)[:, None] * inverse_freqs(HEAD_SIZE)[None, :]
    wide = LANES // (HEAD_SIZE // 2)
    return (jnp.tile(jnp.cos(angles), (1, wide)), jnp.tile(jnp.sin(angles), (1, wide)))


def rms_scale(values):
    return lax.rsqrt(jnp.mean(values * values, axis=-1, keepdims=True) + eps_norm)


def norm_back(gradient, normed, factor):
    return factor * (gradient - normed * jnp.mean(gradient * normed, axis=-1, keepdims=True))


def inner_rows(left, right):
    return lax.dot_general(
        left, right, (((0,), (0,)), ((), ())), preferred_element_type=jnp.float32
    )


def nt(left, right):
    return lax.dot_general(
        left, right, (((1,), (1,)), ((), ())), preferred_element_type=jnp.float32
    )


def nn(left, right):
    return lax.dot_general(
        left, right, (((1,), (0,)), ((), ())), preferred_element_type=jnp.float32
    )


def turned_lanes(values):
    half = HEAD_SIZE // 2
    lane = lax.broadcasted_iota(jnp.int32, values.shape, 1)
    up = pltpu.roll(values, LANES - half, 1)
    down = pltpu.roll(values, half, 1)
    return jnp.where(lane % HEAD_SIZE < half, -up, down)


def rotate(values, cosine, sine):
    return values * cosine + turned_lanes(values) * sine


def rotate_back(gradient, cosine, sine):
    return gradient * cosine - turned_lanes(gradient * sine)


def qkv_kernel(count, x_ref, *refs):
    weights, (cos_ref, sin_ref, q_ref, kv_ref) = refs[:count], refs[count:]
    depth = x_ref.shape[1] // count
    width_q = q_ref.shape[1]
    width_k = kv_ref.shape[1] // 2
    total = width_q + 2 * width_k
    tile = 2 * LANES
    for start in range(0, total, tile):
        product = 0.0
        for index, weight in enumerate(weights):
            product = product + nn(
                x_ref[:, index * depth : (index + 1) * depth], weight[:, start : start + tile]
            )
        for offset in range(0, tile, LANES):
            at = start + offset
            piece = product[:, offset : offset + LANES]
            if at < width_q + width_k:
                piece = rotate(piece, cos_ref[...], sin_ref[...])
            piece = piece.astype(jnp.bfloat16)
            if at < width_q:
                q_ref[:, at : at + LANES] = piece
            else:
                kv_ref[:, at - width_q : at - width_q + LANES] = piece


def project_qkv(attn_in, weights, cosine, sine, width_q, width_k):
    rows, depth = attn_in.shape
    return pl.pallas_call(
        functools.partial(qkv_kernel, len(weights)),
        out_shape=(
            jax.ShapeDtypeStruct((rows, width_q), jnp.bfloat16),
            jax.ShapeDtypeStruct((rows, 2 * width_k), jnp.bfloat16),
        ),
        in_specs=[in_vmem] * (3 + len(weights)),
        out_specs=(in_vmem, in_vmem),
        compiler_params=kernel_params(),
        cost_estimate=cost(2 * rows * depth * (width_q + 2 * width_k), 6 << 20),
        name="qkv",
    )(attn_in, *weights, cosine, sine)


def sequence_block(slots, me, half_block, bits):
    slot = slots[me ^ block_key(half_block // 2, bits)]
    return jnp.where(half_block % 2 == 0, slot, 2 * (1 << bits) - 1 - slot)


def head_lanes(pair, head, heads_per_kv, scale):
    wide = pair.astype(jnp.float32) * scale
    group = head // heads_per_kv
    source = wide if head % 2 == group else pltpu.roll(wide, HEAD_SIZE, 1)
    low = lax.broadcasted_iota(jnp.int32, wide.shape, 1) < HEAD_SIZE
    keep = low if group == 0 else jnp.logical_not(low)
    return jnp.where(keep, source, 0.0).astype(jnp.bfloat16)


def causal_tile(size):
    key_at = lax.broadcasted_iota(jnp.int32, (size, size), 0)
    row_at = lax.broadcasted_iota(jnp.int32, (size, size), 1)
    return key_at <= row_at


def over_blocks(visit, slots, me, bits, half, prepare):
    visit(0, 0, True, True, True)
    visit(1, half, True, True, True)
    visit(1, 0, False, False, False)
    own = slots[me]
    blocks_of_query = (own, 2 * (1 << bits) - 1 - own)

    def step(index, carry):
        block = sequence_block(slots, me, index, bits)
        start = pl.multiple_of(index * half, half)
        prepare(start)
        for q_half in range(2):

            @pl.when(block < blocks_of_query[q_half])
            def _():
                visit(q_half, start, False, False, False)

        return carry

    lax.fori_loop(2, 2 * (1 << bits), step, 0)


def forward_kernel(
    bits, heads, slots, place, q_ref, kv_ref, out_ref, exact_ref, log_ref, qp, run_max, run_sum, acc
):
    rows = q_ref.shape[0]
    half = rows // 2
    per_kv = heads // 2
    for head in range(heads):
        lanes = pl.ds((head // 2) * LANES, LANES)
        qp[head] = head_lanes(q_ref[:, lanes], head, per_kv, HEAD_SIZE ** (-0.5))

    def visit(q_half, key_start, diagonal, first, _):
        keys = kv_ref[pl.ds(key_start, half), 0:LANES]
        values_t = kv_ref[pl.ds(key_start, half), LANES : 2 * LANES].T
        base = q_half * heads
        span = pl.ds(q_half * half, half)
        scores = [nt(keys, qp[head, span, :]) for head in range(heads)]
        if diagonal:
            visible = causal_tile(half)
            scores = [jnp.where(visible, score, big_negative) for score in scores]
        peaks = [jnp.max(score, axis=0, keepdims=True) for score in scores]
        if not first:
            before = [run_max[base + head] for head in range(heads)]
            peaks = [jnp.maximum(peak, old) for peak, old in zip(peaks, before)]
        weights = [jnp.exp(score - peak) for score, peak in zip(scores, peaks)]
        totals = [jnp.sum(weight, axis=0, keepdims=True) for weight in weights]
        outs = []
        for head, weight in enumerate(weights):
            group = head // per_kv
            some = values_t[group * HEAD_SIZE : (group + 1) * HEAD_SIZE]
            outs.append(nn(some, weight.astype(jnp.bfloat16)))
        if not first:
            fades = [jnp.exp(old - peak) for old, peak in zip(before, peaks)]
            totals = [t + run_sum[base + h] * f for h, (t, f) in enumerate(zip(totals, fades))]
            outs = [o + acc[base + h] * f for h, (o, f) in enumerate(zip(outs, fades))]
        for head in range(heads):
            run_max[base + head] = peaks[head]
            run_sum[base + head] = totals[head]
            acc[base + head] = outs[head]

    over_blocks(visit, slots, place[0], bits, half, lambda start: None)
    for q_half in range(2):
        span = pl.ds(q_half * half, half)
        for pair in range(heads // 2):
            parts = []
            for head in (2 * pair, 2 * pair + 1):
                slot = q_half * heads + head
                parts.append(acc[slot] / run_sum[slot])
                log_ref[pl.ds(head, 1), span] = run_max[slot] + jnp.log(run_sum[slot])
            exact = jnp.concatenate(parts, axis=0).T
            exact_ref[span, pl.ds(pair * LANES, LANES)] = exact
            out_ref[span, pl.ds(pair * LANES, LANES)] = exact.astype(jnp.bfloat16)


def attend_forward(slots, place, queries, kv, bits):
    rows, width = queries.shape
    heads = width // HEAD_SIZE
    half = rows // 2
    visits = 2 * (1 << bits) + 1
    return pl.pallas_call(
        functools.partial(forward_kernel, bits, heads),
        out_shape=(
            jax.ShapeDtypeStruct((rows, width), jnp.bfloat16),
            jax.ShapeDtypeStruct((rows, width), jnp.float32),
            jax.ShapeDtypeStruct((heads, rows), jnp.float32),
        ),
        in_specs=[in_smem, in_smem, in_vmem, in_vmem],
        out_specs=(in_vmem, in_vmem, in_vmem),
        scratch_shapes=[
            pltpu.VMEM((heads, rows, LANES), jnp.bfloat16),
            pltpu.VMEM((2 * heads, 1, half), jnp.float32),
            pltpu.VMEM((2 * heads, 1, half), jnp.float32),
            pltpu.VMEM((2 * heads, HEAD_SIZE, half), jnp.float32),
        ],
        compiler_params=kernel_params(),
        cost_estimate=cost(20 * visits * heads * half * half * HEAD_SIZE, 8 << 20),
        name="attention_forward",
    )(slots, place, queries, kv)


def backward_kernel(
    bits,
    heads,
    slots,
    place,
    q_ref,
    kv_ref,
    do_ref,
    exact_ref,
    log_ref,
    cos_ref,
    sin_ref,
    dq_ref,
    dkv_ref,
    qp,
    dop,
    dots,
    dq_acc,
    dkv_acc,
    do_all,
):
    rows = q_ref.shape[0]
    half = rows // 2
    per_kv = heads // 2
    shifts, local, _ = do_ref.shape
    for shift in range(shifts):
        source = lax.rem(place[1] - shift + shifts, shifts)
        do_all[pl.ds(pl.multiple_of(source * local, local), local), :] = do_ref[shift]
    for head in range(heads):
        lanes = pl.ds((head // 2) * LANES, LANES)
        qp[head] = head_lanes(q_ref[:, lanes], head, per_kv, HEAD_SIZE ** (-0.5))
        dop[head] = head_lanes(do_all[:, lanes], head, per_kv, 1.0)
    for pair in range(heads // 2):
        lanes = pl.ds(pair * LANES, LANES)
        product = (do_all[:, lanes].astype(jnp.float32) * exact_ref[:, lanes]).T
        dots[pl.ds(2 * pair, 1), :] = jnp.sum(product[:HEAD_SIZE], axis=0, keepdims=True)
        dots[pl.ds(2 * pair + 1, 1), :] = jnp.sum(product[HEAD_SIZE:], axis=0, keepdims=True)

    def clear(start):
        dkv_acc[pl.ds(start, half), :] = jnp.zeros((half, 2 * LANES), jnp.float32)

    def visit(q_half, key_start, diagonal, first_query, first_key):
        rows_of_key = pl.ds(key_start, half)
        keys = kv_ref[rows_of_key, 0:LANES]
        values = kv_ref[rows_of_key, LANES : 2 * LANES]
        keys_t = keys.T
        base = q_half * heads
        span = pl.ds(q_half * half, half)
        q_heads = [qp[head, span, :] for head in range(heads)]
        do_heads = [dop[head, span, :] for head in range(heads)]
        scores = [nt(keys, q_head) for q_head in q_heads]
        grad_ws = [nt(values, do_head) for do_head in do_heads]
        weights = [
            jnp.exp(score - log_ref[pl.ds(head, 1), span]) for head, score in enumerate(scores)
        ]
        if diagonal:
            visible = causal_tile(half)
            weights = [jnp.where(visible, weight, 0.0) for weight in weights]
        grad_ss = [
            (weight * (grad_w - dots[pl.ds(head, 1), span])).astype(jnp.bfloat16)
            for head, (weight, grad_w) in enumerate(zip(weights, grad_ws))
        ]
        weights = [weight.astype(jnp.bfloat16) for weight in weights]
        grad_v = jnp.zeros((half, LANES), jnp.float32)
        grad_k = jnp.zeros((half, LANES), jnp.float32)
        for weight, do_head in zip(weights, do_heads):
            grad_v = grad_v + nn(weight, do_head)
        for grad_s, q_head in zip(grad_ss, q_heads):
            grad_k = grad_k + nn(grad_s, q_head)
        for head, grad_s in enumerate(grad_ss):
            group = head // per_kv
            grad_q = nn(keys_t[group * HEAD_SIZE : (group + 1) * HEAD_SIZE], grad_s)
            if not first_query:
                grad_q = grad_q + dq_acc[base + head]
            dq_acc[base + head] = grad_q
        if not first_key:
            grad_k = grad_k + dkv_acc[rows_of_key, 0:LANES]
            grad_v = grad_v + dkv_acc[rows_of_key, LANES : 2 * LANES]
        dkv_acc[rows_of_key, 0:LANES] = grad_k
        dkv_acc[rows_of_key, LANES : 2 * LANES] = grad_v

    over_blocks(visit, slots, place[0], bits, half, clear)
    dkv_ref[...] = dkv_acc[...].astype(jnp.bfloat16)
    for q_half in range(2):
        span = pl.ds(q_half * half, half)
        for pair in range(heads // 2):
            slot = q_half * heads + 2 * pair
            gradient = jnp.concatenate([dq_acc[slot], dq_acc[slot + 1]], axis=0).T
            gradient = rotate_back(
                gradient * HEAD_SIZE ** (-0.5), cos_ref[span, :], sin_ref[span, :]
            )
            dq_ref[span, pl.ds(pair * LANES, LANES)] = gradient.astype(jnp.bfloat16)


def attend_backward(slots, place, queries, kv, grad_parts, exact, log_total, cosine, sine, bits):
    rows, width = queries.shape
    heads = width // HEAD_SIZE
    half = rows // 2
    visits = 2 * (1 << bits) + 1
    return pl.pallas_call(
        functools.partial(backward_kernel, bits, heads),
        out_shape=(
            jax.ShapeDtypeStruct((rows, width), jnp.bfloat16),
            jax.ShapeDtypeStruct(kv.shape, jnp.bfloat16),
        ),
        in_specs=[in_smem, in_smem] + [in_vmem] * 7,
        out_specs=(in_vmem, in_vmem),
        scratch_shapes=[
            pltpu.VMEM((heads, rows, LANES), jnp.bfloat16),
            pltpu.VMEM((heads, rows, LANES), jnp.bfloat16),
            pltpu.VMEM((heads, rows), jnp.float32),
            pltpu.VMEM((2 * heads, HEAD_SIZE, half), jnp.float32),
            pltpu.VMEM(kv.shape, jnp.float32),
            pltpu.VMEM((rows, width), jnp.bfloat16),
        ],
        compiler_params=kernel_params(),
        cost_estimate=cost(40 * visits * heads * half * half * HEAD_SIZE, 12 << 20),
        name="attention_backward",
    )(slots, place, queries, kv, grad_parts, exact, log_total, cosine, sine)


def grad_qkv_kernel(dq_ref, own_ref, first_ref, second_ref, cos_ref, sin_ref, out_ref):
    width_q = dq_ref.shape[1]
    out_ref[:, 0:width_q] = dq_ref[...]
    total = (
        own_ref[...].astype(jnp.float32)
        + first_ref[...].astype(jnp.float32)
        + second_ref[...].astype(jnp.float32)
    )
    keys = rotate_back(total[:, 0:LANES], cos_ref[...], sin_ref[...])
    out_ref[:, width_q : width_q + LANES] = keys.astype(jnp.bfloat16)
    out_ref[:, width_q + LANES : width_q + 2 * LANES] = total[:, LANES:].astype(jnp.bfloat16)


def join_grad_qkv(grad_queries, pieces, cosine, sine):
    rows, width_q = grad_queries.shape
    width = width_q + pieces[0].shape[1]
    return pl.pallas_call(
        grad_qkv_kernel,
        out_shape=jax.ShapeDtypeStruct((rows, width), jnp.bfloat16),
        in_specs=[in_vmem] * 6,
        out_specs=in_vmem,
        compiler_params=kernel_params(),
        cost_estimate=cost(rows * width * 8, 3 << 20),
        name="grad_qkv",
    )(grad_queries, *pieces, cosine, sine)


def mlp_kernel(count, x_ref, g_ref, *refs):
    gates, ups, downs = refs[:count], refs[count : 2 * count], refs[2 * count : 3 * count]
    hidden_ref, grad_gate_ref, grad_up_ref = refs[3 * count :]
    depth = x_ref.shape[1] // count

    def product(left, weights):
        total = 0.0
        for index, weight in enumerate(weights):
            total = total + nn(left[:, index * depth : (index + 1) * depth], weight[...])
        return total

    gate = product(x_ref, gates)
    up = product(x_ref, ups)
    grad_hidden = product(g_ref, downs)
    sigmoid = jax.nn.sigmoid(gate)
    silu = gate * sigmoid
    hidden_ref[...] = (silu * up).astype(jnp.bfloat16)
    grad_gate = grad_hidden * up * sigmoid * (1.0 + gate * (1.0 - sigmoid))
    grad_gate_ref[...] = grad_gate.astype(jnp.bfloat16)
    grad_up_ref[...] = (grad_hidden * silu).astype(jnp.bfloat16)


def mlp_inner(mlp_in, grad_rows, gates, ups, downs):
    rows, depth = mlp_in.shape
    units = gates[0].shape[1]
    count = len(gates)
    tile = min(256, units)
    whole = pl.BlockSpec((rows, depth), lambda i: (0, 0))
    weight = pl.BlockSpec((depth // count, tile), lambda i: (0, i))
    out = pl.BlockSpec((rows, tile), lambda i: (0, i))
    shape = jax.ShapeDtypeStruct((rows, units), jnp.bfloat16)
    return pl.pallas_call(
        functools.partial(mlp_kernel, count),
        grid=(units // tile,),
        out_shape=(shape, shape, shape),
        in_specs=[whole, whole] + [weight] * (3 * count),
        out_specs=(out, out, out),
        compiler_params=kernel_params(),
        cost_estimate=cost(6 * rows * depth * units, 6 * depth * units),
        name="mlp_inner",
    )(mlp_in, grad_rows, *gates, *ups, *downs)


def features_kernel(parts, tiles, lefts, *refs):
    out_ref = refs[-1]
    left_refs = refs[:lefts]
    weight_refs = refs[lefts:-1]
    step = pl.program_id(0)
    for part in range(parts):

        @pl.when(step // tiles == part)
        def _():
            total = 0.0
            for left, weight in zip(left_refs, weight_refs[part * lefts : (part + 1) * lefts]):
                for index in range(left.shape[0]):
                    total = total + nt(left[index], weight[index])
            out_ref[...] = total.astype(out_ref.dtype)


def to_features(lefts, weights, out_dtype):
    rows = lefts[0].shape[1]
    features = weights[0][0].shape[1]
    tile = min(256, features)
    tiles = features // tile
    parts = len(weights)
    in_specs = [pl.BlockSpec(left.shape, lambda i: (0, 0, 0)) for left in lefts]
    flops = 0
    for part, group in enumerate(weights):
        for weight in group:
            depth, _, width = weight.shape
            flops += 2 * rows * features * depth * width
            in_specs.append(
                pl.BlockSpec(
                    (depth, tile, width),
                    functools.partial(
                        lambda base, i: (0, jnp.clip(i - base, 0, tiles - 1), 0), part * tiles
                    ),
                )
            )
    return pl.pallas_call(
        functools.partial(features_kernel, parts, tiles, len(lefts)),
        grid=(parts * tiles,),
        out_shape=jax.ShapeDtypeStruct((rows, parts * features), out_dtype),
        in_specs=in_specs,
        out_specs=pl.BlockSpec((rows, tile), lambda i: (0, i)),
        compiler_params=kernel_params(),
        cost_estimate=cost(flops, flops // rows),
        name="to_features",
    )(*lefts, *[weight for group in weights for weight in group])


def groups_kernel(count, place, x_ref, *refs):
    out_ref = refs[-1]
    depth = x_ref.shape[1] // count
    total = 0.0
    for index, weight in enumerate(refs[:-1]):
        total = total + nn(x_ref[:, index * depth : (index + 1) * depth], weight[0])
    out_ref[0] = total.astype(jnp.bfloat16)


def to_groups(place, branch, weights):
    rows, depth = branch.shape
    groups, features, width = weights[0].shape
    count = len(weights)

    def weight_at(shift, place):
        return (lax.rem(place[1] + shift, groups), 0, 0)

    return pl.pallas_call(
        functools.partial(groups_kernel, count),
        grid_spec=pltpu.PrefetchScalarGridSpec(
            num_scalar_prefetch=1,
            grid=(groups,),
            in_specs=[pl.BlockSpec((rows, depth), lambda i, place: (0, 0))]
            + [pl.BlockSpec((1, features, width), weight_at)] * count,
            out_specs=pl.BlockSpec((1, rows, width), lambda i, place: (i, 0, 0)),
        ),
        out_shape=jax.ShapeDtypeStruct((groups, rows, width), jnp.bfloat16),
        compiler_params=kernel_params(),
        cost_estimate=cost(2 * rows * depth * groups * width, 2 * depth * groups * width),
        name="to_groups",
    )(place, branch, *weights)


def weight_gradient(left, right, parts):
    depth = left.shape[1] // parts
    return [
        inner_rows(left[:, index * depth : (index + 1) * depth], right).astype(jnp.bfloat16)
        for index in range(parts)
    ]


def on_device(
    block_in, out_grad, pair_slot, gain_attn, wq, wk, wv, wo, gain_mlp, w_gate, w_up, w_down
):
    bits = (lax.axis_size("ctx") - 1).bit_length()
    shifts = lax.axis_size("tp")
    me = lax.axis_index("ctx")
    tp = lax.axis_index("tp")
    place = jnp.stack([me, tp]).astype(jnp.int32)
    local_rows = block_in.shape[0]
    group_rows = local_rows * shifts
    width_q, width_k = wq.shape[1], wk.shape[1]

    rows_here = to_relative(block_in, me, bits)
    x_all = lax.all_gather(rows_here, "tp", axis=0, tiled=True)
    qkv_w = gather_ctx(jnp.concatenate([wq, wk, wv], axis=1), bits)
    count = len(qkv_w)
    gains = lax.all_gather(jnp.stack([gain_attn, gain_mlp]), "ctx", axis=1, tiled=True)
    gains = to_relative(gains, me, bits).astype(jnp.float32)
    g_attn, g_mlp = gains[0:1], gains[1:2]
    gate_w = gather_ctx(w_gate, bits)
    up_w = gather_ctx(w_up, bits)
    o_w = gather_ctx(lax.all_gather(wo, "tp", axis=0), bits, axis=1)
    down_w = gather_ctx(w_down, bits)
    out_grad_here = to_relative(out_grad, me, bits)
    grad_rows = lax.all_gather(out_grad_here, "tp", axis=0, tiled=True)

    pos_all = block_positions(pair_slot, group_rows // 2)
    pos_rows = lax.dynamic_slice_in_dim(pos_all, me * group_rows, group_rows)
    cosine, sine = rope_tables(pos_rows)

    inputs = x_all.astype(jnp.float32)
    factor_all = rms_scale(inputs)
    attn_in = (inputs * factor_all * g_attn).astype(jnp.bfloat16)
    queries, kv = project_qkv(attn_in, qkv_w, cosine, sine, width_q, width_k)
    kv_all = jnp.concatenate(gather_ctx(kv, bits), axis=0)
    attended, exact, log_total = attend_forward(pair_slot, place, queries, kv_all, bits)

    attended_all = lax.all_gather(attended, "tp", axis=0)
    residual = inputs + to_features([attended_all], [[part] for part in o_w], jnp.float32)
    factor_mlp_all = rms_scale(residual)
    mlp_in = (residual * factor_mlp_all * g_mlp).astype(jnp.bfloat16)
    residual_here = lax.dynamic_slice_in_dim(residual, tp * local_rows, local_rows)
    factor_mlp = lax.dynamic_slice_in_dim(factor_mlp_all, tp * local_rows, local_rows)
    normed_mlp = residual_here * factor_mlp

    hidden, grad_gate, grad_up = mlp_inner(mlp_in, grad_rows, gate_w, up_w, down_w)
    grad_mlp_part = to_features(
        [grad_gate[None], grad_up[None]],
        [[gate[None], up[None]] for gate, up in zip(gate_w, up_w)],
        jnp.bfloat16,
    )
    grad_mlp_in = lax.psum_scatter(
        grad_mlp_part, "tp", scatter_dimension=0, tiled=True
    ).astype(jnp.float32)
    mlp_part = to_features([hidden[None]], [[down[None]] for down in down_w], jnp.bfloat16)
    mlp_out = lax.psum_scatter(mlp_part, "tp", scatter_dimension=0, tiled=True)
    block_out = (residual_here + mlp_out.astype(jnp.float32)).astype(jnp.bfloat16)
    sum_gate_w = scatter_ctx(weight_gradient(mlp_in, grad_gate, count), bits)
    sum_up_w = scatter_ctx(weight_gradient(mlp_in, grad_up, count), bits)
    sum_down_w = scatter_ctx(weight_gradient(grad_rows, hidden, count), bits)

    gain_mlp_part = jnp.sum(grad_mlp_in * normed_mlp, axis=0, keepdims=True)
    grad_residual = out_grad_here.astype(jnp.float32) + norm_back(
        grad_mlp_in * g_mlp, normed_mlp, factor_mlp
    )
    branch_here = grad_residual.astype(jnp.bfloat16)
    grad_groups = to_groups(place, branch_here, o_w)
    grad_parts = jnp.stack(
        [grad_groups[0]]
        + [
            lax.ppermute(grad_groups[d], "tp", [(i, (i + d) % shifts) for i in range(shifts)])
            for d in range(1, shifts)
        ]
    )
    grad_queries, grad_kv = attend_backward(
        pair_slot, place, queries, kv_all, grad_parts, exact, log_total, cosine, sine, bits
    )
    branch_rows = lax.all_gather(branch_here, "tp", axis=0, tiled=True)
    sum_o_w = scatter_ctx(weight_gradient(branch_rows, attended, count), bits)

    grad_kv_pieces = scatter_pieces(jnp.split(grad_kv, count, axis=0), bits)
    grad_qkv = join_grad_qkv(grad_queries, grad_kv_pieces, cosine, sine)
    grad_attn_part = to_features(
        [grad_qkv[None]], [[part[None]] for part in qkv_w], jnp.bfloat16
    )
    grad_attn_in = lax.psum_scatter(
        grad_attn_part, "tp", scatter_dimension=0, tiled=True
    ).astype(jnp.float32)
    sum_qkv_w = scatter_ctx(weight_gradient(attn_in, grad_qkv, count), bits)
    gain_attn_part = jnp.sum(
        grad_attn_part.astype(jnp.float32) * (inputs * factor_all), axis=0, keepdims=True
    )
    gain_parts = to_absolute(jnp.concatenate([gain_attn_part, gain_mlp_part]), me, bits)
    gain_sums = lax.psum(gain_parts, ("ctx", "tp"))
    gain_width = gain_attn.shape[0]
    gain_here = lax.dynamic_slice_in_dim(gain_sums, me * gain_width, gain_width, 1)

    inputs_here = rows_here.astype(jnp.float32)
    factor_attn = lax.dynamic_slice_in_dim(factor_all, tp * local_rows, local_rows)
    input_grad = grad_residual + norm_back(
        grad_attn_in * g_attn, inputs_here * factor_attn, factor_attn
    )
    return (
        to_absolute(block_out, me, bits),
        to_absolute(input_grad, me, bits),
        gain_here[0],
        sum_qkv_w[:, :width_q],
        sum_qkv_w[:, width_q : width_q + width_k],
        sum_qkv_w[:, width_q + width_k :],
        sum_o_w,
        gain_here[1],
        sum_gate_w,
        sum_up_w,
        sum_down_w,
    )


def solution(mesh):
    placed = (
        P(("ctx", "tp"), None),
        P(("ctx", "tp"), None),
        P(),
        P("ctx"),
        P("ctx", "tp"),
        P("ctx", "tp"),
        P("ctx", "tp"),
        P("ctx", "tp"),
        P("ctx"),
        P("ctx", "tp"),
        P("ctx", "tp"),
        P("ctx", "tp"),
    )
    return jax.shard_map(
        on_device,
        mesh=mesh,
        in_specs=placed,
        out_specs=(
            P(("ctx", "tp"), None),
            P(("ctx", "tp"), None),
            P("ctx"),
            P("ctx", "tp"),
            P("ctx", "tp"),
            P("ctx", "tp"),
            P("ctx", "tp"),
            P("ctx"),
            P("ctx", "tp"),
            P("ctx", "tp"),
            P("ctx", "tp"),
        ),
        check_vma=False,
    )
```

time: 1320 us -> 732 us (0.55)
  waiting for transfers between devices: 846 us -> 259 us
  matrix products: 207 us -> 31.7 us
  Pallas kernels: 0 us -> 130 us
  starting transfers between devices: 1.65 us -> 61.4 us
  local copies, waits for them, and re-layouts: 118 us -> 67.8 us
  blocking collectives: 60.7 us -> 100 us
    reduce_scatter x13 -> x3, waiting for transfers between devices: 514 us -> 42.7 us  [the longest x1 42.6 us: on_device(): lax.psum_scatter(grad_mlp_part, 'tp', scatter_dimension=0, tiled=True)]
    all_gather x11 -> x5, waiting for transfers between devices: 328 us -> 31.4 us  [the longest x1 28.1 us: on_device(): grad_rows = lax.all_gather(out_grad_here, 'tp', axis=0, tiled=True)]
    ppermute x0 -> x63, waiting for transfers between devices: none -> 184 us  [the longest x60 175 us: swap(): lax.ppermute(array, 'ctx', [(i, i ^ 1 << bit) for i in range(1 << bits)])]
    dot_general x49 -> x0, matrix products: 170 us -> none  [the longest x7 33.5 us: times_t(): lax.dot_general(left, right, (((1,), (1,)), ((), ())), preferred_element_...]
    pallas_call x0 -> x10, Pallas kernels: none -> 130 us  [the longest x4 46.3 us: to_features(): pl.pallas_call(functools.partial(features_kernel, parts, tiles, len(lefts...]
    ppermute x0 -> x63, starting transfers between devices: none -> 60.3 us  [the longest x60 56.4 us: swap(): lax.ppermute(array, 'ctx', [(i, i ^ 1 << bit) for i in range(1 << bits)])]
    gather x5 -> x0, local copies, waits for them, and re-layouts: 53 us -> none  [the longest x1 15 us: attention_backward(): grad_value = value_buffer.reshape(seq_len, width_kv)[pos_all]]
    psum x1, blocking collectives: 11.1 us -> 52.3 us  [on_device(): gain_sums = lax.psum(gain_parts, ('ctx', 'tp'))]
  transfers between devices with their start and end apart: 24 -> 71, of which waited for: 20 -> 32; matrix products, arithmetic and copies ran while one was open for 17% -> 18% of each run, Pallas kernels for 0% -> 12%
where the time goes in v1:
time: 732 us; the launch traced here: 720 us
  waiting for transfers between devices  259 us (35%)
  Pallas kernels  130 us (18%)
  blocking collectives  100 us (14%)
  local copies, waits for them, and re-layouts  67.8 us (9%)
  starting transfers between devices  61.4 us (8%)
  other arithmetic  54.5 us (7%)
  matrix products  31.7 us (4%)
  between operations  15.7 us (2%)
    ppermute x60, waiting for transfers between devices, swap(): lax.ppermute(array, 'ctx', [(i, i ^ 1 << bit) for i in range(1 << bits)])  175 us
    ppermute x60, starting transfers between devices, swap(): lax.ppermute(array, 'ctx', [(i, i ^ 1 << bit) for i in range(1 << bits)])  56.4 us
    psum x1, blocking collectives, on_device(): gain_sums = lax.psum(gain_parts, ('ctx', 'tp'))  52.3 us
    all_gather x1, blocking collectives, on_device(): lax.all_gather(jnp.stack([gain_attn, gain_mlp]), 'ctx', axis=1, tiled=True)  47.8 us
    pallas_call x4, Pallas kernels, to_features(): pl.pallas_call(functools.partial(features_kernel, parts, tiles, len(lefts...  46.3 us
    unnamed x166, local copies, waits for them, and re-layouts  44.7 us
    reduce_scatter x1, waiting for transfers between devices, on_device(): lax.psum_scatter(grad_mlp_part, 'tp', scatter_dimension=0, tiled=True)  42.6 us
    dot_general x10, matrix products, inner_rows(): lax.dot_general(left, right, (((0,), (0,)), ((), ())), preferred_element_...  31.7 us
  transfers between devices with their start and end apart: 71, of which 32 were waited for; matrix products, arithmetic and copies ran while one was open for 18% of the time, Pallas kernels for 12%

profile of v1, /device:TPU:2, one launch (start us, length us, event | category | flops | bytes accessed | tf_op | source)
XLA Modules:
  0.0 719.9 jit_solution(15121410094768234535)
XLA Ops:
  22.5 2.5 constant_dynamic-update-slice_fusion.54
  26.0 47.8 %all_gather.25 = bf16[2,2048]{1,0:T(2,128)(2,1)S(1)} all-gather(bf16[2,256]{1,0:T(2,128)(2,1)S(1)} %pad_maximum_fusion.13), channel_id=1, replica_groups=mesh['ctx'=8,'tp'=4] {'ctx'}, dimensions={1}, use_global_device_ids=true | all-gather | bytes 9216 | tf_op jit(solution)/shard_map/all_gather | solution.py:639
  79.2 3.8 collective-permute-done.2
  99.6 5.6 qkv.1
  111.1 3.4 collective-permute-done.6
  116.1 6.6 collective-permute-done.5
  123.4 15.8 %collective-permute-done.7 = bf16[256,256]{1,0:T(8,128)(2,1)S(1)} collective-permute-done((bf16[256,256]{1,0:T(8,128)(2,1)S(1)}, bf16[256,256]{1,0:T(8,128)(2,1)S(1)}, u32[]{:S(2)}, u32[]{:S(2)}) %collective-permute-start.7) | collective-permute-done | bytes 131104 | tf_op jit(solution)/shard_map/ppermute | solution.py:49
  149.2 14.4 %collective-permute-done.10 = bf16[4,256,512]{2,1,0:T(8,128)(2,1)S(1)} collective-permute-done((bf16[4,256,512]{2,1,0:T(8,128)(2,1)S(1)}, bf16[4,256,512]{2,1,0:T(8,128)(2,1)S(1)}, u32[]{:S(2)}, u32[]{:S(2)}) %collective-permute-start.10) | collective-permute-done | bytes 1048608 | tf_op jit(solution)/shard_map/ppermute | solution.py:49
  170.0 18.9 %attention_forward.1 = (bf16[512,512]{1,0:T(8,128)(2,1)}, f32[512,512]{1,0:T(8,128)}, f32[8,512]{1,0:T(8,128)}) custom-call(s32[8]{0:T(128)} %slots.3, s32[2]{0:T(128)} %pad_add_fusion.place, bf16[512,512]{1,0:T(8,128)(2,1)} %get-tuple-element.21.q_ref, bf16[4096,256]{1,0:T(8,128)(2,1)} %copy-done.34), custom_call_target="tpu_custom_call" | custom-call | flops 11408506880 | bytes 8388608 | tf_op jit(solution)/shard_map/attention_forward/pallas_call | solution.py:322
  210.0 6.2 collective-permute-done.22
  217.1 4.0 collective-permute-done.23
  223.8 7.1 collective-permute-done.18
  232.8 3.4 all-gather.14.cloned.1.call-done
  236.2 11.4 %to_features.4 = f32[512,2048]{1,0:T(8,128)} custom-call(bf16[4,512,512]{2,1,0:T(8,128)(2,1)} %bitcast.82, bf16[4,1024,512]{2,1,0:T(8,128)(2,1)} %constant_dynamic-update-slice_fusion.37.refs_1_.refs_0_, bf16[4,1024,512]{2,1,0:T(8,128)(2,1)} %collective-permute-done.14.refs_2_.refs_1_), custom_call_target="tpu_custom_call" | custom-call | flops 4294967296 | bytes 8388608 | tf_op jit(solution)/shard_map/to_features/pallas_call | solution.py:570
  247.6 2.8 multiply_reduce_fusion
  254.2 28.1 %all-gather.10.cloned.1.call-done.g_ref = bf16[512,2048]{1,0:T(8,128)(2,1)} async-done(((bf16[128,2048]{1,0:T(8,128)(2,1)}), bf16[512,2048]{1,0:T(8,128)(2,1)}) %all-gather.10.cloned.1.call-update) | async-done | bytes 2097168 | tf_op jit(solution)/shard_map/all_gather | solution.py:647
  282.3 20.4 %mlp_inner.1 = (bf16[512,2048]{1,0:T(8,128)(2,1)}, bf16[512,2048]{1,0:T(8,128)(2,1)}, bf16[512,2048]{1,0:T(8,128)(2,1)}) custom-call(bf16[512,2048]{1,0:T(8,128)(2,1)} %multiply_convert_fusion.x_ref, bf16[512,2048]{1,0:T(8,128)(2,1)} %all-gather.10.cloned.1.call-done.g_ref, bf16[1024,2048]{1,0:T(8,128)(2,1)} %constant_dynamic-update-slice_fusion.50.refs_0_, ...), custom_call_target="tpu_custom_call" | custom-call | flops 12884901888 | bytes 25165824 | tf_op jit(solution)/shard_map/mlp_inner/pallas_call | solution.py:522
  302.7 16.1 %to_features.6 = bf16[512,2048]{1,0:T(8,128)(2,1)} custom-call(bf16[1,512,2048]{2,1,0:T(8,128)(2,1)} %bitcast.85, bf16[1,512,2048]{2,1,0:T(8,128)(2,1)} %bitcast.84, bf16[1,1024,2048]{2,1,0:T(8,128)(2,1)} %bitcast.13.refs_2_, bf16[1,1024,2048]{2,1,0:T(8,128)(2,1)} %bitcast.68, bf16[1,1024,2048]{2,1,0:T(8,128)(2,1)} %bitcast.15.refs_4_, ...), custom_call_target="tpu_custom_call" | custom-call | flops 8589934592 | bytes 16777216 | tf_op jit(solution)/shard_map/to_features/pallas_call | solution.py:570
  318.9 42.6 %reduce-scatter.6.cloned.1.call-done = bf16[128,2048]{1,0:T(8,128)(2,1)} async-done(((bf16[512,2048]{1,0:T(8,128)(2,1)}), bf16[128,2048]{1,0:T(8,128)(2,1)}) %reduce-scatter.6.cloned.1.call-update) | async-done | bytes 524304 | tf_op jit(solution)/shard_map/reduce_scatter | solution.py:674
  363.4 2.5 fusion.35.x_ref
  365.9 6.3 to_groups.1
  379.0 8.1 %collective-permute-done.31 = bf16[128,512]{1,0:T(8,128)(2,1)S(1)} collective-permute-done((bf16[128,512]{1,0:T(8,128)(2,1)S(1)}, bf16[128,512]{1,0:T(8,128)(2,1)S(1)}, u32[]{:S(2)}, u32[]{:S(2)}) %collective-permute-start.31) | collective-permute-done | bytes 131104 | tf_op jit(solution)/shard_map/ppermute | solution.py:693
  388.0 30.0 %attention_backward.1 = (bf16[512,512]{1,0:T(8,128)(2,1)}, bf16[4096,256]{1,0:T(8,128)(2,1)}) custom-call(s32[8]{0:T(128)} %slots.3, s32[2]{0:T(128)} %pad_add_fusion.place, bf16[512,512]{1,0:T(8,128)(2,1)} %get-tuple-element.21.q_ref, bf16[4096,256]{1,0:T(8,128)(2,1)} %copy-done.34, bf16[4,128,512]{2,1,0:T(8,128)(2,1)} %pad_maximum_fusion.6.do_ref, ...), custom_call_target="tpu_custom_call" | custom-call | flops 22817013760 | bytes 12582912 | tf_op jit(solution)/shard_map/attention_backward/pallas_call | solution.py:442
  419.5 2.6 collective-permute-done.33
  424.6 3.5 collective-permute-done.36
  432.3 3.5 collective-permute-done.35.first_ref
  437.7 2.6 grad_qkv.1
  440.3 7.7 %to_features.7 = bf16[512,2048]{1,0:T(8,128)(2,1)} custom-call(bf16[1,512,768]{2,1,0:T(8,128)(2,1)} %bitcast.46, bf16[1,1024,768]{2,1,0:T(8,128)(2,1)} %bitcast.24.refs_1_, bf16[1,1024,768]{2,1,0:T(8,128)(2,1)} %bitcast.25.refs_2_), custom_call_target="tpu_custom_call" | custom-call | flops 1610612736 | bytes 3145728 | tf_op jit(solution)/shard_map/to_features/pallas_call | solution.py:570
  448.2 6.4 convolution_convert_fusion.1
  454.7 4.5 convolution_convert_fusion.2
  459.6 4.4 convolution_convert_fusion
  464.1 11.1 %to_features.5 = bf16[512,2048]{1,0:T(8,128)(2,1)} custom-call(bf16[1,512,2048]{2,1,0:T(8,128)(2,1)} %bitcast.83, bf16[1,1024,2048]{2,1,0:T(8,128)(2,1)} %bitcast.9.refs_1_, bf16[1,1024,2048]{2,1,0:T(8,128)(2,1)} %bitcast.10.refs_2_), custom_call_target="tpu_custom_call" | custom-call | flops 4294967296 | bytes 8388608 | tf_op jit(solution)/shard_map/to_features/pallas_call | solution.py:570
  475.3 4.5 fusion.22
  484.7 4.1 add_convert_fusion.1
  490.4 4.1 add_convert_fusion.2
  496.0 4.3 add_convert_fusion
  507.0 7.9 %collective-permute-done.49 = bf16[128,2048]{1,0:T(8,128)(2,1)S(1)} collective-permute-done((bf16[128,2048]{1,0:T(8,128)(2,1)S(1)}, bf16[128,2048]{1,0:T(8,128)(2,1)S(1)}, u32[]{:S(2)}, u32[]{:S(2)}) %collective-permute-start.49) | collective-permute-done | bytes 524320 | tf_op jit(solution)/shard_map/ppermute | solution.py:49
  518.2 7.5 %collective-permute-done.59 = bf16[128,2048]{1,0:T(8,128)(2,1)S(1)} collective-permute-done((bf16[128,2048]{1,0:T(8,128)(2,1)S(1)}, bf16[128,2048]{1,0:T(8,128)(2,1)S(1)}, u32[]{:S(2)}, u32[]{:S(2)}) %collective-permute-start.59) | collective-permute-done | bytes 524320 | tf_op jit(solution)/shard_map/ppermute | solution.py:49
  530.1 22.3 %collective-permute-done.51 = bf16[128,2048]{1,0:T(8,128)(2,1)S(1)} collective-permute-done((bf16[128,2048]{1,0:T(8,128)(2,1)S(1)}, bf16[128,2048]{1,0:T(8,128)(2,1)S(1)}, u32[]{:S(2)}, u32[]{:S(2)}) %collective-permute-start.51) | collective-permute-done | bytes 524320 | tf_op jit(solution)/shard_map/ppermute | solution.py:49
  555.0 31.1 %collective-permute-done.61 = bf16[128,2048]{1,0:T(8,128)(2,1)S(1)} collective-permute-done((bf16[128,2048]{1,0:T(8,128)(2,1)S(1)}, bf16[128,2048]{1,0:T(8,128)(2,1)S(1)}, u32[]{:S(2)}, u32[]{:S(2)}) %collective-permute-start.61) | collective-permute-done | bytes 524320 | tf_op jit(solution)/shard_map/ppermute | solution.py:49
  592.9 52.3 %psum.7 = f32[2,2048]{1,0:T(2,128)S(1)} all-reduce(f32[2,2048]{1,0:T(2,128)S(1)} %constant_dynamic-update-slice_fusion.81), channel_id=1, replica_groups=mesh['ctx'=8,'tp'=4] {'ctx','tp'}, use_global_device_ids=true, to_apply=%region_9.10 | all-reduce | flops 4096 | bytes 32768 | tf_op jit(solution)/shard_map/psum | solution.py:716
  648.8 3.7 convert_add_fusion.2
  652.5 3.8 convert_add_fusion.3
  658.9 12.7 %collective-permute-done.62 = bf16[256,2048]{1,0:T(8,128)(2,1)S(1)} collective-permute-done((bf16[256,2048]{1,0:T(8,128)(2,1)}, bf16[256,2048]{1,0:T(8,128)(2,1)S(1)}, u32[]{:S(2)}, u32[]{:S(2)}) %collective-permute-start.62) | collective-permute-done | bytes 1048608 | tf_op jit(solution)/shard_map/ppermute | solution.py:49
  671.6 3.4 convert_add_fusion.1
  679.2 3.6 collective-permute-done.39
  686.8 4.0 collective-permute-done.41
  695.4 4.7 collective-permute-done.46
  (401 shorter events, 175.9 us)
Async XLA Ops:
  7.2 88.3 %all-gather.8.cloned.1.call-start = ((), (), s32[]{:S(2)}) async-start(), calls=%async_computation.3 | async-start | bytes 2621440 | tf_op jit(solution)/shard_map/all_gather | solution.py:636
  14.9 94.6 %all-gather.16.cloned.1.call-start = ((), (), s32[]{:S(2)}) async-start(), calls=%async_computation.10 | async-start | bytes 1310720 | tf_op jit(solution)/shard_map/all_gather | solution.py:644
  15.0 78.4 %collective-permute-start.25 = (bf16[256,2048]{1,0:T(8,128)(2,1)}, bf16[256,2048]{1,0:T(8,128)(2,1)S(1)}, u32[]{:S(2)}, u32[]{:S(2)}) collective-permute-start(bf16[256,2048]{1,0:T(8,128)(2,1)} %param.23), channel_id=1, source_target_pairs={{0,8},{4,12},{8,0},{12,4},{16,24},{20,28},{24,16},{28,20},{1,9},{5... | collective-permute-start | bytes 3145736 | tf_op jit(solution)/shard_map/ppermute | solution.py:49
  15.1 79.3 %collective-permute-start.26 = (bf16[256,2048]{1,0:T(8,128)(2,1)}, bf16[256,2048]{1,0:T(8,128)(2,1)S(1)}, u32[]{:S(2)}, u32[]{:S(2)}) collective-permute-start(bf16[256,2048]{1,0:T(8,128)(2,1)} %param.23), channel_id=1, source_target_pairs={{0,16},{4,20},{8,24},{12,28},{16,0},{20,4},{24,8},{28,12},{1,17},{... | collective-permute-start | bytes 3145736 | tf_op jit(solution)/shard_map/ppermute | solution.py:49
  20.2 54.0 %collective-permute-start.1 = (bf16[256,768]{1,0:T(8,128)(2,1)}, bf16[256,768]{1,0:T(8,128)(2,1)S(1)}, u32[]{:S(2)}, u32[]{:S(2)}) collective-permute-start(bf16[256,768]{1,0:T(8,128)(2,1)} %get-tuple-element.81), channel_id=1, source_target_pairs={{0,16},{4,20},{8,24},{12,28},{16,0},{20,4},{24,8},{28,12},{1,17},{... | collective-permute-start | bytes 1179656 | tf_op jit(solution)/shard_map/ppermute | solution.py:49
  20.3 55.8 %collective-permute-start = (bf16[256,768]{1,0:T(8,128)(2,1)}, bf16[256,768]{1,0:T(8,128)(2,1)S(1)}, u32[]{:S(2)}, u32[]{:S(2)}) collective-permute-start(bf16[256,768]{1,0:T(8,128)(2,1)} %get-tuple-element.81), channel_id=1, source_target_pairs={{0,8},{4,12},{8,0},{12,4},{16,24},{20,28},{24,16},{28,20},{1,9},{5... | collective-permute-start | bytes 1179656 | tf_op jit(solution)/shard_map/ppermute | solution.py:49
  22.2 68.7 %collective-permute-start.15 = (bf16[256,2048]{1,0:T(8,128)(2,1)}, bf16[256,2048]{1,0:T(8,128)(2,1)}, u32[]{:S(2)}, u32[]{:S(2)}) collective-permute-start(bf16[256,2048]{1,0:T(8,128)(2,1)} %param.21), channel_id=1, source_target_pairs={{0,8},{4,12},{8,0},{12,4},{16,24},{20,28},{24,16},{28,20},{1,9},{5... | collective-permute-start | bytes 3145736 | tf_op jit(solution)/shard_map/ppermute | solution.py:49
  22.3 213.9 %all-gather.14.cloned.1.call-start = ((), (), s32[]{:S(2)}) async-start(), calls=%async_computation.9 | async-start | bytes 2621440 | tf_op jit(solution)/shard_map/all_gather | solution.py:660
  83.0 59.9 %collective-permute-start.16 = (bf16[256,2048]{1,0:T(8,128)(2,1)}, bf16[256,2048]{1,0:T(8,128)(2,1)}, u32[]{:S(2)}, u32[]{:S(2)}) collective-permute-start(bf16[256,2048]{1,0:T(8,128)(2,1)} %param.21), channel_id=1, source_target_pairs={{0,16},{4,20},{8,24},{12,28},{16,0},{20,4},{24,8},{28,12},{1,17},{... | collective-permute-start | bytes 3145736 | tf_op jit(solution)/shard_map/ppermute | solution.py:49
  90.9 105.4 %collective-permute-start.20 = (bf16[256,2048]{1,0:T(8,128)(2,1)}, bf16[256,2048]{1,0:T(8,128)(2,1)}, u32[]{:S(2)}, u32[]{:S(2)}) collective-permute-start(bf16[256,2048]{1,0:T(8,128)(2,1)} %param.22), channel_id=1, source_target_pairs={{0,8},{4,12},{8,0},{12,4},{16,24},{20,28},{24,16},{28,20},{1,9},{5... | collective-permute-start | bytes 3145736 | tf_op jit(solution)/shard_map/ppermute | solution.py:49
  105.5 17.2 %collective-permute-start.5 = (bf16[512,256]{1,0:T(8,128)(2,1)}, bf16[512,256]{1,0:T(8,128)(2,1)S(1)}, u32[]{:S(2)}, u32[]{:S(2)}) collective-permute-start(bf16[512,256]{1,0:T(8,128)(2,1)} %get-tuple-element.22), channel_id=1, source_target_pairs={{0,8},{4,12},{8,0},{12,4},{16,24},{20,28},{24,16},{28,20},{1,9},{5... | collective-permute-start | bytes 786440 | tf_op jit(solution)/shard_map/ppermute | solution.py:49
  109.6 37.3 %collective-permute-start.11 = (bf16[4,256,512]{2,1,0:T(8,128)(2,1)}, bf16[4,256,512]{2,1,0:T(8,128)(2,1)S(1)}, u32[]{:S(2)}, u32[]{:S(2)}) collective-permute-start(bf16[4,256,512]{2,1,0:T(8,128)(2,1)} %bitcast.49), channel_id=1, source_target_pairs={{0,16},{4,20},{8,24},{12,28},{16,0},{20,4},{24,8},{28,12},{1,17},{... | collective-permute-start | bytes 3145736 | tf_op jit(solution)/shard_map/ppermute | solution.py:49
  114.6 26.1 %collective-permute-start.8 = (bf16[256,256]{1,0:T(8,128)(2,1)S(1)}, bf16[256,256]{1,0:T(8,128)(2,1)S(1)}, u32[]{:S(2)}, u32[]{:S(2)}) collective-permute-start(bf16[256,256]{1,0:T(8,128)(2,1)S(1)} %slice.310), channel_id=1, source_target_pairs={{0,8},{4,12},{8,0},{12,4},{16,24},{20,28},{24,16},{28,20},{1,9},{5... | collective-permute-start | bytes 393224 | tf_op jit(solution)/shard_map/ppermute | solution.py:49
  122.7 16.4 %collective-permute-start.7 = (bf16[256,256]{1,0:T(8,128)(2,1)S(1)}, bf16[256,256]{1,0:T(8,128)(2,1)S(1)}, u32[]{:S(2)}, u32[]{:S(2)}) collective-permute-start(bf16[256,256]{1,0:T(8,128)(2,1)S(1)} %slice.309), channel_id=1, source_target_pairs={{0,16},{4,20},{8,24},{12,28},{16,0},{20,4},{24,8},{28,12},{1,17},{... | collective-permute-start | bytes 393224 | tf_op jit(solution)/shard_map/ppermute | solution.py:49
  139.1 24.5 %collective-permute-start.10 = (bf16[4,256,512]{2,1,0:T(8,128)(2,1)S(1)}, bf16[4,256,512]{2,1,0:T(8,128)(2,1)S(1)}, u32[]{:S(2)}, u32[]{:S(2)}) collective-permute-start(bf16[4,256,512]{2,1,0:T(8,128)(2,1)S(1)} %bitcast.50), channel_id=1, source_target_pairs={{0,8},{4,12},{8,0},{12,4},{16,24},{20,28},{24,16},{28,20},{1,9},{5... | collective-permute-start | bytes 3145736 | tf_op jit(solution)/shard_map/ppermute | solution.py:49
  140.7 27.4 %collective-permute-start.9 = (bf16[2048,256]{1,0:T(8,128)(2,1)S(1)}, bf16[2048,256]{1,0:T(8,128)(2,1)S(1)}, u32[]{:S(2)}, u32[]{:S(2)}) collective-permute-start(bf16[2048,256]{1,0:T(8,128)(2,1)S(1)} %get-tuple-element.77), channel_id=1, source_target_pairs={{0,4},{4,0},{8,12},{12,8},{16,20},{20,16},{24,28},{28,24},{1,5},{5... | collective-permute-start | bytes 3145736 | tf_op jit(solution)/shard_map/ppermute | solution.py:49
  142.9 57.0 %collective-permute-start.21 = (bf16[256,2048]{1,0:T(8,128)(2,1)}, bf16[256,2048]{1,0:T(8,128)(2,1)}, u32[]{:S(2)}, u32[]{:S(2)}) collective-permute-start(bf16[256,2048]{1,0:T(8,128)(2,1)} %param.22), channel_id=1, source_target_pairs={{0,16},{4,20},{8,24},{12,28},{16,0},{20,4},{24,8},{28,12},{1,17},{... | collective-permute-start | bytes 3145736 | tf_op jit(solution)/shard_map/ppermute | solution.py:49
  146.8 75.1 %collective-permute-start.17 = (bf16[128,2048]{1,0:T(8,128)(2,1)S(1)}, bf16[128,2048]{1,0:T(8,128)(2,1)}, u32[]{:S(2)}, u32[]{:S(2)}) collective-permute-start(bf16[128,2048]{1,0:T(8,128)(2,1)S(1)} %copy-done.26), channel_id=1, source_target_pairs={{0,16},{4,20},{8,24},{12,28},{16,0},{20,4},{24,8},{28,12},{1,17},{... | collective-permute-start | bytes 1572872 | tf_op jit(solution)/shard_map/ppermute | solution.py:49
  163.6 30.0 %collective-permute-start.13 = (bf16[4,128,512]{2,1,0:T(8,128)(2,1)}, bf16[4,128,512]{2,1,0:T(8,128)(2,1)}, u32[]{:S(2)}, u32[]{:S(2)}) collective-permute-start(bf16[4,128,512]{2,1,0:T(8,128)(2,1)} %slice.312), channel_id=1, source_target_pairs={{0,8},{4,12},{8,0},{12,4},{16,24},{20,28},{24,16},{28,20},{1,9},{5... | collective-permute-start | bytes 1572872 | tf_op jit(solution)/shard_map/ppermute | solution.py:49
  168.1 23.1 %collective-permute-start.12 = (bf16[4,128,512]{2,1,0:T(8,128)(2,1)}, bf16[4,128,512]{2,1,0:T(8,128)(2,1)}, u32[]{:S(2)}, u32[]{:S(2)}) collective-permute-start(bf16[4,128,512]{2,1,0:T(8,128)(2,1)} %slice.311), channel_id=1, source_target_pairs={{0,16},{4,20},{8,24},{12,28},{16,0},{20,4},{24,8},{28,12},{1,17},{... | collective-permute-start | bytes 1572872 | tf_op jit(solution)/shard_map/ppermute | solution.py:49
  188.9 93.4 %all-gather.10.cloned.1.call-start = ((), (), s32[]{:S(2)}) async-start(), calls=%async_computation.4 | async-start | bytes 2621440 | tf_op jit(solution)/shard_map/all_gather | solution.py:647
  196.3 36.5 %collective-permute-start.14 = (bf16[4,1024,512]{2,1,0:T(8,128)(2,1)}, bf16[4,1024,512]{2,1,0:T(8,128)(2,1)}, u32[]{:S(2)}, u32[]{:S(2)}) collective-permute-start(bf16[4,1024,512]{2,1,0:T(8,128)(2,1)} %constant_dynamic-update-slice_fusion.37.refs_1_.refs_0_), channel_id=1, source_target_pairs={{0,4},{4,0},{8,12},{12,8},{16,20},{20,16},{24,28},{28,24},{1,5},{5... | collective-permute-start | bytes 12582920 | tf_op jit(solution)/shard_map/ppermute | solution.py:49
  199.9 16.3 %collective-permute-start.22 = (bf16[128,2048]{1,0:T(8,128)(2,1)S(1)}, bf16[128,2048]{1,0:T(8,128)(2,1)S(1)}, u32[]{:S(2)}, u32[]{:S(2)}) collective-permute-start(bf16[128,2048]{1,0:T(8,128)(2,1)S(1)} %slice.316), channel_id=1, source_target_pairs={{0,16},{4,20},{8,24},{12,28},{16,0},{20,4},{24,8},{28,12},{1,17},{... | collective-permute-start | bytes 1572872 | tf_op jit(solution)/shard_map/ppermute | solution.py:49
  208.0 23.0 %collective-permute-start.18 = (bf16[128,2048]{1,0:T(8,128)(2,1)S(1)}, bf16[128,2048]{1,0:T(8,128)(2,1)S(1)}, u32[]{:S(2)}, u32[]{:S(2)}) collective-permute-start(bf16[128,2048]{1,0:T(8,128)(2,1)S(1)} %slice.315), channel_id=1, source_target_pairs={{0,8},{4,12},{8,0},{12,4},{16,24},{20,28},{24,16},{28,20},{1,9},{5... | collective-permute-start | bytes 1572872 | tf_op jit(solution)/shard_map/ppermute | solution.py:49
  216.2 66.1 %collective-permute-start.29 = (bf16[1024,2048]{1,0:T(8,128)(2,1)}, bf16[1024,2048]{1,0:T(8,128)(2,1)}, u32[]{:S(2)}, u32[]{:S(2)}) collective-permute-start(bf16[1024,2048]{1,0:T(8,128)(2,1)} %constant_dynamic-update-slice_fusion.60.refs_4_), channel_id=1, source_target_pairs={{0,4},{4,0},{8,12},{12,8},{16,20},{20,16},{24,28},{28,24},{1,5},{5... | collective-permute-start | bytes 12582920 | tf_op jit(solution)/shard_map/ppermute | solution.py:49
  221.9 60.3 %collective-permute-start.24 = (bf16[1024,2048]{1,0:T(8,128)(2,1)}, bf16[1024,2048]{1,0:T(8,128)(2,1)}, u32[]{:S(2)}, u32[]{:S(2)}) collective-permute-start(bf16[1024,2048]{1,0:T(8,128)(2,1)} %constant_dynamic-update-slice_fusion.55.refs_2_), channel_id=1, source_target_pairs={{0,4},{4,0},{8,12},{12,8},{16,20},{20,16},{24,28},{28,24},{1,5},{5... | collective-permute-start | bytes 12582920 | tf_op jit(solution)/shard_map/ppermute | solution.py:49
  231.8 50.5 %collective-permute-start.19 = (bf16[1024,2048]{1,0:T(8,128)(2,1)}, bf16[1024,2048]{1,0:T(8,128)(2,1)}, u32[]{:S(2)}, u32[]{:S(2)}) collective-permute-start(bf16[1024,2048]{1,0:T(8,128)(2,1)} %constant_dynamic-update-slice_fusion.50.refs_0_), channel_id=1, source_target_pairs={{0,4},{4,0},{8,12},{12,8},{16,20},{20,16},{24,28},{28,24},{1,5},{5... | collective-permute-start | bytes 12582920 | tf_op jit(solution)/shard_map/ppermute | solution.py:49
  232.8 128.8 %reduce-scatter.6.cloned.1.call-start = ((), (), s32[]{:S(2)}) async-start(), calls=%async_computation.6 | async-start | bytes 2621440 | tf_op jit(solution)/shard_map/reduce_scatter | solution.py:674
  318.8 337.5 %all-gather.12.cloned.1.call-start = ((), (), s32[]{:S(2)}) async-start(), calls=%async_computation.8 | async-start | bytes 2621440 | tf_op jit(solution)/shard_map/all_gather | solution.py:700
  377.2 330.3 %reduce-scatter.8.cloned.1.call-start = ((), (), s32[]{:S(2)}) async-start(), calls=%async_computation.7 | async-start | bytes 2621440 | tf_op jit(solution)/shard_map/reduce_scatter | solution.py:708
  448.0 261.0 %reduce-scatter.4.cloned.1.call-start = ((), (), s32[]{:S(2)}) async-start(), calls=%async_computation.5 | async-start | bytes 2621440 | tf_op jit(solution)/shard_map/reduce_scatter | solution.py:678
  454.6 30.1 %collective-permute-start.53 = (bf16[1024,2048]{1,0:T(8,128)(2,1)}, bf16[1024,2048]{1,0:T(8,128)(2,1)}, u32[]{:S(2)}, u32[]{:S(2)}) collective-permute-start(bf16[1024,2048]{1,0:T(8,128)(2,1)} %convolution_convert_fusion.1), channel_id=1, source_target_pairs={{0,4},{4,0},{8,12},{12,8},{16,20},{20,16},{24,28},{28,24},{1,5},{5... | collective-permute-start | bytes 12582920 | tf_op jit(solution)/shard_map/ppermute | solution.py:49
  459.1 31.3 %collective-permute-start.48 = (bf16[1024,2048]{1,0:T(8,128)(2,1)}, bf16[1024,2048]{1,0:T(8,128)(2,1)}, u32[]{:S(2)}, u32[]{:S(2)}) collective-permute-start(bf16[1024,2048]{1,0:T(8,128)(2,1)} %convolution_convert_fusion.2), channel_id=1, source_target_pairs={{0,4},{4,0},{8,12},{12,8},{16,20},{20,16},{24,28},{28,24},{1,5},{5... | collective-permute-start | bytes 12582920 | tf_op jit(solution)/shard_map/ppermute | solution.py:49
  464.0 32.0 %collective-permute-start.58 = (bf16[1024,2048]{1,0:T(8,128)(2,1)}, bf16[1024,2048]{1,0:T(8,128)(2,1)}, u32[]{:S(2)}, u32[]{:S(2)}) collective-permute-start(bf16[1024,2048]{1,0:T(8,128)(2,1)} %convolution_convert_fusion), channel_id=1, source_target_pairs={{0,4},{4,0},{8,12},{12,8},{16,20},{20,16},{24,28},{28,24},{1,5},{5... | collective-permute-start | bytes 12582920 | tf_op jit(solution)/shard_map/ppermute | solution.py:49
  494.6 20.3 %collective-permute-start.49 = (bf16[128,2048]{1,0:T(8,128)(2,1)S(1)}, bf16[128,2048]{1,0:T(8,128)(2,1)S(1)}, u32[]{:S(2)}, u32[]{:S(2)}) collective-permute-start(bf16[128,2048]{1,0:T(8,128)(2,1)S(1)} %slice.352), channel_id=1, source_target_pairs={{0,16},{4,20},{8,24},{12,28},{16,0},{20,4},{24,8},{28,12},{1,17},{... | collective-permute-start | bytes 1572872 | tf_op jit(solution)/shard_map/ppermute | solution.py:49
  500.4 25.3 %collective-permute-start.59 = (bf16[128,2048]{1,0:T(8,128)(2,1)S(1)}, bf16[128,2048]{1,0:T(8,128)(2,1)S(1)}, u32[]{:S(2)}, u32[]{:S(2)}) collective-permute-start(bf16[128,2048]{1,0:T(8,128)(2,1)S(1)} %slice.366), channel_id=1, source_target_pairs={{0,16},{4,20},{8,24},{12,28},{16,0},{20,4},{24,8},{28,12},{1,17},{... | collective-permute-start | bytes 1572872 | tf_op jit(solution)/shard_map/ppermute | solution.py:49
  503.8 23.7 %collective-permute-start.56 = (bf16[128,2048]{1,0:T(8,128)(2,1)S(1)}, bf16[128,2048]{1,0:T(8,128)(2,1)S(1)}, u32[]{:S(2)}, u32[]{:S(2)}) collective-permute-start(bf16[128,2048]{1,0:T(8,128)(2,1)S(1)} %get-tuple-element.40), channel_id=1, source_target_pairs={{0,8},{4,12},{8,0},{12,4},{16,24},{20,28},{24,16},{28,20},{1,9},{5... | collective-permute-start | bytes 1572872 | tf_op jit(solution)/shard_map/ppermute | solution.py:49
  505.5 142.5 %collective-permute-start.55 = (bf16[256,2048]{1,0:T(8,128)(2,1)}, bf16[256,2048]{1,0:T(8,128)(2,1)}, u32[]{:S(2)}, u32[]{:S(2)}) collective-permute-start(bf16[256,2048]{1,0:T(8,128)(2,1)} %pad_maximum_fusion.2), channel_id=1, source_target_pairs={{0,8},{4,12},{8,0},{12,4},{16,24},{20,28},{24,16},{28,20},{1,9},{5... | collective-permute-start | bytes 3145736 | tf_op jit(solution)/shard_map/ppermute | solution.py:49
  515.0 37.4 %collective-permute-start.51 = (bf16[128,2048]{1,0:T(8,128)(2,1)S(1)}, bf16[128,2048]{1,0:T(8,128)(2,1)S(1)}, u32[]{:S(2)}, u32[]{:S(2)}) collective-permute-start(bf16[128,2048]{1,0:T(8,128)(2,1)S(1)} %get-tuple-element.44), channel_id=1, source_target_pairs={{0,8},{4,12},{8,0},{12,4},{16,24},{20,28},{24,16},{28,20},{1,9},{5... | collective-permute-start | bytes 1572872 | tf_op jit(solution)/shard_map/ppermute | solution.py:49
  516.7 135.8 %collective-permute-start.50 = (bf16[256,2048]{1,0:T(8,128)(2,1)}, bf16[256,2048]{1,0:T(8,128)(2,1)}, u32[]{:S(2)}, u32[]{:S(2)}) collective-permute-start(bf16[256,2048]{1,0:T(8,128)(2,1)} %pad_maximum_fusion), channel_id=1, source_target_pairs={{0,8},{4,12},{8,0},{12,4},{16,24},{20,28},{24,16},{28,20},{1,9},{5... | collective-permute-start | bytes 3145736 | tf_op jit(solution)/shard_map/ppermute | solution.py:49
  525.8 60.3 %collective-permute-start.61 = (bf16[128,2048]{1,0:T(8,128)(2,1)S(1)}, bf16[128,2048]{1,0:T(8,128)(2,1)S(1)}, u32[]{:S(2)}, u32[]{:S(2)}) collective-permute-start(bf16[128,2048]{1,0:T(8,128)(2,1)S(1)} %get-tuple-element.36), channel_id=1, source_target_pairs={{0,8},{4,12},{8,0},{12,4},{16,24},{20,28},{24,16},{28,20},{1,9},{5... | collective-permute-start | bytes 1572872 | tf_op jit(solution)/shard_map/ppermute | solution.py:49
  527.5 131.3 %collective-permute-start.60 = (bf16[256,2048]{1,0:T(8,128)(2,1)}, bf16[256,2048]{1,0:T(8,128)(2,1)}, u32[]{:S(2)}, u32[]{:S(2)}) collective-permute-start(bf16[256,2048]{1,0:T(8,128)(2,1)} %pad_maximum_fusion.4), channel_id=1, source_target_pairs={{0,8},{4,12},{8,0},{12,4},{16,24},{20,28},{24,16},{28,20},{1,9},{5... | collective-permute-start | bytes 3145736 | tf_op jit(solution)/shard_map/ppermute | solution.py:49
  552.4 96.4 %collective-permute-start.57 = (bf16[256,2048]{1,0:T(8,128)(2,1)}, bf16[256,2048]{1,0:T(8,128)(2,1)}, u32[]{:S(2)}, u32[]{:S(2)}) collective-permute-start(bf16[256,2048]{1,0:T(8,128)(2,1)} %pad_maximum_fusion.3), channel_id=1, source_target_pairs={{0,16},{4,20},{8,24},{12,28},{16,0},{20,4},{24,8},{28,12},{1,17},{... | collective-permute-start | bytes 3145736 | tf_op jit(solution)/shard_map/ppermute | solution.py:49
  586.1 66.4 %collective-permute-start.52 = (bf16[256,2048]{1,0:T(8,128)(2,1)}, bf16[256,2048]{1,0:T(8,128)(2,1)}, u32[]{:S(2)}, u32[]{:S(2)}) collective-permute-start(bf16[256,2048]{1,0:T(8,128)(2,1)} %pad_maximum_fusion.1), channel_id=1, source_target_pairs={{0,16},{4,20},{8,24},{12,28},{16,0},{20,4},{24,8},{28,12},{1,17},{... | collective-permute-start | bytes 3145736 | tf_op jit(solution)/shard_map/ppermute | solution.py:49
  648.0 23.5 %collective-permute-start.62 = (bf16[256,2048]{1,0:T(8,128)(2,1)}, bf16[256,2048]{1,0:T(8,128)(2,1)S(1)}, u32[]{:S(2)}, u32[]{:S(2)}) collective-permute-start(bf16[256,2048]{1,0:T(8,128)(2,1)} %pad_maximum_fusion.5), channel_id=1, source_target_pairs={{0,16},{4,20},{8,24},{12,28},{16,0},{20,4},{24,8},{28,12},{1,17},{... | collective-permute-start | bytes 3145736 | tf_op jit(solution)/shard_map/ppermute | solution.py:49
  648.8 26.2 %collective-permute-start.38 = (bf16[1024,768]{1,0:T(8,128)(2,1)}, bf16[1024,768]{1,0:T(8,128)(2,1)}, u32[]{:S(2)}, u32[]{:S(2)}) collective-permute-start(bf16[1024,768]{1,0:T(8,128)(2,1)} %convolution_convert_fusion.3), channel_id=1, source_target_pairs={{0,4},{4,0},{8,12},{12,8},{16,20},{20,16},{24,28},{28,24},{1,5},{5... | collective-permute-start | bytes 4718600 | tf_op jit(solution)/shard_map/ppermute | solution.py:49
  658.3 26.8 %collective-permute-start.43 = (bf16[1024,512]{1,0:T(8,128)(2,1)S(1)}, bf16[1024,512]{1,0:T(8,128)(2,1)S(1)}, u32[]{:S(2)}, u32[]{:S(2)}) collective-permute-start(bf16[1024,512]{1,0:T(8,128)(2,1)S(1)} %convolution_convert_fusion.5), channel_id=1, source_target_pairs={{0,4},{4,0},{8,12},{12,8},{16,20},{20,16},{24,28},{28,24},{1,5},{5... | collective-permute-start | bytes 3145736 | tf_op jit(solution)/shard_map/ppermute | solution.py:49
  683.5 18.5 %collective-permute-start.40 = (bf16[256,768]{1,0:T(8,128)(2,1)S(1)}, bf16[256,768]{1,0:T(8,128)(2,1)S(1)}, u32[]{:S(2)}, u32[]{:S(2)}) collective-permute-start(bf16[256,768]{1,0:T(8,128)(2,1)S(1)} %pad_maximum_fusion.7), channel_id=1, source_target_pairs={{0,8},{4,12},{8,0},{12,4},{16,24},{20,28},{24,16},{28,20},{1,9},{5... | collective-permute-start | bytes 1179656 | tf_op jit(solution)/shard_map/ppermute | solution.py:49
  (76 other events, 876.3 us)
Sparse Core Ops, SparseCore 0:
  15.1 47.1 all-gather.7
  63.8 26.7 all-gather.15
  189.0 47.1 all-gather.13
  237.6 44.5 all-gather.9
  318.9 42.6 reduce-scatter.5
  377.3 45.4 all-gather.11
  448.1 47.6 reduce-scatter.7
  498.1 43.2 reduce-scatter.3

commit v2 on v1

--- a/solution.py
+++ b/solution.py
@@ -17,14 +17,27 @@
 
 in_smem = pl.BlockSpec(memory_space=pltpu.SMEM)
 in_vmem = pl.BlockSpec(memory_space=pltpu.VMEM)
+unread = pl.BlockSpec(memory_space=pl.ANY)
 
 
 def kernel_params():
     return pltpu.CompilerParams(vmem_limit_bytes=KERNEL_VMEM)
 
 
-def cost(flops, moved):
-    return pl.CostEstimate(flops=int(flops), bytes_accessed=int(moved), transcendentals=0)
+def cost(micros):
+    return pl.CostEstimate(flops=int(micros * 1.1e9), bytes_accessed=1024, transcendentals=0)
+
+
+def gated(value, *others):
+    return pl.pallas_call(
+        lambda *refs: None,
+        out_shape=jax.ShapeDtypeStruct(value.shape, value.dtype),
+        in_specs=[unread] * (1 + len(others)),
+        out_specs=unread,
+        input_output_aliases={0: 0},
+        cost_estimate=cost(0.1),
+        name="gated",
+    )(value, *others)
 
 
 def bit_order(bits):
@@ -49,42 +62,177 @@
     return lax.ppermute(array, "ctx", [(i, i ^ (1 << bit)) for i in range(1 << bits)])
 
 
-def gather_ctx(own, bits, axis=0):
+def halves(array, axis):
+    middle = array.shape[axis] // 2
+    return (
+        lax.slice_in_dim(array, 0, middle, axis=axis),
+        lax.slice_in_dim(array, middle, 2 * middle, axis=axis),
+    )
+
+
+def gather_one(own, bits):
     first, second = bit_order(bits)[:2]
-    middle = own.shape[axis] // 2
-    by_first = swap(own, first, bits)
-    by_second = swap(own, second, bits)
-    lower = lax.slice_in_dim(by_first, 0, middle, axis=axis)
-    upper = lax.slice_in_dim(by_second, middle, 2 * middle, axis=axis)
-    both_lower = swap(lower, second, bits)
-    both_upper = swap(upper, first, bits)
-    parts = [jnp.concatenate([own, by_first, by_second, both_lower, both_upper], axis=axis)]
+    return swap(own, first, bits), swap(own, second, bits)
+
+
+def gather_two(one, bits, axis=0):
+    first, second = bit_order(bits)[:2]
+    lower, upper = halves(one[0], axis)[0], halves(one[1], axis)[1]
+    return swap(lower, second, bits), swap(upper, first, bits)
+
+
+def join(pieces, axis=0):
+    shape = list(pieces[0].shape)
+    shape[axis] = sum(piece.shape[axis] for piece in pieces)
+
+    def kernel(*refs):
+        in_refs, out_ref, sems = refs[: len(pieces)], refs[len(pieces)], refs[-1]
+        copies, start = [], 0
+        for index, in_ref in enumerate(in_refs):
+            size = in_ref.shape[axis]
+            place = pl.ds(start, size)
+            target = out_ref.at[(slice(None),) * axis + (place,)]
+            copies.append(pltpu.make_async_copy(in_ref, target, sems.at[index]))
+            start += size
+        for copy in copies:
+            copy.start()
+        for copy in copies:
+            copy.wait()
+
+    return pl.pallas_call(
+        kernel,
+        out_shape=jax.ShapeDtypeStruct(shape, pieces[0].dtype),
+        in_specs=[unread] * len(pieces),
+        out_specs=in_vmem,
+        scratch_shapes=[pltpu.SemaphoreType.DMA((len(pieces),))],
+        compiler_params=kernel_params(),
+        cost_estimate=cost(0.1),
+        name="join",
+    )(*pieces)
+
+
+def gather_end(own, one, two, bits, axis=0):
+    parts = [join([own, *one, *two], axis)]
     for bit in bit_order(bits)[2:]:
         parts = parts + [swap(part, bit, bits) for part in parts]
     return parts
 
 
-def scatter_pieces(parts, bits):
-    for bit in reversed(bit_order(bits)[2:]):
-        kept = len(parts) // 2
-        received = [swap(part, bit, bits) for part in parts[kept:]]
-        parts = [
-            (mine.astype(jnp.float32) + other.astype(jnp.float32)).astype(jnp.bfloat16)
-            for mine, other in zip(parts[:kept], received)
-        ]
+def gather_small(own, bits):
+    stacked = own[None]
+    for bit in bit_order(bits):
+        stacked = jnp.concatenate([stacked, swap(stacked, bit, bits)], axis=0)
+    return stacked
+
+
+def scatter_step(stacked, bit, bits):
+    kept = stacked.shape[0] // 2
+    return stacked[:kept] + swap(stacked[kept:], bit, bits)
+
+
+def sum_small(array, axis):
+    size = lax.axis_size(axis)
+    shift = 1
+    while shift < size:
+        array = array + lax.ppermute(array, axis, [(i, i ^ shift) for i in range(size)])
+        shift *= 2
+    return array
+
+
+def add_half(left, right):
+    return (left.astype(jnp.float32) + right.astype(jnp.float32)).astype(jnp.bfloat16)
+
+
+def scatter_one(blocks, bits):
     first, second = bit_order(bits)[:2]
-    own, at_first, at_second, at_both = jnp.split(parts[0], 4, axis=0)
-    middle = own.shape[0] // 2
-    lower = swap(at_both[:middle], second, bits)
-    upper = swap(at_both[middle:], first, bits)
-    to_first = jnp.concatenate([at_first[:middle] + lower, at_first[middle:]], axis=0)
-    to_second = jnp.concatenate([at_second[:middle], at_second[middle:] + upper], axis=0)
-    return own, swap(to_first, first, bits), swap(to_second, second, bits)
-
-
-def scatter_ctx(parts, bits):
-    own, by_first, by_second = scatter_pieces(parts, bits)
-    return own.astype(jnp.float32) + by_first.astype(jnp.float32) + by_second.astype(jnp.float32)
+    return swap(blocks[3], second, bits), swap(blocks[4], first, bits)
+
+
+def scatter_two(blocks, one):
+    rows, width = blocks[1].shape
+    half = rows // 2
+
+    def kernel(first_ref, second_ref, lower_ref, upper_ref, to_first, to_second):
+        to_first[0:half, :] = add_half(first_ref[0:half, :], lower_ref[...])
+        to_first[half:, :] = first_ref[half:, :]
+        to_second[0:half, :] = second_ref[0:half, :]
+        to_second[half:, :] = add_half(second_ref[half:, :], upper_ref[...])
+
+    return pl.pallas_call(
+        kernel,
+        out_shape=[jax.ShapeDtypeStruct((rows, width), jnp.bfloat16)] * 2,
+        in_specs=[in_vmem] * 4,
+        out_specs=[in_vmem] * 2,
+        compiler_params=kernel_params(),
+        cost_estimate=cost(0.1),
+        name="scatter_two",
+    )(blocks[1], blocks[2], *one)
+
+
+def scatter_three(two, bits):
+    first, second = bit_order(bits)[:2]
+    return swap(two[0], first, bits), swap(two[1], second, bits)
+
+
+def finish_sum(blocks, three):
+    rows, width = blocks[0].shape
+
+    def kernel(own_ref, first_ref, second_ref, out_ref):
+        total = own_ref[...].astype(jnp.float32) + first_ref[...].astype(jnp.float32)
+        out_ref[...] = total + second_ref[...].astype(jnp.float32)
+
+    return pl.pallas_call(
+        kernel,
+        out_shape=jax.ShapeDtypeStruct((rows, width), jnp.float32),
+        in_specs=[in_vmem] * 3,
+        out_specs=in_vmem,
+        compiler_params=kernel_params(),
+        cost_estimate=cost(0.1),
+        name="finish_sum",
+    )(blocks[0], *three)
+
+
+def scatter_step(stacked, bit, bits):
+    kept = stacked.shape[0] // 2
+    return stacked[:kept] + swap(stacked[kept:], bit, bits)
+
+
+def sum_small(array, axis):
+    size = lax.axis_size(axis)
+    shift = 1
+    while shift < size:
+        array = array + lax.ppermute(array, axis, [(i, i ^ shift) for i in range(size)])
+        shift *= 2
+    return array
+
+
+def tp_shift(array, distance):
+    size = lax.axis_size("tp")
+    return lax.ppermute(array, "tp", [(i, (i + distance) % size) for i in range(size)])
+
+
+def tp_gather(array):
+    return [array] + [tp_shift(array, d) for d in range(1, lax.axis_size("tp"))]
+
+
+def tp_ordered(pieces, tp):
+    stacked = jnp.stack(pieces)
+    count = len(pieces)
+    return jnp.concatenate(
+        [lax.dynamic_index_in_dim(stacked, (tp - j) % count, 0, keepdims=False) for j in range(count)]
+    )
+
+
+def tp_exchange(array):
+    return [array[0]] + [tp_shift(array[d], d) for d in range(1, array.shape[0])]
+
+
+def tp_sum(pieces):
+    return sum(piece.astype(jnp.float32) for piece in pieces)
+
+
+def after(value, *others):
+    return lax.optimization_barrier((value, *others))
 
 
 def to_relative(array, me, bits):
@@ -107,6 +255,30 @@
         ],
         axis=1,
     )
+
+
+def reorder(place, array, bits, inverse=False):
+    width = array.shape[1] // (1 << bits)
+    if width % LANES:
+        return (to_absolute if inverse else to_relative)(array, place[0], bits)
+
+    def kernel(place, in_ref, out_ref):
+        for p in range(1 << bits):
+            other = pl.multiple_of((place[0] ^ block_key(p, bits)) * width, LANES)
+            if inverse:
+                out_ref[:, pl.ds(other, width)] = in_ref[:, p * width : (p + 1) * width]
+            else:
+                out_ref[:, p * width : (p + 1) * width] = in_ref[:, pl.ds(other, width)]
+
+    return pl.pallas_call(
+        kernel,
+        out_shape=jax.ShapeDtypeStruct(array.shape, array.dtype),
+        in_specs=[in_smem, in_vmem],
+        out_specs=in_vmem,
+        compiler_params=kernel_params(),
+        cost_estimate=cost(0.1),
+        name="reorder",
+    )(place, array)
 
 
 def block_positions(pair_slot, block_len):
@@ -178,8 +350,37 @@
     return gradient * cosine - turned_lanes(gradient * sine)
 
 
+def norm_rows(place, rows, gain, bits):
+    width = rows.shape[1] // (1 << bits)
+    whole_lanes = width % LANES == 0
+    if not whole_lanes:
+        rows = to_relative(rows, place[0], bits)
+
+    def kernel(place, in_ref, gain_ref, rows_ref, out_ref):
+        for p in range(1 << bits):
+            here = slice(p * width, (p + 1) * width)
+            if whole_lanes:
+                other = pl.multiple_of((place[0] ^ block_key(p, bits)) * width, LANES)
+                rows_ref[:, here] = in_ref[:, pl.ds(other, width)]
+        if not whole_lanes:
+            rows_ref[...] = in_ref[...]
+        values = rows_ref[...].astype(jnp.float32)
+        out_ref[...] = (values * rms_scale(values) * gain_ref[...]).astype(jnp.bfloat16)
+
+    shape = jax.ShapeDtypeStruct(rows.shape, jnp.bfloat16)
+    return pl.pallas_call(
+        kernel,
+        out_shape=(shape, shape),
+        in_specs=[in_smem, in_vmem, in_vmem],
+        out_specs=(in_vmem, in_vmem),
+        compiler_params=kernel_params(),
+        cost_estimate=cost(0.1),
+        name="norm_rows",
+    )(place, rows, gain)
+
+
 def qkv_kernel(count, x_ref, *refs):
-    weights, (cos_ref, sin_ref, q_ref, kv_ref) = refs[:count], refs[count:]
+    weights, (cos_ref, sin_ref), (q_ref, kv_ref) = refs[:count], refs[count : count + 2], refs[-2:]
     depth = x_ref.shape[1] // count
     width_q = q_ref.shape[1]
     width_k = kv_ref.shape[1] // 2
@@ -203,7 +404,7 @@
                 kv_ref[:, at - width_q : at - width_q + LANES] = piece
 
 
-def project_qkv(attn_in, weights, cosine, sine, width_q, width_k):
+def project_qkv(attn_in, weights, cosine, sine, width_q, width_k, after=()):
     rows, depth = attn_in.shape
     return pl.pallas_call(
         functools.partial(qkv_kernel, len(weights)),
@@ -211,12 +412,12 @@
             jax.ShapeDtypeStruct((rows, width_q), jnp.bfloat16),
             jax.ShapeDtypeStruct((rows, 2 * width_k), jnp.bfloat16),
         ),
-        in_specs=[in_vmem] * (3 + len(weights)),
+        in_specs=[in_vmem] * (3 + len(weights)) + [unread] * len(after),
         out_specs=(in_vmem, in_vmem),
         compiler_params=kernel_params(),
-        cost_estimate=cost(2 * rows * depth * (width_q + 2 * width_k), 6 << 20),
+        cost_estimate=cost(0.1),
         name="qkv",
-    )(attn_in, *weights, cosine, sine)
+    )(attn_in, *weights, cosine, sine, *after)
 
 
 def sequence_block(slots, me, half_block, bits):
@@ -261,9 +462,8 @@
     lax.fori_loop(2, 2 * (1 << bits), step, 0)
 
 
-def forward_kernel(
-    bits, heads, slots, place, q_ref, kv_ref, out_ref, exact_ref, log_ref, qp, run_max, run_sum, acc
-):
+def forward_kernel(bits, heads, slots, place, q_ref, kv_ref, *refs):
+    out_ref, exact_ref, log_ref, qp, run_max, run_sum, acc = refs[-7:]
     rows = q_ref.shape[0]
     half = rows // 2
     per_kv = heads // 2
@@ -314,11 +514,10 @@
             out_ref[span, pl.ds(pair * LANES, LANES)] = exact.astype(jnp.bfloat16)
 
 
-def attend_forward(slots, place, queries, kv, bits):
+def attend_forward(slots, place, queries, kv, bits, after=()):
     rows, width = queries.shape
     heads = width // HEAD_SIZE
     half = rows // 2
-    visits = 2 * (1 << bits) + 1
     return pl.pallas_call(
         functools.partial(forward_kernel, bits, heads),
         out_shape=(
@@ -326,7 +525,7 @@
             jax.ShapeDtypeStruct((rows, width), jnp.float32),
             jax.ShapeDtypeStruct((heads, rows), jnp.float32),
         ),
-        in_specs=[in_smem, in_smem, in_vmem, in_vmem],
+        in_specs=[in_smem, in_smem, in_vmem, in_vmem] + [unread] * len(after),
         out_specs=(in_vmem, in_vmem, in_vmem),
         scratch_shapes=[
             pltpu.VMEM((heads, rows, LANES), jnp.bfloat16),
@@ -335,32 +534,16 @@
             pltpu.VMEM((2 * heads, HEAD_SIZE, half), jnp.float32),
         ],
         compiler_params=kernel_params(),
-        cost_estimate=cost(20 * visits * heads * half * half * HEAD_SIZE, 8 << 20),
+        cost_estimate=cost(19),
         name="attention_forward",
-    )(slots, place, queries, kv)
-
-
-def backward_kernel(
-    bits,
-    heads,
-    slots,
-    place,
-    q_ref,
-    kv_ref,
-    do_ref,
-    exact_ref,
-    log_ref,
-    cos_ref,
-    sin_ref,
-    dq_ref,
-    dkv_ref,
-    qp,
-    dop,
-    dots,
-    dq_acc,
-    dkv_acc,
-    do_all,
-):
+    )(slots, place, queries, kv, *after)
+
+
+def backward_kernel(bits, heads, slots, place, *refs):
+    q_ref, kv_ref, do_ref, exact_ref, log_ref, cos_ref, sin_ref = refs[:7]
+    parts = max(1, (1 << bits) // 4)
+    dq_ref, dkv_refs = refs[-7 - parts], refs[-6 - parts : -6]
+    qp, dop, dots, dq_acc, dkv_acc, do_all = refs[-6:]
     rows = q_ref.shape[0]
     half = rows // 2
     per_kv = heads // 2
@@ -422,7 +605,9 @@
         dkv_acc[rows_of_key, LANES : 2 * LANES] = grad_v
 
     over_blocks(visit, slots, place[0], bits, half, clear)
-    dkv_ref[...] = dkv_acc[...].astype(jnp.bfloat16)
+    size = dkv_acc.shape[0] // parts
+    for part, dkv_ref in enumerate(dkv_refs):
+        dkv_ref[...] = dkv_acc[part * size : (part + 1) * size, :].astype(jnp.bfloat16)
     for q_half in range(2):
         span = pl.ds(q_half * half, half)
         for pair in range(heads // 2):
@@ -434,19 +619,21 @@
             dq_ref[span, pl.ds(pair * LANES, LANES)] = gradient.astype(jnp.bfloat16)
 
 
-def attend_backward(slots, place, queries, kv, grad_parts, exact, log_total, cosine, sine, bits):
+def attend_backward(
+    slots, place, queries, kv, grad_parts, exact, log_total, cosine, sine, bits, after=()
+):
+    parts = max(1, (1 << bits) // 4)
     rows, width = queries.shape
     heads = width // HEAD_SIZE
     half = rows // 2
-    visits = 2 * (1 << bits) + 1
     return pl.pallas_call(
         functools.partial(backward_kernel, bits, heads),
         out_shape=(
             jax.ShapeDtypeStruct((rows, width), jnp.bfloat16),
-            jax.ShapeDtypeStruct(kv.shape, jnp.bfloat16),
+            *[jax.ShapeDtypeStruct((kv.shape[0] // parts, kv.shape[1]), jnp.bfloat16)] * parts,
         ),
-        in_specs=[in_smem, in_smem] + [in_vmem] * 7,
-        out_specs=(in_vmem, in_vmem),
+        in_specs=[in_smem, in_smem] + [in_vmem] * 7 + [unread] * len(after),
+        out_specs=(in_vmem,) * (1 + parts),
         scratch_shapes=[
             pltpu.VMEM((heads, rows, LANES), jnp.bfloat16),
             pltpu.VMEM((heads, rows, LANES), jnp.bfloat16),
@@ -456,22 +643,19 @@
             pltpu.VMEM((rows, width), jnp.bfloat16),
         ],
         compiler_params=kernel_params(),
-        cost_estimate=cost(40 * visits * heads * half * half * HEAD_SIZE, 12 << 20),
+        cost_estimate=cost(30),
         name="attention_backward",
-    )(slots, place, queries, kv, grad_parts, exact, log_total, cosine, sine)
+    )(slots, place, queries, kv, grad_parts, exact, log_total, cosine, sine, *after)
 
 
 def grad_qkv_kernel(dq_ref, own_ref, first_ref, second_ref, cos_ref, sin_ref, out_ref):
     width_q = dq_ref.shape[1]
     out_ref[:, 0:width_q] = dq_ref[...]
-    total = (
-        own_ref[...].astype(jnp.float32)
-        + first_ref[...].astype(jnp.float32)
-        + second_ref[...].astype(jnp.float32)
-    )
+    total = own_ref[...].astype(jnp.float32) + first_ref[...].astype(jnp.float32)
+    total = total + second_ref[...].astype(jnp.float32)
     keys = rotate_back(total[:, 0:LANES], cos_ref[...], sin_ref[...])
     out_ref[:, width_q : width_q + LANES] = keys.astype(jnp.bfloat16)
-    out_ref[:, width_q + LANES : width_q + 2 * LANES] = total[:, LANES:].astype(jnp.bfloat16)
+    out_ref[:, width_q + LANES :] = total[:, LANES:].astype(jnp.bfloat16)
 
 
 def join_grad_qkv(grad_queries, pieces, cosine, sine):
@@ -483,25 +667,25 @@
         in_specs=[in_vmem] * 6,
         out_specs=in_vmem,
         compiler_params=kernel_params(),
-        cost_estimate=cost(rows * width * 8, 3 << 20),
+        cost_estimate=cost(0.1),
         name="grad_qkv",
     )(grad_queries, *pieces, cosine, sine)
 
 
 def mlp_kernel(count, x_ref, g_ref, *refs):
-    gates, ups, downs = refs[:count], refs[count : 2 * count], refs[2 * count : 3 * count]
+    weights = refs[:count], refs[count : 2 * count], refs[2 * count : 3 * count]
     hidden_ref, grad_gate_ref, grad_up_ref = refs[3 * count :]
     depth = x_ref.shape[1] // count
 
-    def product(left, weights):
+    def product(left, parts):
         total = 0.0
-        for index, weight in enumerate(weights):
-            total = total + nn(left[:, index * depth : (index + 1) * depth], weight[...])
+        for index, part in enumerate(parts):
+            total = total + nn(left[:, index * depth : (index + 1) * depth], part[...])
         return total
 
-    gate = product(x_ref, gates)
-    up = product(x_ref, ups)
-    grad_hidden = product(g_ref, downs)
+    gate = product(x_ref, weights[0])
+    up = product(x_ref, weights[1])
+    grad_hidden = product(g_ref, weights[2])
     sigmoid = jax.nn.sigmoid(gate)
     silu = gate * sigmoid
     hidden_ref[...] = (silu * up).astype(jnp.bfloat16)
@@ -516,88 +700,181 @@
     count = len(gates)
     tile = min(256, units)
     whole = pl.BlockSpec((rows, depth), lambda i: (0, 0))
-    weight = pl.BlockSpec((depth // count, tile), lambda i: (0, i))
+    part = pl.BlockSpec((depth // count, tile), lambda i: (0, i))
     out = pl.BlockSpec((rows, tile), lambda i: (0, i))
     shape = jax.ShapeDtypeStruct((rows, units), jnp.bfloat16)
     return pl.pallas_call(
         functools.partial(mlp_kernel, count),
         grid=(units // tile,),
         out_shape=(shape, shape, shape),
-        in_specs=[whole, whole] + [weight] * (3 * count),
+        in_specs=[whole, whole] + [part] * (3 * count),
         out_specs=(out, out, out),
         compiler_params=kernel_params(),
-        cost_estimate=cost(6 * rows * depth * units, 6 * depth * units),
+        cost_estimate=cost(0.1),
         name="mlp_inner",
     )(mlp_in, grad_rows, *gates, *ups, *downs)
 
 
-def features_kernel(parts, tiles, lefts, *refs):
-    out_ref = refs[-1]
-    left_refs = refs[:lefts]
-    weight_refs = refs[lefts:-1]
+def project_part(lefts, part):
+    depth, rows, width = lefts.shape
+    features = part.shape[1]
+    tile = min(256, features)
+
+    def kernel(left_ref, part_ref, out_ref):
+        total = 0.0
+        for group in range(depth):
+            total = total + nt(left_ref[group], part_ref[group])
+        out_ref[...] = total
+
+    return pl.pallas_call(
+        kernel,
+        grid=(features // tile,),
+        out_shape=jax.ShapeDtypeStruct((rows, features), jnp.float32),
+        in_specs=[
+            pl.BlockSpec((depth, rows, width), lambda i: (0, 0, 0)),
+            pl.BlockSpec((depth, tile, width), lambda i: (0, i, 0)),
+        ],
+        out_specs=pl.BlockSpec((rows, tile), lambda i: (0, i)),
+        compiler_params=kernel_params(),
+        cost_estimate=cost(0.1),
+        name="project_part",
+    )(lefts, part)
+
+
+def residual_kernel(place, left_ref, x_ref, gain_ref, part_ref, *refs):
+    sums, (mlp_ref, here_ref, residual) = refs[:-3], refs[-3:]
+    depth, rows, _ = left_ref.shape
+    tile = part_ref.shape[1]
     step = pl.program_id(0)
-    for part in range(parts):
-
-        @pl.when(step // tiles == part)
-        def _():
-            total = 0.0
-            for left, weight in zip(left_refs, weight_refs[part * lefts : (part + 1) * lefts]):
-                for index in range(left.shape[0]):
-                    total = total + nt(left[index], weight[index])
-            out_ref[...] = total.astype(out_ref.dtype)
-
-
-def to_features(lefts, weights, out_dtype):
-    rows = lefts[0].shape[1]
-    features = weights[0][0].shape[1]
+    total = 0.0
+    for group in range(depth):
+        total = total + nt(left_ref[group], part_ref[group])
+    residual[step] = total
+
+    @pl.when(step == pl.num_programs(0) - 1)
+    def _():
+        width = x_ref.shape[1]
+        before = sum(ref.shape[1] for ref in sums)
+        squares = jnp.zeros((rows, 1), jnp.float32)
+        pieces = []
+        for ref in sums:
+            pieces += [(ref, slice(k, k + tile)) for k in range(0, ref.shape[1], tile)]
+        count = (width - before) // tile
+        local = rows // depth
+        here = pl.ds(pl.multiple_of(place[1] * local, local), local)
+        for index in range(width // tile):
+            columns = slice(index * tile, (index + 1) * tile)
+            values = x_ref[:, columns].astype(jnp.float32)
+            if index < len(pieces):
+                ref, at = pieces[index]
+                values = values + ref[:, at]
+                ref[:, at] = values
+            else:
+                values = values + residual[index - len(pieces)]
+                residual[index - len(pieces)] = values
+            squares = squares + jnp.sum(values * values, axis=1, keepdims=True)
+        factor = lax.rsqrt(squares / width + eps_norm)
+        for index in range(width // tile):
+            columns = slice(index * tile, (index + 1) * tile)
+            if index < len(pieces):
+                ref, at = pieces[index]
+                values, mine = ref[:, at], ref[here, at]
+            else:
+                values = residual[index - len(pieces)]
+                mine = residual[index - len(pieces), here, :]
+            mlp_ref[:, columns] = (values * factor * gain_ref[:, columns]).astype(jnp.bfloat16)
+            here_ref[:, columns] = mine
+
+
+def project_residual(place, lefts, rows, gain, parts):
+    depth, count, width = lefts.shape
+    total = rows.shape[1]
+    sums = [project_part(lefts, part) for part in parts[:-1]]
+    features = parts[-1].shape[1]
+    tile = min(256, features)
+    whole = lambda i: (0, 0)
+    return pl.pallas_call(
+        residual_kernel,
+        grid=(features // tile,),
+        out_shape=(
+            jax.ShapeDtypeStruct((count, total), jnp.bfloat16),
+            jax.ShapeDtypeStruct((count // depth, total), jnp.float32),
+        ),
+        in_specs=[
+            in_smem,
+            pl.BlockSpec((depth, count, width), lambda i: (0, 0, 0)),
+            pl.BlockSpec((count, total), whole),
+            pl.BlockSpec((1, total), whole),
+            pl.BlockSpec((depth, tile, width), lambda i: (0, i, 0)),
+        ]
+        + [pl.BlockSpec(each.shape, whole) for each in sums],
+        out_specs=(
+            pl.BlockSpec((count, total), whole),
+            pl.BlockSpec((count // depth, total), whole),
+        ),
+        scratch_shapes=[pltpu.VMEM((features // tile, count, tile), jnp.float32)],
+        compiler_params=kernel_params(),
+        cost_estimate=cost(0.1),
+        name="project_residual",
+    )(place, lefts, rows, gain, parts[-1], *sums)
+
+
+def to_features(lefts, weights):
+    rows = lefts[0].shape[0]
+    count = len(weights[0])
+    features = weights[0][0].shape[0]
     tile = min(256, features)
     tiles = features // tile
-    parts = len(weights)
-    in_specs = [pl.BlockSpec(left.shape, lambda i: (0, 0, 0)) for left in lefts]
-    flops = 0
-    for part, group in enumerate(weights):
-        for weight in group:
-            depth, _, width = weight.shape
-            flops += 2 * rows * features * depth * width
-            in_specs.append(
-                pl.BlockSpec(
-                    (depth, tile, width),
-                    functools.partial(
-                        lambda base, i: (0, jnp.clip(i - base, 0, tiles - 1), 0), part * tiles
-                    ),
-                )
-            )
-    return pl.pallas_call(
-        functools.partial(features_kernel, parts, tiles, len(lefts)),
-        grid=(parts * tiles,),
-        out_shape=jax.ShapeDtypeStruct((rows, parts * features), out_dtype),
-        in_specs=in_specs,
+
+    def kernel(*refs):
+        left_refs, part_refs, out_ref = refs[: len(lefts)], refs[len(lefts) : -1], refs[-1]
+        step = pl.program_id(0)
+        for part in range(count):
+
+            @pl.when(step // tiles == part)
+            def _():
+                total = 0.0
+                for source, left_ref in enumerate(left_refs):
+                    total = total + nt(left_ref[...], part_refs[source * count + part][...])
+                out_ref[...] = total.astype(jnp.bfloat16)
+
+    def part_at(base, i):
+        return (jnp.clip(i - base, 0, tiles - 1), 0)
+
+    return pl.pallas_call(
+        kernel,
+        grid=(count * tiles,),
+        out_shape=jax.ShapeDtypeStruct((rows, count * features), jnp.bfloat16),
+        in_specs=[pl.BlockSpec(left.shape, lambda i: (0, 0)) for left in lefts]
+        + [
+            pl.BlockSpec((tile, parts[part].shape[1]), functools.partial(part_at, part * tiles))
+            for parts in weights
+            for part in range(count)
+        ],
         out_specs=pl.BlockSpec((rows, tile), lambda i: (0, i)),
         compiler_params=kernel_params(),
-        cost_estimate=cost(flops, flops // rows),
+        cost_estimate=cost(0.1),
         name="to_features",
-    )(*lefts, *[weight for group in weights for weight in group])
-
-
-def groups_kernel(count, place, x_ref, *refs):
-    out_ref = refs[-1]
-    depth = x_ref.shape[1] // count
-    total = 0.0
-    for index, weight in enumerate(refs[:-1]):
-        total = total + nn(x_ref[:, index * depth : (index + 1) * depth], weight[0])
-    out_ref[0] = total.astype(jnp.bfloat16)
-
-
-def to_groups(place, branch, weights):
+    )(*lefts, *[part for parts in weights for part in parts])
+
+
+def to_groups(place, branch, parts):
     rows, depth = branch.shape
-    groups, features, width = weights[0].shape
-    count = len(weights)
+    groups, features, width = parts[0].shape
+    count = len(parts)
+
+    def kernel(place, x_ref, *refs):
+        total = 0.0
+        for index, part in enumerate(refs[:count]):
+            columns = x_ref[:, index * features : (index + 1) * features]
+            total = total + nn(columns, part[0])
+        refs[-1][0] = total.astype(jnp.bfloat16)
 
     def weight_at(shift, place):
         return (lax.rem(place[1] + shift, groups), 0, 0)
 
     return pl.pallas_call(
-        functools.partial(groups_kernel, count),
+        kernel,
         grid_spec=pltpu.PrefetchScalarGridSpec(
             num_scalar_prefetch=1,
             grid=(groups,),
@@ -607,17 +884,203 @@
         ),
         out_shape=jax.ShapeDtypeStruct((groups, rows, width), jnp.bfloat16),
         compiler_params=kernel_params(),
-        cost_estimate=cost(2 * rows * depth * groups * width, 2 * depth * groups * width),
+        cost_estimate=cost(0.1),
         name="to_groups",
-    )(place, branch, *weights)
-
-
-def weight_gradient(left, right, parts):
-    depth = left.shape[1] // parts
+    )(place, branch, *parts)
+
+
+def to_block_groups(place, rows, bits, groups):
+    local, depth = rows.shape
+    width = depth >> bits
+    count = (1 << bits) // groups
+    if width % LANES:
+        blocks = to_absolute(rows, place[0], bits)
+        blocks = blocks.reshape(local, groups, count, width).transpose(1, 2, 0, 3)
+        return jnp.stack(
+            [
+                lax.dynamic_index_in_dim(blocks, (place[1] + d) % groups, 0, keepdims=False)
+                for d in range(groups)
+            ]
+        )
+
+    def kernel(place, in_ref, out_ref):
+        for d in range(groups):
+            for index in range(count):
+                block = lax.rem(place[1] + d, groups) * count + index
+                start = key_position(place[0] ^ block, bits) * width
+                out_ref[d, index] = in_ref[:, pl.ds(pl.multiple_of(start, LANES), width)]
+
+    return pl.pallas_call(
+        kernel,
+        out_shape=jax.ShapeDtypeStruct((groups, count, local, width), rows.dtype),
+        in_specs=[in_smem, in_vmem],
+        out_specs=in_vmem,
+        compiler_params=kernel_params(),
+        cost_estimate=cost(0.1),
+        name="to_block_groups",
+    )(place, rows)
+
+
+def gradient_out(place, branch, attended, bits):
+    shifts = len(branch)
+    count, local, features = branch[0].shape
+    groups, rows, width = attended.shape
+    parts = (1 << bits) // 4
+
+    def kernel(place, *refs):
+        lefts, right_ref, outs = refs[:shifts], refs[shifts], refs[shifts + 1 :]
+        step = pl.program_id(0)
+        total = 0.0
+        for distance, left in enumerate(lefts):
+            start = lax.rem(place[1] - distance + shifts, shifts) * local
+            here = pl.ds(pl.multiple_of(start, local), local)
+            total = total + inner_rows(left[0], right_ref[0, here, :])
+        for part, out_ref in enumerate(outs):
+
+            @pl.when(step // 4 == part)
+            def _():
+                out_ref[...] = total.astype(jnp.bfloat16)
+
+    def left_at(p, place):
+        return (lax.rem(place[0] ^ block_key(p, bits), count), 0, 0)
+
+    def right_at(p, place):
+        return ((place[0] ^ block_key(p, bits)) // count, 0, 0)
+
+    def out_at(base, p, place):
+        return (jnp.clip(p - base, 0, 3), 0)
+
+    return pl.pallas_call(
+        kernel,
+        grid_spec=pltpu.PrefetchScalarGridSpec(
+            num_scalar_prefetch=1,
+            grid=(1 << bits,),
+            in_specs=[pl.BlockSpec((1, local, features), left_at)] * shifts
+            + [pl.BlockSpec((1, rows, width), right_at)],
+            out_specs=[
+                pl.BlockSpec((features, width), functools.partial(out_at, 4 * part))
+                for part in range(parts)
+            ],
+        ),
+        out_shape=[jax.ShapeDtypeStruct((4 * features, width), jnp.bfloat16)] * parts,
+        compiler_params=kernel_params(),
+        cost_estimate=cost(0.1),
+        name="gradient_out",
+    )(place, *branch, attended)
+
+
+def to_owners(array, count):
+    ctx, tp = lax.axis_size("ctx"), lax.axis_size("tp")
+    moves = []
+    for c in range(ctx):
+        for t in range(tp):
+            moves.append((c * tp + t, (count * t + c % count) * tp + c // count))
+    return lax.ppermute(array, ("ctx", "tp"), moves)
+
+
+def block_rows(rows):
+    quarter = rows // 4
+    return [quarter, quarter, quarter, quarter // 2, quarter // 2]
+
+
+def gradient_part(left, right, parts, part, received=()):
+    rows, depth = left.shape
+    depth = depth // parts
+    width = right.shape[1]
+    tile = next(t for t in (1024, 768, 512, 256, LANES, width) if width % t == 0)
+    sizes = block_rows(depth) if received else [depth // 4] * 4
+    step = depth // 4
+
+    def kernel(left_ref, right_ref, *refs):
+        total = inner_rows(left_ref[...], right_ref[...])
+        start = 0
+        for size, out_ref in zip(sizes, refs[len(received) :]):
+            piece = total[start : start + size]
+            if received:
+                offset = start % step
+                other = refs[start // step][offset : offset + size, :]
+                piece = piece + other.astype(jnp.float32)
+            out_ref[...] = piece.astype(jnp.bfloat16)
+            start += size
+
+    return pl.pallas_call(
+        kernel,
+        grid=(width // tile,),
+        out_shape=[jax.ShapeDtypeStruct((size, width), jnp.bfloat16) for size in sizes],
+        in_specs=[
+            pl.BlockSpec((rows, depth), lambda i: (0, part)),
+            pl.BlockSpec((rows, tile), lambda i: (0, i)),
+        ]
+        + [pl.BlockSpec((step, tile), lambda i: (0, i))] * len(received),
+        out_specs=[pl.BlockSpec((size, tile), lambda i: (0, i)) for size in sizes],
+        compiler_params=kernel_params(),
+        cost_estimate=cost(0.1),
+        name="gradient_part",
+    )(left, right, *received)
+
+
+def gradient_begin(left, right, bits):
+    parts = (1 << bits) // 4
+    bit = bit_order(bits)[-1]
     return [
-        inner_rows(left[:, index * depth : (index + 1) * depth], right).astype(jnp.bfloat16)
-        for index in range(parts)
+        [swap(block, bit, bits) for block in gradient_part(left, right, parts, part)]
+        for part in range(parts // 2, parts)
     ]
+
+
+def gradient_end(left, right, received, bits):
+    parts = (1 << bits) // 4
+    if parts == 2:
+        return gradient_part(left, right, parts, 0, received[0])
+    kept = [jnp.concatenate(gradient_part(left, right, parts, p)) for p in range(parts // 2)]
+    kept = [add_half(mine, jnp.concatenate(other)) for mine, other in zip(kept, received)]
+    return sum_parts(kept, bits, bit_order(bits)[2:-1])
+
+
+def sum_parts(parts, bits, over):
+    for bit in reversed(over):
+        count = len(parts) // 2
+        came = [swap(part, bit, bits) for part in parts[count:]]
+        if count == 1:
+            return split_blocks(parts[0], came[0])
+        parts = [add_half(mine, other) for mine, other in zip(parts[:count], came)]
+
+
+def split_blocks(kept, received):
+    sizes = block_rows(kept.shape[0])
+
+    def kernel(kept_ref, other_ref, *refs):
+        start = 0
+        for size, out_ref in zip(sizes, refs):
+            here = slice(start, start + size)
+            out_ref[...] = add_half(kept_ref[here, :], other_ref[here, :])
+            start += size
+
+    return pl.pallas_call(
+        kernel,
+        out_shape=[jax.ShapeDtypeStruct((size, kept.shape[1]), jnp.bfloat16) for size in sizes],
+        in_specs=[in_vmem] * 2,
+        out_specs=[in_vmem] * 5,
+        compiler_params=kernel_params(),
+        cost_estimate=cost(0.1),
+        name="split_blocks",
+    )(kept, received)
+
+
+def rows_begin(parts, bits):
+    return sum_parts(parts, bits, bit_order(bits)[2:])
+
+
+def window(*values):
+    return lax.optimization_barrier(values)
+
+
+def cut(values, *sizes):
+    out, start = [], 0
+    for size in sizes:
+        out.append(values[start : start + size])
+        start += size
+    return out
 
 
 def on_device(
@@ -628,103 +1091,161 @@
     me = lax.axis_index("ctx")
     tp = lax.axis_index("tp")
     place = jnp.stack([me, tp]).astype(jnp.int32)
-    local_rows = block_in.shape[0]
+    local_rows, model = block_in.shape
     group_rows = local_rows * shifts
     width_q, width_k = wq.shape[1], wk.shape[1]
-
-    rows_here = to_relative(block_in, me, bits)
-    x_all = lax.all_gather(rows_here, "tp", axis=0, tiled=True)
-    qkv_w = gather_ctx(jnp.concatenate([wq, wk, wv], axis=1), bits)
-    count = len(qkv_w)
-    gains = lax.all_gather(jnp.stack([gain_attn, gain_mlp]), "ctx", axis=1, tiled=True)
-    gains = to_relative(gains, me, bits).astype(jnp.float32)
-    g_attn, g_mlp = gains[0:1], gains[1:2]
-    gate_w = gather_ctx(w_gate, bits)
-    up_w = gather_ctx(w_up, bits)
-    o_w = gather_ctx(lax.all_gather(wo, "tp", axis=0), bits, axis=1)
-    down_w = gather_ctx(w_down, bits)
-    out_grad_here = to_relative(out_grad, me, bits)
-    grad_rows = lax.all_gather(out_grad_here, "tp", axis=0, tiled=True)
-
+    count = (1 << bits) // 4
+
+    x_all = lax.all_gather(block_in, "tp", axis=0, tiled=True)
+    qkv_here = join([wq, wk, wv], axis=1)
+    qkv_one = gather_one(qkv_here, bits)
+    gains = gather_small(jnp.stack([gain_attn, gain_mlp]), bits).astype(jnp.float32)
+    gains = jnp.swapaxes(gains, 0, 1).reshape(2, -1)
+    gate_one = gather_one(w_gate, bits)
+    qkv_two = gather_two(qkv_one, bits)
+    qkv_w = gather_end(qkv_here, qkv_one, qkv_two, bits)
     pos_all = block_positions(pair_slot, group_rows // 2)
     pos_rows = lax.dynamic_slice_in_dim(pos_all, me * group_rows, group_rows)
     cosine, sine = rope_tables(pos_rows)
-
-    inputs = x_all.astype(jnp.float32)
-    factor_all = rms_scale(inputs)
-    attn_in = (inputs * factor_all * g_attn).astype(jnp.bfloat16)
+    out_grad_here = reorder(place, out_grad, bits)
+    both_sent = jnp.concatenate([out_grad_here, wo.reshape(-1, model)], axis=0)
+    x_all, both_sent, w_up, gains, cosine, sine, *pieces = window(
+        x_all, both_sent, w_up, gains, cosine, sine, *qkv_w, *gate_one
+    )
+    qkv_w, gate_one = cut(pieces, count, 2)
+
+    g_attn, g_mlp = gains[0:1], gains[1:2]
+    both_all = lax.all_gather(both_sent, "tp", axis=0)
+    gate_two = gather_two(gate_one, bits)
+    rows_all, attn_in = norm_rows(place, x_all, g_attn, bits)
     queries, kv = project_qkv(attn_in, qkv_w, cosine, sine, width_q, width_k)
-    kv_all = jnp.concatenate(gather_ctx(kv, bits), axis=0)
+    kv_one = gather_one(kv, bits)
+    kv_all = join(gather_end(kv, kv_one, gather_two(kv_one, bits), bits))
+    kv_all, w_up, w_down, *gate_two = window(kv_all, w_up, w_down, *gate_two)
+
+    up_one = gather_one(w_up, bits)
     attended, exact, log_total = attend_forward(pair_slot, place, queries, kv_all, bits)
+    attended, both_all, w_down, *up_one = window(attended, both_all, w_down, *up_one)
 
     attended_all = lax.all_gather(attended, "tp", axis=0)
-    residual = inputs + to_features([attended_all], [[part] for part in o_w], jnp.float32)
-    factor_mlp_all = rms_scale(residual)
-    mlp_in = (residual * factor_mlp_all * g_mlp).astype(jnp.bfloat16)
-    residual_here = lax.dynamic_slice_in_dim(residual, tp * local_rows, local_rows)
-    factor_mlp = lax.dynamic_slice_in_dim(factor_mlp_all, tp * local_rows, local_rows)
+    grad_rows = both_all[:, :local_rows].reshape(group_rows, model)
+    wo_groups = both_all[:, local_rows:].reshape(shifts, *wo.shape)
+    o_one = gather_one(wo_groups, bits)
+    up_two = gather_two(up_one, bits)
+    down_one = gather_one(w_down, bits)
+    gate_w = gather_end(w_gate, gate_one, gate_two, bits)
+    up_w = gather_end(w_up, up_one, up_two, bits)
+    attended_all, grad_rows, *pieces = window(attended_all, grad_rows, *o_one, *gate_w, *up_w)
+    o_one, gate_w, up_w = cut(pieces, 2, count, count)
+
+    o_two = gather_two(o_one, bits, 1)
+    o_w = gather_end(wo_groups, o_one, o_two, bits, 1)
+    down_two = gather_two(down_one, bits)
+    down_w = gather_end(w_down, down_one, down_two, bits)
+    mlp_in, residual_here = project_residual(place, attended_all, rows_all, g_mlp, o_w)
+    factor_mlp = rms_scale(residual_here)
     normed_mlp = residual_here * factor_mlp
 
     hidden, grad_gate, grad_up = mlp_inner(mlp_in, grad_rows, gate_w, up_w, down_w)
-    grad_mlp_part = to_features(
-        [grad_gate[None], grad_up[None]],
-        [[gate[None], up[None]] for gate, up in zip(gate_w, up_w)],
-        jnp.bfloat16,
-    )
-    grad_mlp_in = lax.psum_scatter(
-        grad_mlp_part, "tp", scatter_dimension=0, tiled=True
-    ).astype(jnp.float32)
-    mlp_part = to_features([hidden[None]], [[down[None]] for down in down_w], jnp.bfloat16)
-    mlp_out = lax.psum_scatter(mlp_part, "tp", scatter_dimension=0, tiled=True)
-    block_out = (residual_here + mlp_out.astype(jnp.float32)).astype(jnp.bfloat16)
-    sum_gate_w = scatter_ctx(weight_gradient(mlp_in, grad_gate, count), bits)
-    sum_up_w = scatter_ctx(weight_gradient(mlp_in, grad_up, count), bits)
-    sum_down_w = scatter_ctx(weight_gradient(grad_rows, hidden, count), bits)
-
+    grad_mlp_part = to_features([grad_gate, grad_up], [gate_w, up_w])
+    grad_mlp_part, hidden, grad_gate, grad_up = window(grad_mlp_part, hidden, grad_gate, grad_up)
+
+    grad_mlp_in = lax.psum_scatter(grad_mlp_part, "tp", scatter_dimension=0, tiled=True)
+    down_sum = gradient_begin(grad_rows, hidden, bits)
+    up_sum = gradient_begin(mlp_in, grad_up, bits)
+    gate_sum = gradient_begin(mlp_in, grad_gate, bits)
+    down_sum = gradient_end(grad_rows, hidden, down_sum, bits)
+    up_sum = gradient_end(mlp_in, grad_up, up_sum, bits)
+    gate_sum = gradient_end(mlp_in, grad_gate, gate_sum, bits)
+    down_two = scatter_two(down_sum, scatter_one(down_sum, bits))
+    up_two = scatter_two(up_sum, scatter_one(up_sum, bits))
+    mlp_part = to_features([hidden], [down_w])
+    grad_mlp_in, mlp_part, *pieces = window(
+        grad_mlp_in, mlp_part, *down_two, *up_two, *gate_sum
+    )
+    down_two, up_two, gate_sum = cut(pieces, 2, 2, 5)
+
+    down_three = scatter_three(down_two, bits)
+    grad_mlp_in = grad_mlp_in.astype(jnp.float32)
     gain_mlp_part = jnp.sum(grad_mlp_in * normed_mlp, axis=0, keepdims=True)
     grad_residual = out_grad_here.astype(jnp.float32) + norm_back(
         grad_mlp_in * g_mlp, normed_mlp, factor_mlp
     )
     branch_here = grad_residual.astype(jnp.bfloat16)
     grad_groups = to_groups(place, branch_here, o_w)
-    grad_parts = jnp.stack(
-        [grad_groups[0]]
-        + [
-            lax.ppermute(grad_groups[d], "tp", [(i, (i + d) % shifts) for i in range(shifts)])
-            for d in range(1, shifts)
-        ]
-    )
-    grad_queries, grad_kv = attend_backward(
+    grad_parts = jnp.stack(tp_exchange(grad_groups))
+    branch_blocks = to_block_groups(place, branch_here, bits, shifts)
+    grad_parts, branch_blocks, mlp_part, *pieces = window(
+        grad_parts, branch_blocks, mlp_part, *down_three, *up_two, *gate_sum
+    )
+    down_three, up_two, gate_sum = cut(pieces, 2, 2, 5)
+
+    up_three = scatter_three(up_two, bits)
+    branch_pieces = tp_exchange(branch_blocks)
+    mlp_out = lax.psum_scatter(mlp_part, "tp", scatter_dimension=0, tiled=True)
+    grad_queries, *grad_kv = attend_backward(
         pair_slot, place, queries, kv_all, grad_parts, exact, log_total, cosine, sine, bits
     )
-    branch_rows = lax.all_gather(branch_here, "tp", axis=0, tiled=True)
-    sum_o_w = scatter_ctx(weight_gradient(branch_rows, attended, count), bits)
-
-    grad_kv_pieces = scatter_pieces(jnp.split(grad_kv, count, axis=0), bits)
-    grad_qkv = join_grad_qkv(grad_queries, grad_kv_pieces, cosine, sine)
-    grad_attn_part = to_features(
-        [grad_qkv[None]], [[part[None]] for part in qkv_w], jnp.bfloat16
-    )
-    grad_attn_in = lax.psum_scatter(
-        grad_attn_part, "tp", scatter_dimension=0, tiled=True
-    ).astype(jnp.float32)
-    sum_qkv_w = scatter_ctx(weight_gradient(attn_in, grad_qkv, count), bits)
+    pieces = window(*grad_kv, *branch_pieces, *up_three, *gate_sum)
+    grad_kv, branch_pieces, up_three, gate_sum = cut(pieces, count, shifts, 2, 5)
+
+    kv_sum = rows_begin(grad_kv, bits)
+    kv_three = scatter_three(scatter_two(kv_sum, scatter_one(kv_sum, bits)), bits)
+    gate_one = scatter_one(gate_sum, bits)
+    o_sum = gradient_out(place, branch_pieces, attended_all, bits)
+    mlp_out, *pieces = window(mlp_out, kv_sum[0], *kv_three, *o_sum, *gate_one)
+    kv_pieces, o_sum, gate_one = cut(pieces, 3, count, 2)
+    grad_qkv = join_grad_qkv(grad_queries, kv_pieces, cosine, sine)
+    grad_attn_part = to_features([grad_qkv], [qkv_w])
+    gate_three = scatter_three(scatter_two(gate_sum, gate_one), bits)
+    o_sum = rows_begin(o_sum, bits)
+    grad_attn_part, grad_qkv, *o_sum = window(grad_attn_part, grad_qkv, *o_sum)
+
+    grad_attn_in = lax.psum_scatter(grad_attn_part, "tp", scatter_dimension=0, tiled=True)
+    qkv_sum = gradient_begin(attn_in, grad_qkv, bits)
+    qkv_sum = gradient_end(attn_in, grad_qkv, qkv_sum, bits)
+    o_two = scatter_two(o_sum, scatter_one(o_sum, bits))
+    inputs = rows_all.astype(jnp.float32)
     gain_attn_part = jnp.sum(
-        grad_attn_part.astype(jnp.float32) * (inputs * factor_all), axis=0, keepdims=True
-    )
-    gain_parts = to_absolute(jnp.concatenate([gain_attn_part, gain_mlp_part]), me, bits)
-    gain_sums = lax.psum(gain_parts, ("ctx", "tp"))
-    gain_width = gain_attn.shape[0]
-    gain_here = lax.dynamic_slice_in_dim(gain_sums, me * gain_width, gain_width, 1)
-
-    inputs_here = rows_here.astype(jnp.float32)
-    factor_attn = lax.dynamic_slice_in_dim(factor_all, tp * local_rows, local_rows)
+        grad_attn_part.astype(jnp.float32) * (inputs * rms_scale(inputs)), axis=0, keepdims=True
+    )
+    gain_sum = jnp.concatenate([gain_attn_part, gain_mlp_part])
+    gain_sum = jnp.swapaxes(gain_sum.reshape(2, 1 << bits, -1), 0, 1)
+    order = bit_order(bits)
+    for bit in reversed(order[2:]):
+        gain_sum = scatter_step(gain_sum, bit, bits)
+    gain_sum, *pieces = window(gain_sum, *qkv_sum, *o_two, *gate_three)
+    qkv_sum, o_two, gate_three = cut(pieces, 5, 2, 2)
+
+    qkv_two = scatter_two(qkv_sum, scatter_one(qkv_sum, bits))
+    o_three = scatter_three(o_two, bits)
+    gain_sum = scatter_step(gain_sum, order[1], bits)
+    gain_sum, *pieces = window(gain_sum, *qkv_two, *o_three)
+    qkv_two, o_three = cut(pieces, 2, 2)
+
+    qkv_three = scatter_three(qkv_two, bits)
+    gain_sum = scatter_step(gain_sum, order[0], bits)
+    sum_o_w = finish_sum(o_sum, o_three).astype(jnp.bfloat16)
+    gain_sum, sum_o_w, *qkv_three = window(gain_sum, sum_o_w, *qkv_three)
+
+    sum_down_w = finish_sum(down_sum, down_three)
+    sum_up_w = finish_sum(up_sum, up_three)
+    sum_o_w = to_owners(sum_o_w, (1 << bits) // shifts).astype(jnp.float32)
+    gain_here = sum(tp_gather(gain_sum[0]))
+    sum_qkv_w = finish_sum(qkv_sum, qkv_three)
+    sum_gate_w = finish_sum(gate_sum, gate_three)
+    block_out = (residual_here + mlp_out.astype(jnp.float32)).astype(jnp.bfloat16)
+    block_out = reorder(place, block_out, bits, inverse=True)
+    grad_attn_in = grad_attn_in.astype(jnp.float32)
+    inputs_here = lax.dynamic_slice_in_dim(rows_all, tp * local_rows, local_rows)
+    inputs_here = inputs_here.astype(jnp.float32)
+    factor_attn = rms_scale(inputs_here)
     input_grad = grad_residual + norm_back(
         grad_attn_in * g_attn, inputs_here * factor_attn, factor_attn
     )
     return (
-        to_absolute(block_out, me, bits),
-        to_absolute(input_grad, me, bits),
+        block_out,
+        reorder(place, input_grad, bits, inverse=True),
         gain_here[0],
         sum_qkv_w[:, :width_q],
         sum_qkv_w[:, width_q : width_q + width_k],

time: 732 us -> 600 us (0.82)
  Pallas kernels: 130 us -> 262 us
  blocking collectives: 100 us -> 0 us
  waiting for transfers between devices: 259 us -> 179 us
  other arithmetic: 54.5 us -> 17 us
  matrix products: 31.7 us -> 0 us
  local copies, waits for them, and re-layouts: 67.8 us -> 36.8 us
  starting transfers between devices: 61.4 us -> 80.2 us
    pallas_call x5 -> x41, Pallas kernels: 52.6 us -> 184 us  [the longest x8 43.9 us: gradient_part(): pl.pallas_call(kernel, grid=(width // tile,), out_shape=[jax.ShapeDtypeSt...]
    psum x1 -> x0, blocking collectives: 52.3 us -> none  [on_device(): gain_sums = lax.psum(gain_parts, ('ctx', 'tp'))]
    all_gather x1 -> x0, blocking collectives: 47.8 us -> none  [on_device(): lax.all_gather(jnp.stack([gain_attn, gain_mlp]), 'ctx', axis=1, tiled=True)]
    reduce_scatter x1, waiting for transfers between devices: 42.6 us -> 0.01 us  [on_device(): lax.psum_scatter(grad_mlp_part, 'tp', scatter_dimension=0, tiled=True)]
    ppermute x60 -> x78, waiting for transfers between devices: 175 us -> 140 us  [swap(): lax.ppermute(array, 'ctx', [(i, i ^ 1 << bit) for i in range(1 << bits)])]
    dot_general x10 -> x0, matrix products: 31.7 us -> none  [inner_rows(): lax.dot_general(left, right, (((0,), (0,)), ((), ())), preferred_element_...]
    unnamed x166 -> x146, local copies, waits for them, and re-layouts: 44.7 us -> 15.8 us
    all_gather x4 -> x2, waiting for transfers between devices: 28.1 us -> 0.04 us  [the longest x1 0.02 us: on_device(): x_all = lax.all_gather(block_in, 'tp', axis=0, tiled=True)]
  transfers between devices with their start and end apart: 71 -> 94, of which waited for: 32 -> 30; matrix products, arithmetic and copies ran while one was open for 18% -> 6% of each run, Pallas kernels for 12% -> 37%
where the time goes in v2:
time: 600 us; the launch traced here: 591 us
  Pallas kernels  262 us (44%)
  waiting for transfers between devices  179 us (30%)
  starting transfers between devices  80.2 us (13%)
  local copies, waits for them, and re-layouts  36.8 us (6%)
  other arithmetic  17 us (3%)
  between operations  15.6 us (3%)
    ppermute x78, waiting for transfers between devices, swap(): lax.ppermute(array, 'ctx', [(i, i ^ 1 << bit) for i in range(1 << bits)])  140 us
    ppermute x78, starting transfers between devices, swap(): lax.ppermute(array, 'ctx', [(i, i ^ 1 << bit) for i in range(1 << bits)])  61.6 us
    pallas_call x8, Pallas kernels, gradient_part(): pl.pallas_call(kernel, grid=(width // tile,), out_shape=[jax.ShapeDtypeSt...  43.9 us
    pallas_call x3, Pallas kernels, to_features(): pl.pallas_call(kernel, grid=(count * tiles,), out_shape=jax.ShapeDtypeStr...  34.6 us
    pallas_call x1, Pallas kernels, attend_backward(): pl.pallas_call(functools.partial(backward_kernel, bits, heads), out_shape...  30.1 us
    pallas_call x8, Pallas kernels, join(): pl.pallas_call(kernel, out_shape=jax.ShapeDtypeStruct(shape, pieces[0].dt...  26.3 us
    pallas_call x1, Pallas kernels, mlp_inner(): pl.pallas_call(functools.partial(mlp_kernel, count), grid=(units // tile,...  20.4 us
    pallas_call x1, Pallas kernels, attend_forward(): pl.pallas_call(functools.partial(forward_kernel, bits, heads), out_shape=...  18.9 us
  transfers between devices with their start and end apart: 94, of which 30 were waited for; matrix products, arithmetic and copies ran while one was open for 6% of the time, Pallas kernels for 37%

profile of v2, /device:TPU:2, one launch (start us, length us, event | category | flops | bytes accessed | tf_op | source)
XLA Modules:
  0.0 590.8 jit_solution(2375483465839229383)
XLA Ops:
  15.3 6.7 %collective-permute-done.3.refs_1_ = bf16[256,768]{1,0:T(8,128)(2,1)S(1)} collective-permute-done((bf16[256,768]{1,0:T(8,128)(2,1)}, bf16[256,768]{1,0:T(8,128)(2,1)S(1)}, u32[]{:S(2)}, u32[]{:S(2)}) %collective-permute-start.3) | collective-permute-done | bytes 393248 | tf_op jit(solution)/shard_map/ppermute | solution.py:62
  24.2 23.4 %collective-permute-done.5.refs_3_ = bf16[128,768]{1,0:T(8,128)(2,1)S(1)} collective-permute-done((bf16[128,768]{1,0:T(8,128)(2,1)S(1)}, bf16[128,768]{1,0:T(8,128)(2,1)S(1)}, u32[]{:S(2)}, u32[]{:S(2)}) %collective-permute-start.5) | collective-permute-done | bytes 196640 | tf_op jit(solution)/shard_map/ppermute | solution.py:62
  64.2 4.0 norm_rows.1
  68.3 5.9 qkv.1
  77.5 5.3 collective-permute-done.10.refs_1_
  97.0 2.9 join.11.kv_ref.refs_1_
  99.9 7.1 %collective-permute-done.15.refs_3_ = bf16[128,2048]{1,0:T(8,128)(2,1)S(1)} collective-permute-done((bf16[128,2048]{1,0:T(8,128)(2,1)S(1)}, bf16[128,2048]{1,0:T(8,128)(2,1)S(1)}, u32[]{:S(2)}, u32[]{:S(2)}) %collective-permute-start.15) | collective-permute-done | bytes 524320 | tf_op jit(solution)/shard_map/ppermute | solution.py:62
  111.5 4.2 join.12.refs_0_.refs_2_
  115.8 18.9 %attention_forward.1 = (bf16[512,512]{1,0:T(8,128)(2,1)}, f32[512,512]{1,0:T(8,128)}, f32[8,512]{1,0:T(8,128)}) custom-call(s32[8]{0:T(128)} %slots.3, s32[2]{0:T(128)} %pad_add_fusion.place, bf16[512,512]{1,0:T(8,128)(2,1)} %get-tuple-element.195.q_ref.refs_0_, bf16[4096,256]{1,0:T(8,128)(2,1)} %join.11.kv_ref.refs_1_), custom_call_target="tpu_custom_call" | custom-call | flops 20899999744 | bytes 1024 | tf_op jit(solution)/shard_map/attention_forward/pallas_call | solution.py:521
  136.7 12.6 %collective-permute-done.22.refs_3_ = bf16[128,2048]{1,0:T(8,128)(2,1)S(1)} collective-permute-done((bf16[128,2048]{1,0:T(8,128)(2,1)S(1)}, bf16[128,2048]{1,0:T(8,128)(2,1)S(1)}, u32[]{:S(2)}, u32[]{:S(2)}) %collective-permute-start.22) | collective-permute-done | bytes 524320 | tf_op jit(solution)/shard_map/ppermute | solution.py:62
  150.9 4.2 join.13.refs_2_.refs_4_
  161.9 3.3 slice.112
  165.2 18.6 %collective-permute-done.19.refs_1_ = bf16[4,256,512]{2,1,0:T(8,128)(2,1)S(1)} collective-permute-done((bf16[4,256,512]{2,1,0:T(8,128)(2,1)S(1)}, bf16[4,256,512]{2,1,0:T(8,128)(2,1)S(1)}, u32[]{:S(2)}, u32[]{:S(2)}) %collective-permute-start.19) | collective-permute-done | bytes 1048608 | tf_op jit(solution)/shard_map/ppermute | solution.py:62
  184.7 17.4 %all-gather.10.cloned.1.call-done = bf16[2048,512]{1,0:T(8,128)(2,1)} async-done(((bf16[512,512]{1,0:T(8,128)(2,1)}), bf16[2048,512]{1,0:T(8,128)(2,1)}) %all-gather.10.cloned.1.call-update) | async-done | bytes 2097168 | tf_op jit(solution)/shard_map/all_gather | solution.py:1130
  208.7 9.4 %collective-permute-done.25.refs_3_ = bf16[4,128,512]{2,1,0:T(8,128)(2,1)S(1)} collective-permute-done((bf16[4,128,512]{2,1,0:T(8,128)(2,1)S(1)}, bf16[4,128,512]{2,1,0:T(8,128)(2,1)S(1)}, u32[]{:S(2)}, u32[]{:S(2)}) %collective-permute-start.25) | collective-permute-done | bytes 524320 | tf_op jit(solution)/shard_map/ppermute | solution.py:62
  221.5 4.2 join.14.part_ref.refs_0_
  231.3 4.2 join.15.refs_4_.refs_1_
  235.6 6.6 %project_part.1.refs_0_ = f32[512,1024]{1,0:T(8,128)} custom-call(bf16[4,512,512]{2,1,0:T(8,128)(2,1)} %bitcast.46, bf16[4,1024,512]{2,1,0:T(8,128)(2,1)} %join.14.part_ref.refs_0_), custom_call_target="tpu_custom_call" | custom-call | flops 110000000 | bytes 1024 | tf_op jit(solution)/shard_map/project_part/pallas_call | solution.py:729
  242.2 9.8 %project_residual.1 = (bf16[512,2048]{1,0:T(8,128)(2,1)}, f32[128,2048]{1,0:T(8,128)}) custom-call(s32[2]{0:T(128)} %pad_add_fusion.place, bf16[4,512,512]{2,1,0:T(8,128)(2,1)} %bitcast.47, bf16[512,2048]{1,0:T(8,128)(2,1)} %get-tuple-element.212.x_ref, f32[1,2048]{1,0:T(1,128)} %get-tuple-element.379.gain_ref, ...), custom_call_target="tpu_custom_call" | custom-call | flops 110000000 | bytes 1024 | tf_op jit(solution)/shard_map/project_residual/pallas_call | solution.py:796
  254.0 20.4 %mlp_inner.1 = (bf16[512,2048]{1,0:T(8,128)(2,1)}, bf16[512,2048]{1,0:T(8,128)(2,1)}, bf16[512,2048]{1,0:T(8,128)(2,1)}) custom-call(bf16[512,2048]{1,0:T(8,128)(2,1)} %get-tuple-element.216.x_ref.left_ref, bf16[512,2048]{1,0:T(8,128)(2,1)} %bitcast.43, bf16[1024,2048]{1,0:T(8,128)(2,1)} %join.12.refs_0_.refs_2_, ...), custom_call_target="tpu_custom_call" | custom-call | flops 110000000 | bytes 1024 | tf_op jit(solution)/shard_map/mlp_inner/pallas_call | solution.py:706
  274.3 15.8 %to_features.3 = bf16[512,2048]{1,0:T(8,128)(2,1)} custom-call(bf16[512,2048]{1,0:T(8,128)(2,1)} %get-tuple-element.249.refs_0_.right_ref, bf16[512,2048]{1,0:T(8,128)(2,1)} %get-tuple-element.238.refs_1_.right_ref, bf16[1024,2048]{1,0:T(8,128)(2,1)} %join.12.refs_0_.refs_2_, bf16[1024,2048]{1,0:T(8,128)(2,1)} %collective-permute-done.21.refs_1_.refs_3_, ...), custom_call_target="tpu_custom_call" | custom-call | flops 110000000 | bytes 1024 | tf_op jit(solution)/shard_map/to_features/pallas_call | solution.py:844
  290.4 5.4 gradient_part.12
  296.3 5.5 gradient_part.10
  302.8 5.4 gradient_part.8
  314.3 6.7 %gradient_part.11 = (bf16[256,2048]{1,0:T(8,128)(2,1)}, bf16[256,2048]{1,0:T(8,128)(2,1)}, bf16[256,2048]{1,0:T(8,128)(2,1)}, bf16[128,2048]{1,0:T(8,128)(2,1)}, bf16[128,2048]{1,0:T(8,128)(2,1)}) custom-call(bf16[512,2048]{1,0:T(8,128)(2,1)} %get-tuple-element.216.x_ref.left_ref, bf16[512,2048]{1,0:T(8,128)(2,1)} %get-tuple-element.238.refs_1_.right_ref, ...), custom_call_target="tpu_custom_call" | custom-call | flops 110000000 | bytes 1024 | tf_op jit(solution)/shard_map/gradient_part/pallas_call | solution.py:1006
  322.7 6.7 %gradient_part.9 = (bf16[256,2048]{1,0:T(8,128)(2,1)}, bf16[256,2048]{1,0:T(8,128)(2,1)}, bf16[256,2048]{1,0:T(8,128)(2,1)}, bf16[128,2048]{1,0:T(8,128)(2,1)}, bf16[128,2048]{1,0:T(8,128)(2,1)}) custom-call(bf16[512,2048]{1,0:T(8,128)(2,1)} %bitcast.45, bf16[512,2048]{1,0:T(8,128)(2,1)} %get-tuple-element.227.refs_0_.right_ref, ...), custom_call_target="tpu_custom_call" | custom-call | flops 110000000 | bytes 1024 | tf_op jit(solution)/shard_map/gradient_part/pallas_call | solution.py:1006
  332.9 10.9 %to_features.4 = bf16[512,2048]{1,0:T(8,128)(2,1)} custom-call(bf16[512,2048]{1,0:T(8,128)(2,1)} %get-tuple-element.227.refs_0_.right_ref, bf16[1024,2048]{1,0:T(8,128)(2,1)} %join.15.refs_4_.refs_1_, bf16[1024,2048]{1,0:T(8,128)(2,1)} %copy-done.2), custom_call_target="tpu_custom_call" | custom-call | flops 110000000 | bytes 1024 | tf_op jit(solution)/shard_map/to_features/pallas_call | solution.py:844
  344.0 6.8 %gradient_part.13 = (bf16[256,2048]{1,0:T(8,128)(2,1)}, bf16[256,2048]{1,0:T(8,128)(2,1)}, bf16[256,2048]{1,0:T(8,128)(2,1)}, bf16[128,2048]{1,0:T(8,128)(2,1)}, bf16[128,2048]{1,0:T(8,128)(2,1)}) custom-call(bf16[512,2048]{1,0:T(8,128)(2,1)} %get-tuple-element.216.x_ref.left_ref, bf16[512,2048]{1,0:T(8,128)(2,1)} %get-tuple-element.249.refs_0_.right_ref, ...), custom_call_target="tpu_custom_call" | custom-call | flops 110000000 | bytes 1024 | tf_op jit(solution)/shard_map/gradient_part/pallas_call | solution.py:1006
  351.8 3.3 scatter_two.7
  355.1 3.4 scatter_two.6
  363.7 6.3 %to_groups.1 = bf16[4,128,512]{2,1,0:T(8,128)(2,1)} custom-call(s32[2]{0:T(128)} %pad_add_fusion.place, bf16[128,2048]{1,0:T(8,128)(2,1)} %fusion.19.x_ref.in_ref, bf16[4,1024,512]{2,1,0:T(8,128)(2,1)} %join.14.part_ref.refs_0_, bf16[4,1024,512]{2,1,0:T(8,128)(2,1)} %collective-permute-done.27.part_ref.refs_1_), custom_call_target="tpu_custom_call" | custom-call | flops 110000000 | bytes 1024 | tf_op jit(solution)/shard_map/to_groups/pallas_call | solution.py:876
  379.5 3.2 collective-permute-done.50
  393.4 30.1 %attention_backward.1 = (bf16[512,512]{1,0:T(8,128)(2,1)}, bf16[2048,256]{1,0:T(8,128)(2,1)}, bf16[2048,256]{1,0:T(8,128)(2,1)}) custom-call(s32[8]{0:T(128)} %slots.3, s32[2]{0:T(128)} %pad_add_fusion.place, bf16[512,512]{1,0:T(8,128)(2,1)} %get-tuple-element.195.q_ref.refs_0_, bf16[4096,256]{1,0:T(8,128)(2,1)} %join.11.kv_ref.refs_1_, ...), custom_call_target="tpu_custom_call" | custom-call | flops 32999999488 | bytes 1024 | tf_op jit(solution)/shard_map/attention_backward/pallas_call | solution.py:629
  432.1 8.7 %collective-permute-done.60.lower_ref = bf16[256,256]{1,0:T(8,128)(2,1)S(1)} collective-permute-done((bf16[256,256]{1,0:T(8,128)(2,1)}, bf16[256,256]{1,0:T(8,128)(2,1)S(1)}, u32[]{:S(2)}, u32[]{:S(2)}) %collective-permute-start.60) | collective-permute-done | bytes 131104 | tf_op jit(solution)/shard_map/ppermute | solution.py:62
  446.2 8.8 %gradient_out.1 = (bf16[1024,512]{1,0:T(8,128)(2,1)}, bf16[1024,512]{1,0:T(8,128)(2,1)}) custom-call(s32[2]{0:T(128)} %pad_add_fusion.place, bf16[2,128,256]{2,1,0:T(8,128)(2,1)} %get-tuple-element.293.refs_0_, bf16[2,128,256]{2,1,0:T(8,128)(2,1)} %copy-done.55, bf16[2,128,256]{2,1,0:T(8,128)(2,1)} %copy-done.56, bf16[2,128,256]{2,1,0:T(8,128)(2,1)} %copy-done.57, ...), custom_call_target="tpu_custom_call" | custom-call | flops 110000000 | bytes 1024 | tf_op jit(solution)/shard_map/gradient_out/pallas_call | solution.py:953
  458.4 7.9 %to_features.5 = bf16[512,2048]{1,0:T(8,128)(2,1)} custom-call(bf16[512,768]{1,0:T(8,128)(2,1)} %grad_qkv.1.refs_0_.right_ref, bf16[1024,768]{1,0:T(8,128)(2,1)} %join.9.refs_0_.refs_1_, bf16[1024,768]{1,0:T(8,128)(2,1)} %copy-done.5), custom_call_target="tpu_custom_call" | custom-call | flops 110000000 | bytes 1024 | tf_op jit(solution)/shard_map/to_features/pallas_call | solution.py:844
  469.5 3.3 scatter_two.10
  475.8 3.6 gradient_part.14
  484.2 17.3 %collective-permute-done.72.lower_ref = bf16[128,512]{1,0:T(8,128)(2,1)S(1)} collective-permute-done((bf16[128,512]{1,0:T(8,128)(2,1)}, bf16[128,512]{1,0:T(8,128)(2,1)S(1)}, u32[]{:S(2)}, u32[]{:S(2)}) %collective-permute-start.72) | collective-permute-done | bytes 131104 | tf_op jit(solution)/shard_map/ppermute | solution.py:62
  505.7 3.9 gradient_part.15
  514.9 5.4 collective-permute-done.76
  520.2 3.4 collective-permute-done.77.lower_ref
  529.1 3.5 finish_sum.9
  532.6 3.5 finish_sum.8
  536.1 3.5 finish_sum.7
  553.7 2.9 collective-permute-start.87
  557.3 16.6 %collective-permute-done.87 = bf16[256,512]{1,0:T(8,128)(2,1)S(1)} collective-permute-done((bf16[256,512]{1,0:T(8,128)(2,1)S(1)}, bf16[256,512]{1,0:T(8,128)(2,1)S(1)}, u32[]{:S(2)}, u32[]{:S(2)}) %collective-permute-start.87) | collective-permute-done | bytes 262176 | tf_op jit(solution)/shard_map/ppermute | solution.py:978
  576.1 3.2 fusion.10
  (405 shorter events, 181.1 us)
Async XLA Ops:
  7.2 54.3 %all-gather.6.cloned.1.call-start = ((), (), s32[]{:S(2)}) async-start(), calls=%async_computation.3 | async-start | bytes 2621440 | tf_op jit(solution)/shard_map/all_gather | solution.py:1099
  7.9 126.8 %all-gather.8.cloned.1.call-start = ((), (), s32[]{:S(2)}) async-start(), calls=%async_computation.7 | async-start | bytes 3932160 | tf_op jit(solution)/shard_map/all_gather | solution.py:1118
  11.8 49.6 %collective-permute-start.8 = (bf16[256,2048]{1,0:T(8,128)(2,1)}, bf16[256,2048]{1,0:T(8,128)(2,1)S(1)}, u32[]{:S(2)}, u32[]{:S(2)}) collective-permute-start(bf16[256,2048]{1,0:T(8,128)(2,1)} %refs_0_.3), channel_id=1, source_target_pairs={{0,8},{4,12},{8,0},{12,4},{16,24},{20,28},{24,16},{28,20},{1,9},{5... | collective-permute-start | bytes 3145736 | tf_op jit(solution)/shard_map/ppermute | solution.py:62
  13.3 48.1 %collective-permute-start.9 = (bf16[256,2048]{1,0:T(8,128)(2,1)}, bf16[256,2048]{1,0:T(8,128)(2,1)}, u32[]{:S(2)}, u32[]{:S(2)}) collective-permute-start(bf16[256,2048]{1,0:T(8,128)(2,1)} %refs_0_.3), channel_id=1, source_target_pairs={{0,16},{4,20},{8,24},{12,28},{16,0},{20,4},{24,8},{28,12},{1,17},{... | collective-permute-start | bytes 3145736 | tf_op jit(solution)/shard_map/ppermute | solution.py:62
  15.2 41.4 %collective-permute-start = (bf16[1,2,256]{2,1,0:T(2,128)(2,1)S(1)}, bf16[1,2,256]{2,1,0:T(2,128)(2,1)S(1)}, u32[]{:S(2)}, u32[]{:S(2)}) collective-permute-start(bf16[1,2,256]{2,1,0:T(2,128)(2,1)S(1)} %maximum_bitcast_fusion.1), channel_id=1, source_target_pairs={{0,8},{4,12},{8,0},{12,4},{16,24},{20,28},{24,16},{28,20},{1,9},{5... | collective-permute-start | bytes 3080 | tf_op jit(solution)/shard_map/ppermute | solution.py:62
  22.0 25.6 %collective-permute-start.5 = (bf16[128,768]{1,0:T(8,128)(2,1)S(1)}, bf16[128,768]{1,0:T(8,128)(2,1)S(1)}, u32[]{:S(2)}, u32[]{:S(2)}) collective-permute-start(bf16[128,768]{1,0:T(8,128)(2,1)S(1)} %slice.140), channel_id=1, source_target_pairs={{0,16},{4,20},{8,24},{12,28},{16,0},{20,4},{24,8},{28,12},{1,17},{... | collective-permute-start | bytes 589832 | tf_op jit(solution)/shard_map/ppermute | solution.py:62
  23.6 24.0 %collective-permute-start.6 = (bf16[128,768]{1,0:T(8,128)(2,1)S(1)}, bf16[128,768]{1,0:T(8,128)(2,1)S(1)}, u32[]{:S(2)}, u32[]{:S(2)}) collective-permute-start(bf16[128,768]{1,0:T(8,128)(2,1)S(1)} %slice.141), channel_id=1, source_target_pairs={{0,8},{4,12},{8,0},{12,4},{16,24},{20,28},{24,16},{28,20},{1,9},{5... | collective-permute-start | bytes 589832 | tf_op jit(solution)/shard_map/ppermute | solution.py:62
  61.6 140.6 %all-gather.10.cloned.1.call-start = ((), (), s32[]{:S(2)}) async-start(), calls=%async_computation.8 | async-start | bytes 2621440 | tf_op jit(solution)/shard_map/all_gather | solution.py:1130
  109.1 25.6 %collective-permute-start.17 = (bf16[256,2048]{1,0:T(8,128)(2,1)S(1)}, bf16[256,2048]{1,0:T(8,128)(2,1)S(1)}, u32[]{:S(2)}, u32[]{:S(2)}) collective-permute-start(bf16[256,2048]{1,0:T(8,128)(2,1)S(1)} %copy-done.16), channel_id=1, source_target_pairs={{0,8},{4,12},{8,0},{12,4},{16,24},{20,28},{24,16},{28,20},{1,9},{5... | collective-permute-start | bytes 3145736 | tf_op jit(solution)/shard_map/ppermute | solution.py:62
  110.0 24.6 %collective-permute-start.18 = (bf16[256,2048]{1,0:T(8,128)(2,1)S(1)}, bf16[256,2048]{1,0:T(8,128)(2,1)S(1)}, u32[]{:S(2)}, u32[]{:S(2)}) collective-permute-start(bf16[256,2048]{1,0:T(8,128)(2,1)S(1)} %copy-done.16), channel_id=1, source_target_pairs={{0,16},{4,20},{8,24},{12,28},{16,0},{20,4},{24,8},{28,12},{1,17},{... | collective-permute-start | bytes 3145736 | tf_op jit(solution)/shard_map/ppermute | solution.py:62
  115.7 45.1 %collective-permute-start.21 = (bf16[1024,2048]{1,0:T(8,128)(2,1)}, bf16[1024,2048]{1,0:T(8,128)(2,1)}, u32[]{:S(2)}, u32[]{:S(2)}) collective-permute-start(bf16[1024,2048]{1,0:T(8,128)(2,1)} %join.12.refs_0_.refs_2_), channel_id=1, source_target_pairs={{0,4},{4,0},{8,12},{12,8},{16,20},{20,16},{24,28},{28,24},{1,5},{5... | collective-permute-start | bytes 12582920 | tf_op jit(solution)/shard_map/ppermute | solution.py:62
  155.1 47.0 %collective-permute-start.24 = (bf16[1024,2048]{1,0:T(8,128)(2,1)}, bf16[1024,2048]{1,0:T(8,128)(2,1)}, u32[]{:S(2)}, u32[]{:S(2)}) collective-permute-start(bf16[1024,2048]{1,0:T(8,128)(2,1)} %join.13.refs_2_.refs_4_), channel_id=1, source_target_pairs={{0,4},{4,0},{8,12},{12,8},{16,20},{20,16},{24,28},{28,24},{1,5},{5... | collective-permute-start | bytes 12582920 | tf_op jit(solution)/shard_map/ppermute | solution.py:62
  155.2 203.3 %reduce-scatter.4.cloned.1.call-start = ((), (), s32[]{:S(2)}) async-start(), calls=%async_computation.4 | async-start | bytes 2621440 | tf_op jit(solution)/shard_map/reduce_scatter | solution.py:1153
  157.8 26.0 %collective-permute-start.19 = (bf16[4,256,512]{2,1,0:T(8,128)(2,1)S(1)}, bf16[4,256,512]{2,1,0:T(8,128)(2,1)S(1)}, u32[]{:S(2)}, u32[]{:S(2)}) collective-permute-start(bf16[4,256,512]{2,1,0:T(8,128)(2,1)S(1)} %reshape.185.refs_0_), channel_id=1, source_target_pairs={{0,8},{4,12},{8,0},{12,4},{16,24},{20,28},{24,16},{28,20},{1,9},{5... | collective-permute-start | bytes 3145736 | tf_op jit(solution)/shard_map/ppermute | solution.py:62
  158.5 26.3 %collective-permute-start.20 = (bf16[4,256,512]{2,1,0:T(8,128)(2,1)S(1)}, bf16[4,256,512]{2,1,0:T(8,128)(2,1)}, u32[]{:S(2)}, u32[]{:S(2)}) collective-permute-start(bf16[4,256,512]{2,1,0:T(8,128)(2,1)S(1)} %reshape.185.refs_0_), channel_id=1, source_target_pairs={{0,16},{4,20},{8,24},{12,28},{16,0},{20,4},{24,8},{28,12},{1,17},{... | collective-permute-start | bytes 3145736 | tf_op jit(solution)/shard_map/ppermute | solution.py:62
  159.5 47.0 %collective-permute-start.28 = (bf16[256,2048]{1,0:T(8,128)(2,1)}, bf16[256,2048]{1,0:T(8,128)(2,1)S(1)}, u32[]{:S(2)}, u32[]{:S(2)}) collective-permute-start(bf16[256,2048]{1,0:T(8,128)(2,1)} %refs_0_.5), channel_id=1, source_target_pairs={{0,8},{4,12},{8,0},{12,4},{16,24},{20,28},{24,16},{28,20},{1,9},{5... | collective-permute-start | bytes 3145736 | tf_op jit(solution)/shard_map/ppermute | solution.py:62
  160.9 46.3 %collective-permute-start.29 = (bf16[256,2048]{1,0:T(8,128)(2,1)}, bf16[256,2048]{1,0:T(8,128)(2,1)S(1)}, u32[]{:S(2)}, u32[]{:S(2)}) collective-permute-start(bf16[256,2048]{1,0:T(8,128)(2,1)} %refs_0_.5), channel_id=1, source_target_pairs={{0,16},{4,20},{8,24},{12,28},{16,0},{20,4},{24,8},{28,12},{1,17},{... | collective-permute-start | bytes 3145736 | tf_op jit(solution)/shard_map/ppermute | solution.py:62
  206.5 22.2 %collective-permute-start.30 = (bf16[128,2048]{1,0:T(8,128)(2,1)S(1)}, bf16[128,2048]{1,0:T(8,128)(2,1)S(1)}, u32[]{:S(2)}, u32[]{:S(2)}) collective-permute-start(bf16[128,2048]{1,0:T(8,128)(2,1)S(1)} %slice.144), channel_id=1, source_target_pairs={{0,16},{4,20},{8,24},{12,28},{16,0},{20,4},{24,8},{28,12},{1,17},{... | collective-permute-start | bytes 1572872 | tf_op jit(solution)/shard_map/ppermute | solution.py:62
  207.2 23.3 %collective-permute-start.31 = (bf16[128,2048]{1,0:T(8,128)(2,1)S(1)}, bf16[128,2048]{1,0:T(8,128)(2,1)S(1)}, u32[]{:S(2)}, u32[]{:S(2)}) collective-permute-start(bf16[128,2048]{1,0:T(8,128)(2,1)S(1)} %slice.145), channel_id=1, source_target_pairs={{0,8},{4,12},{8,0},{12,4},{16,24},{20,28},{24,16},{28,20},{1,9},{5... | collective-permute-start | bytes 1572872 | tf_op jit(solution)/shard_map/ppermute | solution.py:62
  225.8 16.4 %collective-permute-start.27 = (bf16[4,1024,512]{2,1,0:T(8,128)(2,1)}, bf16[4,1024,512]{2,1,0:T(8,128)(2,1)}, u32[]{:S(2)}, u32[]{:S(2)}) collective-permute-start(bf16[4,1024,512]{2,1,0:T(8,128)(2,1)} %join.14.part_ref.refs_0_), channel_id=1, source_target_pairs={{0,4},{4,0},{8,12},{12,8},{16,20},{20,16},{24,28},{28,24},{1,5},{5... | collective-permute-start | bytes 12582920 | tf_op jit(solution)/shard_map/ppermute | solution.py:62
  235.6 16.4 %collective-permute-start.32 = (bf16[1024,2048]{1,0:T(8,128)(2,1)}, bf16[1024,2048]{1,0:T(8,128)(2,1)S(1)}, u32[]{:S(2)}, u32[]{:S(2)}) collective-permute-start(bf16[1024,2048]{1,0:T(8,128)(2,1)} %join.15.refs_4_.refs_1_), channel_id=1, source_target_pairs={{0,4},{4,0},{8,12},{12,8},{16,20},{20,16},{24,28},{28,24},{1,5},{5... | collective-permute-start | bytes 12582920 | tf_op jit(solution)/shard_map/ppermute | solution.py:62
  290.1 164.9 %reduce-scatter.6.cloned.1.call-start = ((), (), s32[]{:S(2)}) async-start(), calls=%async_computation.5 | async-start | bytes 2621440 | tf_op jit(solution)/shard_map/reduce_scatter | solution.py:1185
  309.3 20.1 %collective-permute-start.46 = (bf16[256,2048]{1,0:T(8,128)(2,1)}, bf16[256,2048]{1,0:T(8,128)(2,1)S(1)}, u32[]{:S(2)}, u32[]{:S(2)}) collective-permute-start(bf16[256,2048]{1,0:T(8,128)(2,1)} %get-tuple-element.251), channel_id=1, source_target_pairs={{0,4},{4,0},{8,12},{12,8},{16,20},{20,16},{24,28},{28,24},{1,5},{5... | collective-permute-start | bytes 3145736 | tf_op jit(solution)/shard_map/ppermute | solution.py:62
  311.6 18.8 %collective-permute-start.47 = (bf16[256,2048]{1,0:T(8,128)(2,1)}, bf16[256,2048]{1,0:T(8,128)(2,1)S(1)}, u32[]{:S(2)}, u32[]{:S(2)}) collective-permute-start(bf16[256,2048]{1,0:T(8,128)(2,1)} %get-tuple-element.252), channel_id=1, source_target_pairs={{0,4},{4,0},{8,12},{12,8},{16,20},{20,16},{24,28},{28,24},{1,5},{5... | collective-permute-start | bytes 3145736 | tf_op jit(solution)/shard_map/ppermute | solution.py:62
  313.9 30.1 %collective-permute-start.48 = (bf16[256,2048]{1,0:T(8,128)(2,1)}, bf16[256,2048]{1,0:T(8,128)(2,1)}, u32[]{:S(2)}, u32[]{:S(2)}) collective-permute-start(bf16[256,2048]{1,0:T(8,128)(2,1)} %get-tuple-element.253), channel_id=1, source_target_pairs={{0,4},{4,0},{8,12},{12,8},{16,20},{20,16},{24,28},{28,24},{1,5},{5... | collective-permute-start | bytes 3145736 | tf_op jit(solution)/shard_map/ppermute | solution.py:62
  321.0 29.8 %collective-permute-start.43 = (bf16[128,2048]{1,0:T(8,128)(2,1)}, bf16[128,2048]{1,0:T(8,128)(2,1)S(1)}, u32[]{:S(2)}, u32[]{:S(2)}) collective-permute-start(bf16[128,2048]{1,0:T(8,128)(2,1)} %get-tuple-element.245), channel_id=1, source_target_pairs={{0,16},{4,20},{8,24},{12,28},{16,0},{20,4},{24,8},{28,12},{1,17},{... | collective-permute-start | bytes 1572872 | tf_op jit(solution)/shard_map/ppermute | solution.py:62
  321.9 28.8 %collective-permute-start.44 = (bf16[128,2048]{1,0:T(8,128)(2,1)}, bf16[128,2048]{1,0:T(8,128)(2,1)S(1)}, u32[]{:S(2)}, u32[]{:S(2)}) collective-permute-start(bf16[128,2048]{1,0:T(8,128)(2,1)} %get-tuple-element.246), channel_id=1, source_target_pairs={{0,8},{4,12},{8,0},{12,4},{16,24},{20,28},{24,16},{28,20},{1,9},{5... | collective-permute-start | bytes 1572872 | tf_op jit(solution)/shard_map/ppermute | solution.py:62
  329.4 25.7 %collective-permute-start.37 = (bf16[128,2048]{1,0:T(8,128)(2,1)}, bf16[128,2048]{1,0:T(8,128)(2,1)}, u32[]{:S(2)}, u32[]{:S(2)}) collective-permute-start(bf16[128,2048]{1,0:T(8,128)(2,1)} %get-tuple-element.234), channel_id=1, source_target_pairs={{0,16},{4,20},{8,24},{12,28},{16,0},{20,4},{24,8},{28,12},{1,17},{... | collective-permute-start | bytes 1572872 | tf_op jit(solution)/shard_map/ppermute | solution.py:62
  331.4 23.7 %collective-permute-start.38 = (bf16[128,2048]{1,0:T(8,128)(2,1)}, bf16[128,2048]{1,0:T(8,128)(2,1)}, u32[]{:S(2)}, u32[]{:S(2)}) collective-permute-start(bf16[128,2048]{1,0:T(8,128)(2,1)} %get-tuple-element.235), channel_id=1, source_target_pairs={{0,8},{4,12},{8,0},{12,4},{16,24},{20,28},{24,16},{28,20},{1,9},{5... | collective-permute-start | bytes 1572872 | tf_op jit(solution)/shard_map/ppermute | solution.py:62
  358.5 25.1 %collective-permute-start.52 = (bf16[256,2048]{1,0:T(8,128)(2,1)}, bf16[256,2048]{1,0:T(8,128)(2,1)S(1)}, u32[]{:S(2)}, u32[]{:S(2)}) collective-permute-start(bf16[256,2048]{1,0:T(8,128)(2,1)} %get-tuple-element.261), channel_id=1, source_target_pairs={{0,8},{4,12},{8,0},{12,4},{16,24},{20,28},{24,16},{28,20},{1,9},{5... | collective-permute-start | bytes 3145736 | tf_op jit(solution)/shard_map/ppermute | solution.py:62
  359.0 24.6 %collective-permute-start.53 = (bf16[256,2048]{1,0:T(8,128)(2,1)}, bf16[256,2048]{1,0:T(8,128)(2,1)}, u32[]{:S(2)}, u32[]{:S(2)}) collective-permute-start(bf16[256,2048]{1,0:T(8,128)(2,1)} %get-tuple-element.262), channel_id=1, source_target_pairs={{0,16},{4,20},{8,24},{12,28},{16,0},{20,4},{24,8},{28,12},{1,17},{... | collective-permute-start | bytes 3145736 | tf_op jit(solution)/shard_map/ppermute | solution.py:62
  383.6 40.0 %collective-permute-start.57 = (bf16[256,2048]{1,0:T(8,128)(2,1)}, bf16[256,2048]{1,0:T(8,128)(2,1)}, u32[]{:S(2)}, u32[]{:S(2)}) collective-permute-start(bf16[256,2048]{1,0:T(8,128)(2,1)} %get-tuple-element.277), channel_id=1, source_target_pairs={{0,8},{4,12},{8,0},{12,4},{16,24},{20,28},{24,16},{28,20},{1,9},{5... | collective-permute-start | bytes 3145736 | tf_op jit(solution)/shard_map/ppermute | solution.py:62
  384.9 38.7 %collective-permute-start.58 = (bf16[256,2048]{1,0:T(8,128)(2,1)}, bf16[256,2048]{1,0:T(8,128)(2,1)}, u32[]{:S(2)}, u32[]{:S(2)}) collective-permute-start(bf16[256,2048]{1,0:T(8,128)(2,1)} %get-tuple-element.278), channel_id=1, source_target_pairs={{0,16},{4,20},{8,24},{12,28},{16,0},{20,4},{24,8},{28,12},{1,17},{... | collective-permute-start | bytes 3145736 | tf_op jit(solution)/shard_map/ppermute | solution.py:62
  387.9 35.6 %collective-permute-start.54 = (bf16[2,128,256]{2,1,0:T(8,128)(2,1)S(1)}, bf16[2,128,256]{2,1,0:T(8,128)(2,1)S(1)}, u32[]{:S(2)}, u32[]{:S(2)}) collective-permute-start(bf16[2,128,256]{2,1,0:T(8,128)(2,1)S(1)} %get-tuple-element.373), channel_id=1, source_target_pairs={{0,1},{1,2},{2,3},{3,0},{4,5},{5,6},{6,7},{7,4},{8,9},{9,10},{10,1... | collective-permute-start | bytes 393224 | tf_op jit(solution)/shard_map/ppermute | solution.py:211
  390.7 32.8 %collective-permute-start.55 = (bf16[2,128,256]{2,1,0:T(8,128)(2,1)S(1)}, bf16[2,128,256]{2,1,0:T(8,128)(2,1)S(1)}, u32[]{:S(2)}, u32[]{:S(2)}) collective-permute-start(bf16[2,128,256]{2,1,0:T(8,128)(2,1)S(1)} %get-tuple-element.372), channel_id=1, source_target_pairs={{0,2},{1,3},{2,0},{3,1},{4,6},{5,7},{6,4},{7,5},{8,10},{9,11},{10,... | collective-permute-start | bytes 393224 | tf_op jit(solution)/shard_map/ppermute | solution.py:211
  392.4 31.2 %collective-permute-start.56 = (bf16[2,128,256]{2,1,0:T(8,128)(2,1)S(1)}, bf16[2,128,256]{2,1,0:T(8,128)(2,1)S(1)}, u32[]{:S(2)}, u32[]{:S(2)}) collective-permute-start(bf16[2,128,256]{2,1,0:T(8,128)(2,1)S(1)} %get-tuple-element.371), channel_id=1, source_target_pairs={{0,3},{1,0},{2,1},{3,2},{4,7},{5,4},{6,5},{7,6},{8,11},{9,8},{10,9... | collective-permute-start | bytes 393224 | tf_op jit(solution)/shard_map/ppermute | solution.py:211
  393.1 181.7 %reduce-scatter.8.cloned.1.call-start = ((), (), s32[]{:S(2)}) async-start(), calls=%async_computation.6 | async-start | bytes 2621440 | tf_op jit(solution)/shard_map/reduce_scatter | solution.py:1204
  423.7 31.3 %collective-permute-start.64 = (bf16[128,2048]{1,0:T(8,128)(2,1)S(1)}, bf16[128,2048]{1,0:T(8,128)(2,1)}, u32[]{:S(2)}, u32[]{:S(2)}) collective-permute-start(bf16[128,2048]{1,0:T(8,128)(2,1)S(1)} %copy-done.71), channel_id=1, source_target_pairs={{0,16},{4,20},{8,24},{12,28},{16,0},{20,4},{24,8},{28,12},{1,17},{... | collective-permute-start | bytes 1572872 | tf_op jit(solution)/shard_map/ppermute | solution.py:62
  424.6 30.4 %collective-permute-start.65 = (bf16[128,2048]{1,0:T(8,128)(2,1)S(1)}, bf16[128,2048]{1,0:T(8,128)(2,1)}, u32[]{:S(2)}, u32[]{:S(2)}) collective-permute-start(bf16[128,2048]{1,0:T(8,128)(2,1)S(1)} %copy-done.70), channel_id=1, source_target_pairs={{0,8},{4,12},{8,0},{12,4},{16,24},{20,28},{24,16},{28,20},{1,9},{5... | collective-permute-start | bytes 1572872 | tf_op jit(solution)/shard_map/ppermute | solution.py:62
  472.9 36.8 %collective-permute-start.74 = (bf16[256,2048]{1,0:T(8,128)(2,1)}, bf16[256,2048]{1,0:T(8,128)(2,1)}, u32[]{:S(2)}, u32[]{:S(2)}) collective-permute-start(bf16[256,2048]{1,0:T(8,128)(2,1)} %get-tuple-element.334), channel_id=1, source_target_pairs={{0,8},{4,12},{8,0},{12,4},{16,24},{20,28},{24,16},{28,20},{1,9},{5... | collective-permute-start | bytes 3145736 | tf_op jit(solution)/shard_map/ppermute | solution.py:62
  473.9 35.8 %collective-permute-start.75 = (bf16[256,2048]{1,0:T(8,128)(2,1)}, bf16[256,2048]{1,0:T(8,128)(2,1)}, u32[]{:S(2)}, u32[]{:S(2)}) collective-permute-start(bf16[256,2048]{1,0:T(8,128)(2,1)} %get-tuple-element.335), channel_id=1, source_target_pairs={{0,16},{4,20},{8,24},{12,28},{16,0},{20,4},{24,8},{28,12},{1,17},{... | collective-permute-start | bytes 3145736 | tf_op jit(solution)/shard_map/ppermute | solution.py:62
  479.4 22.6 %collective-permute-start.68 = (bf16[256,768]{1,0:T(8,128)(2,1)}, bf16[256,768]{1,0:T(8,128)(2,1)S(1)}, u32[]{:S(2)}, u32[]{:S(2)}) collective-permute-start(bf16[256,768]{1,0:T(8,128)(2,1)} %get-tuple-element.315), channel_id=1, source_target_pairs={{0,4},{4,0},{8,12},{12,8},{16,20},{20,16},{24,28},{28,24},{1,5},{5... | collective-permute-start | bytes 1179656 | tf_op jit(solution)/shard_map/ppermute | solution.py:62
  482.0 19.5 %collective-permute-start.72 = (bf16[128,512]{1,0:T(8,128)(2,1)}, bf16[128,512]{1,0:T(8,128)(2,1)S(1)}, u32[]{:S(2)}, u32[]{:S(2)}) collective-permute-start(bf16[128,512]{1,0:T(8,128)(2,1)} %get-tuple-element.326), channel_id=1, source_target_pairs={{0,16},{4,20},{8,24},{12,28},{16,0},{20,4},{24,8},{28,12},{1,17},{... | collective-permute-start | bytes 393224 | tf_op jit(solution)/shard_map/ppermute | solution.py:62
  483.2 18.3 %collective-permute-start.73 = (bf16[128,512]{1,0:T(8,128)(2,1)}, bf16[128,512]{1,0:T(8,128)(2,1)S(1)}, u32[]{:S(2)}, u32[]{:S(2)}) collective-permute-start(bf16[128,512]{1,0:T(8,128)(2,1)} %get-tuple-element.327), channel_id=1, source_target_pairs={{0,8},{4,12},{8,0},{12,4},{16,24},{20,28},{24,16},{28,20},{1,9},{5... | collective-permute-start | bytes 393224 | tf_op jit(solution)/shard_map/ppermute | solution.py:62
  509.7 17.5 %collective-permute-start.79 = (bf16[256,512]{1,0:T(8,128)(2,1)}, bf16[256,512]{1,0:T(8,128)(2,1)S(1)}, u32[]{:S(2)}, u32[]{:S(2)}) collective-permute-start(bf16[256,512]{1,0:T(8,128)(2,1)} %get-tuple-element.343), channel_id=1, source_target_pairs={{0,8},{4,12},{8,0},{12,4},{16,24},{20,28},{24,16},{28,20},{1,9},{5... | collective-permute-start | bytes 786440 | tf_op jit(solution)/shard_map/ppermute | solution.py:62
  510.8 16.4 %collective-permute-start.80 = (bf16[256,512]{1,0:T(8,128)(2,1)}, bf16[256,512]{1,0:T(8,128)(2,1)}, u32[]{:S(2)}, u32[]{:S(2)}) collective-permute-start(bf16[256,512]{1,0:T(8,128)(2,1)} %get-tuple-element.344), channel_id=1, source_target_pairs={{0,16},{4,20},{8,24},{12,28},{16,0},{20,4},{24,8},{28,12},{1,17},{... | collective-permute-start | bytes 786440 | tf_op jit(solution)/shard_map/ppermute | solution.py:62
  527.2 16.8 %collective-permute-start.82 = (bf16[256,768]{1,0:T(8,128)(2,1)}, bf16[256,768]{1,0:T(8,128)(2,1)S(1)}, u32[]{:S(2)}, u32[]{:S(2)}) collective-permute-start(bf16[256,768]{1,0:T(8,128)(2,1)} %get-tuple-element.349), channel_id=1, source_target_pairs={{0,8},{4,12},{8,0},{12,4},{16,24},{20,28},{24,16},{28,20},{1,9},{5... | collective-permute-start | bytes 1179656 | tf_op jit(solution)/shard_map/ppermute | solution.py:62
  553.7 20.2 %collective-permute-start.87 = (bf16[256,512]{1,0:T(8,128)(2,1)S(1)}, bf16[256,512]{1,0:T(8,128)(2,1)S(1)}, u32[]{:S(2)}, u32[]{:S(2)}) collective-permute-start(bf16[256,512]{1,0:T(8,128)(2,1)S(1)} %convert_element_type.55), channel_id=1, source_target_pairs={{0,0},{1,8},{2,16},{3,24},{4,4},{5,12},{6,20},{7,28},{8,1},{9,9},{... | collective-permute-start | bytes 786440 | tf_op jit(solution)/shard_map/ppermute | solution.py:978
  (118 other events, 1097.1 us)
Sparse Core Ops, SparseCore 0:
  9.6 47.2 all-gather.5
  61.7 64.9 all-gather.7
  155.4 46.7 all-gather.9
  290.3 43.6 reduce-scatter.3
  393.2 42.8 reduce-scatter.5
  469.2 43.0 reduce-scatter.7

commit v3 on v2

--- a/solution.py
+++ b/solution.py
@@ -130,13 +130,9 @@
     return stacked[:kept] + swap(stacked[kept:], bit, bits)
 
 
-def sum_small(array, axis):
+def sum_step(array, shift, axis):
     size = lax.axis_size(axis)
-    shift = 1
-    while shift < size:
-        array = array + lax.ppermute(array, axis, [(i, i ^ shift) for i in range(size)])
-        shift *= 2
-    return array
+    return array + lax.ppermute(array, axis, [(i, i ^ shift) for i in range(size)])
 
 
 def add_half(left, right):
@@ -174,27 +170,27 @@
     return swap(two[0], first, bits), swap(two[1], second, bits)
 
 
-def finish_sum(blocks, three):
+def finish_sum(blocks, three, widths=None):
     rows, width = blocks[0].shape
-
-    def kernel(own_ref, first_ref, second_ref, out_ref):
-        total = own_ref[...].astype(jnp.float32) + first_ref[...].astype(jnp.float32)
-        out_ref[...] = total + second_ref[...].astype(jnp.float32)
+    widths = widths or [width]
+
+    def kernel(own_ref, first_ref, second_ref, *out_refs):
+        start = 0
+        for out_ref in out_refs:
+            here = slice(start, start + out_ref.shape[1])
+            total = own_ref[:, here].astype(jnp.float32) + first_ref[:, here].astype(jnp.float32)
+            out_ref[...] = total + second_ref[:, here].astype(jnp.float32)
+            start += out_ref.shape[1]
 
     return pl.pallas_call(
         kernel,
-        out_shape=jax.ShapeDtypeStruct((rows, width), jnp.float32),
+        out_shape=[jax.ShapeDtypeStruct((rows, each), jnp.float32) for each in widths],
         in_specs=[in_vmem] * 3,
-        out_specs=in_vmem,
+        out_specs=[in_vmem] * len(widths),
         compiler_params=kernel_params(),
         cost_estimate=cost(0.1),
         name="finish_sum",
     )(blocks[0], *three)
-
-
-def scatter_step(stacked, bit, bits):
-    kept = stacked.shape[0] // 2
-    return stacked[:kept] + swap(stacked[kept:], bit, bits)
 
 
 def sum_small(array, axis):
@@ -819,7 +815,7 @@
     )(place, lefts, rows, gain, parts[-1], *sums)
 
 
-def to_features(lefts, weights):
+def to_features(lefts, weights, after=()):
     rows = lefts[0].shape[0]
     count = len(weights[0])
     features = weights[0][0].shape[0]
@@ -827,7 +823,7 @@
     tiles = features // tile
 
     def kernel(*refs):
-        left_refs, part_refs, out_ref = refs[: len(lefts)], refs[len(lefts) : -1], refs[-1]
+        left_refs, part_refs, out_ref = refs[: len(lefts)], refs[len(lefts) :], refs[-1]
         step = pl.program_id(0)
         for part in range(count):
 
@@ -850,12 +846,13 @@
             pl.BlockSpec((tile, parts[part].shape[1]), functools.partial(part_at, part * tiles))
             for parts in weights
             for part in range(count)
-        ],
+        ]
+        + [unread] * len(after),
         out_specs=pl.BlockSpec((rows, tile), lambda i: (0, i)),
         compiler_params=kernel_params(),
         cost_estimate=cost(0.1),
         name="to_features",
-    )(*lefts, *[part for parts in weights for part in parts])
+    )(*lefts, *[part for parts in weights for part in parts], *after)
 
 
 def to_groups(place, branch, parts):
@@ -929,40 +926,23 @@
 
     def kernel(place, *refs):
         lefts, right_ref, outs = refs[:shifts], refs[shifts], refs[shifts + 1 :]
-        step = pl.program_id(0)
-        total = 0.0
-        for distance, left in enumerate(lefts):
-            start = lax.rem(place[1] - distance + shifts, shifts) * local
-            here = pl.ds(pl.multiple_of(start, local), local)
-            total = total + inner_rows(left[0], right_ref[0, here, :])
         for part, out_ref in enumerate(outs):
-
-            @pl.when(step // 4 == part)
-            def _():
-                out_ref[...] = total.astype(jnp.bfloat16)
-
-    def left_at(p, place):
-        return (lax.rem(place[0] ^ block_key(p, bits), count), 0, 0)
-
-    def right_at(p, place):
-        return ((place[0] ^ block_key(p, bits)) // count, 0, 0)
-
-    def out_at(base, p, place):
-        return (jnp.clip(p - base, 0, 3), 0)
+            for block in range(4):
+                device = place[0] ^ block_key(4 * part + block, bits)
+                index = lax.rem(device, count)
+                group = device // count
+                total = 0.0
+                for distance, left in enumerate(lefts):
+                    start = lax.rem(place[1] - distance + shifts, shifts) * local
+                    here = pl.ds(pl.multiple_of(start, local), local)
+                    total = total + inner_rows(left[index], right_ref[group, here, :])
+                out_ref[block * features : (block + 1) * features, :] = total.astype(jnp.bfloat16)
 
     return pl.pallas_call(
         kernel,
-        grid_spec=pltpu.PrefetchScalarGridSpec(
-            num_scalar_prefetch=1,
-            grid=(1 << bits,),
-            in_specs=[pl.BlockSpec((1, local, features), left_at)] * shifts
-            + [pl.BlockSpec((1, rows, width), right_at)],
-            out_specs=[
-                pl.BlockSpec((features, width), functools.partial(out_at, 4 * part))
-                for part in range(parts)
-            ],
-        ),
         out_shape=[jax.ShapeDtypeStruct((4 * features, width), jnp.bfloat16)] * parts,
+        in_specs=[in_smem] + [in_vmem] * (shifts + 1),
+        out_specs=[in_vmem] * parts,
         compiler_params=kernel_params(),
         cost_estimate=cost(0.1),
         name="gradient_out",
@@ -983,18 +963,18 @@
     return [quarter, quarter, quarter, quarter // 2, quarter // 2]
 
 
-def gradient_part(left, right, parts, part, received=()):
+def gradient_part(left, right, parts, part, received=(), pieces=4, after=()):
     rows, depth = left.shape
     depth = depth // parts
     width = right.shape[1]
     tile = next(t for t in (1024, 768, 512, 256, LANES, width) if width % t == 0)
-    sizes = block_rows(depth) if received else [depth // 4] * 4
-    step = depth // 4
+    sizes = block_rows(depth) if received else [depth // pieces] * pieces
+    step = depth // max(1, len(received))
 
     def kernel(left_ref, right_ref, *refs):
         total = inner_rows(left_ref[...], right_ref[...])
         start = 0
-        for size, out_ref in zip(sizes, refs[len(received) :]):
+        for size, out_ref in zip(sizes, refs[len(received) + len(after) :]):
             piece = total[start : start + size]
             if received:
                 offset = start % step
@@ -1011,19 +991,23 @@
             pl.BlockSpec((rows, depth), lambda i: (0, part)),
             pl.BlockSpec((rows, tile), lambda i: (0, i)),
         ]
-        + [pl.BlockSpec((step, tile), lambda i: (0, i))] * len(received),
+        + [pl.BlockSpec((step, tile), lambda i: (0, i))] * len(received)
+        + [unread] * len(after),
         out_specs=[pl.BlockSpec((size, tile), lambda i: (0, i)) for size in sizes],
         compiler_params=kernel_params(),
         cost_estimate=cost(0.1),
         name="gradient_part",
-    )(left, right, *received)
-
-
-def gradient_begin(left, right, bits):
+    )(left, right, *received, *after)
+
+
+def gradient_begin(left, right, bits, pieces=4, after=()):
     parts = (1 << bits) // 4
     bit = bit_order(bits)[-1]
     return [
-        [swap(block, bit, bits) for block in gradient_part(left, right, parts, part)]
+        [
+            swap(block, bit, bits)
+            for block in gradient_part(left, right, parts, part, pieces=pieces, after=after)
+        ]
         for part in range(parts // 2, parts)
     ]
 
@@ -1035,6 +1019,37 @@
     kept = [jnp.concatenate(gradient_part(left, right, parts, p)) for p in range(parts // 2)]
     kept = [add_half(mine, jnp.concatenate(other)) for mine, other in zip(kept, received)]
     return sum_parts(kept, bits, bit_order(bits)[2:-1])
+
+
+def finish_input(place, gradient, residual, rows, gain, bits):
+    local, depth = gradient.shape
+    width = depth >> bits
+    whole_lanes = width % LANES == 0
+
+    def kernel(place, grad_ref, residual_ref, rows_ref, gain_ref, out_ref, *scratch):
+        start = pl.multiple_of(place[1] * local, local)
+        values = rows_ref[pl.ds(start, local), :].astype(jnp.float32)
+        factor = rms_scale(values)
+        normed = values * factor
+        scaled = grad_ref[...].astype(jnp.float32) * gain_ref[...]
+        total = residual_ref[...] + norm_back(scaled, normed, factor)
+        if not whole_lanes:
+            out_ref[...] = total
+            return
+        for p in range(1 << bits):
+            other = pl.multiple_of((place[0] ^ block_key(p, bits)) * width, LANES)
+            out_ref[:, pl.ds(other, width)] = total[:, p * width : (p + 1) * width]
+
+    out = pl.pallas_call(
+        kernel,
+        out_shape=jax.ShapeDtypeStruct((local, depth), jnp.float32),
+        in_specs=[in_smem] + [in_vmem] * 4,
+        out_specs=in_vmem,
+        compiler_params=kernel_params(),
+        cost_estimate=cost(0.1),
+        name="finish_input",
+    )(place, gradient, residual, rows, gain)
+    return out if whole_lanes else to_absolute(out, place[0], bits)
 
 
 def sum_parts(parts, bits, over):
@@ -1121,28 +1136,35 @@
     queries, kv = project_qkv(attn_in, qkv_w, cosine, sine, width_q, width_k)
     kv_one = gather_one(kv, bits)
     kv_all = join(gather_end(kv, kv_one, gather_two(kv_one, bits), bits))
-    kv_all, w_up, w_down, *gate_two = window(kv_all, w_up, w_down, *gate_two)
+    kv_all, w_up, w_down = window(kv_all, w_up, w_down)
 
     up_one = gather_one(w_up, bits)
     attended, exact, log_total = attend_forward(pair_slot, place, queries, kv_all, bits)
-    attended, both_all, w_down, *up_one = window(attended, both_all, w_down, *up_one)
+    attended, both_all, w_down, *pieces = window(
+        attended, both_all, w_down, *gate_two, *up_one
+    )
+    gate_two, up_one = cut(pieces, 2, 2)
 
     attended_all = lax.all_gather(attended, "tp", axis=0)
     grad_rows = both_all[:, :local_rows].reshape(group_rows, model)
     wo_groups = both_all[:, local_rows:].reshape(shifts, *wo.shape)
     o_one = gather_one(wo_groups, bits)
     up_two = gather_two(up_one, bits)
+    o_two = gather_two(o_one, bits, 1)
+    gate_w = gather_end(w_gate, gate_one, gate_two, bits)
+    attended_all, grad_rows, w_down, *pieces = window(
+        attended_all, grad_rows, w_down, *o_two, *up_two, *gate_w
+    )
+    o_two, up_two, gate_w = cut(pieces, 2, 2, count)
+
     down_one = gather_one(w_down, bits)
-    gate_w = gather_end(w_gate, gate_one, gate_two, bits)
     up_w = gather_end(w_up, up_one, up_two, bits)
-    attended_all, grad_rows, *pieces = window(attended_all, grad_rows, *o_one, *gate_w, *up_w)
-    o_one, gate_w, up_w = cut(pieces, 2, count, count)
-
-    o_two = gather_two(o_one, bits, 1)
     o_w = gather_end(wo_groups, o_one, o_two, bits, 1)
+    mlp_in, residual_here = project_residual(place, attended_all, rows_all, g_mlp, o_w)
+    mlp_in, residual_here, *pieces = window(mlp_in, residual_here, *down_one, *up_w)
+    down_one, up_w = cut(pieces, 2, count)
     down_two = gather_two(down_one, bits)
     down_w = gather_end(w_down, down_one, down_two, bits)
-    mlp_in, residual_here = project_residual(place, attended_all, rows_all, g_mlp, o_w)
     factor_mlp = rms_scale(residual_here)
     normed_mlp = residual_here * factor_mlp
 
@@ -1159,11 +1181,12 @@
     gate_sum = gradient_end(mlp_in, grad_gate, gate_sum, bits)
     down_two = scatter_two(down_sum, scatter_one(down_sum, bits))
     up_two = scatter_two(up_sum, scatter_one(up_sum, bits))
+    gate_one = scatter_one(gate_sum, bits)
     mlp_part = to_features([hidden], [down_w])
     grad_mlp_in, mlp_part, *pieces = window(
-        grad_mlp_in, mlp_part, *down_two, *up_two, *gate_sum
-    )
-    down_two, up_two, gate_sum = cut(pieces, 2, 2, 5)
+        grad_mlp_in, mlp_part, *down_two, *up_two, *gate_one, *gate_sum
+    )
+    down_two, up_two, gate_one, gate_sum = cut(pieces, 2, 2, 2, 5)
 
     down_three = scatter_three(down_two, bits)
     grad_mlp_in = grad_mlp_in.astype(jnp.float32)
@@ -1174,37 +1197,34 @@
     branch_here = grad_residual.astype(jnp.bfloat16)
     grad_groups = to_groups(place, branch_here, o_w)
     grad_parts = jnp.stack(tp_exchange(grad_groups))
+    gate_two = scatter_two(gate_sum, gate_one)
+    grad_parts, branch_here, mlp_part, *pieces = window(
+        grad_parts, branch_here, mlp_part, *down_three, *up_two, *gate_two
+    )
+    down_three, up_two, gate_two = cut(pieces, 2, 2, 2)
+
+    up_three = scatter_three(up_two, bits)
+    gate_three = scatter_three(gate_two, bits)
     branch_blocks = to_block_groups(place, branch_here, bits, shifts)
-    grad_parts, branch_blocks, mlp_part, *pieces = window(
-        grad_parts, branch_blocks, mlp_part, *down_three, *up_two, *gate_sum
-    )
-    down_three, up_two, gate_sum = cut(pieces, 2, 2, 5)
-
-    up_three = scatter_three(up_two, bits)
-    branch_pieces = tp_exchange(branch_blocks)
     mlp_out = lax.psum_scatter(mlp_part, "tp", scatter_dimension=0, tiled=True)
     grad_queries, *grad_kv = attend_backward(
         pair_slot, place, queries, kv_all, grad_parts, exact, log_total, cosine, sine, bits
     )
-    pieces = window(*grad_kv, *branch_pieces, *up_three, *gate_sum)
-    grad_kv, branch_pieces, up_three, gate_sum = cut(pieces, count, shifts, 2, 5)
+    branch_blocks, *pieces = window(branch_blocks, *grad_kv, *up_three)
+    grad_kv, up_three = cut(pieces, count, 2)
 
     kv_sum = rows_begin(grad_kv, bits)
     kv_three = scatter_three(scatter_two(kv_sum, scatter_one(kv_sum, bits)), bits)
-    gate_one = scatter_one(gate_sum, bits)
-    o_sum = gradient_out(place, branch_pieces, attended_all, bits)
-    mlp_out, *pieces = window(mlp_out, kv_sum[0], *kv_three, *o_sum, *gate_one)
-    kv_pieces, o_sum, gate_one = cut(pieces, 3, count, 2)
+    branch_pieces = tp_exchange(branch_blocks)
+    mlp_out, *pieces = window(mlp_out, kv_sum[0], *kv_three, *branch_pieces)
+    kv_pieces, branch_pieces = cut(pieces, 3, shifts)
     grad_qkv = join_grad_qkv(grad_queries, kv_pieces, cosine, sine)
     grad_attn_part = to_features([grad_qkv], [qkv_w])
-    gate_three = scatter_three(scatter_two(gate_sum, gate_one), bits)
-    o_sum = rows_begin(o_sum, bits)
-    grad_attn_part, grad_qkv, *o_sum = window(grad_attn_part, grad_qkv, *o_sum)
+    grad_attn_part, grad_qkv, *branch_pieces = window(grad_attn_part, grad_qkv, *branch_pieces)
 
     grad_attn_in = lax.psum_scatter(grad_attn_part, "tp", scatter_dimension=0, tiled=True)
-    qkv_sum = gradient_begin(attn_in, grad_qkv, bits)
+    qkv_sum = gradient_begin(attn_in, grad_qkv, bits, pieces=1)
     qkv_sum = gradient_end(attn_in, grad_qkv, qkv_sum, bits)
-    o_two = scatter_two(o_sum, scatter_one(o_sum, bits))
     inputs = rows_all.astype(jnp.float32)
     gain_attn_part = jnp.sum(
         grad_attn_part.astype(jnp.float32) * (inputs * rms_scale(inputs)), axis=0, keepdims=True
@@ -1214,43 +1234,46 @@
     order = bit_order(bits)
     for bit in reversed(order[2:]):
         gain_sum = scatter_step(gain_sum, bit, bits)
-    gain_sum, *pieces = window(gain_sum, *qkv_sum, *o_two, *gate_three)
-    qkv_sum, o_two, gate_three = cut(pieces, 5, 2, 2)
+    o_sum = rows_begin(gradient_out(place, branch_pieces, attended_all, bits), bits)
+    gain_sum, *pieces = window(gain_sum, *qkv_sum, *o_sum, *gate_three, *down_three, *up_three)
+    qkv_sum, o_sum, gate_three, down_three, up_three = cut(pieces, 5, 5, 2, 2, 2)
 
     qkv_two = scatter_two(qkv_sum, scatter_one(qkv_sum, bits))
-    o_three = scatter_three(o_two, bits)
+    o_two = scatter_two(o_sum, scatter_one(o_sum, bits))
     gain_sum = scatter_step(gain_sum, order[1], bits)
-    gain_sum, *pieces = window(gain_sum, *qkv_two, *o_three)
-    qkv_two, o_three = cut(pieces, 2, 2)
-
-    qkv_three = scatter_three(qkv_two, bits)
+    pieces = window(gain_sum, *qkv_two, *o_two, *gate_three, *down_three, *up_three, mlp_out)
+    (gain_sum,), qkv_two, o_two, gate_three, down_three, up_three, (mlp_out,) = cut(
+        pieces, 1, 2, 2, 2, 2, 2, 1
+    )
+
+    qkv_three, o_three = scatter_three(qkv_two, bits), scatter_three(o_two, bits)
     gain_sum = scatter_step(gain_sum, order[0], bits)
-    sum_o_w = finish_sum(o_sum, o_three).astype(jnp.bfloat16)
-    gain_sum, sum_o_w, *qkv_three = window(gain_sum, sum_o_w, *qkv_three)
-
-    sum_down_w = finish_sum(down_sum, down_three)
-    sum_up_w = finish_sum(up_sum, up_three)
-    sum_o_w = to_owners(sum_o_w, (1 << bits) // shifts).astype(jnp.float32)
-    gain_here = sum(tp_gather(gain_sum[0]))
-    sum_qkv_w = finish_sum(qkv_sum, qkv_three)
-    sum_gate_w = finish_sum(gate_sum, gate_three)
+    (sum_down_w,) = finish_sum(down_sum, down_three)
+    (sum_up_w,) = finish_sum(up_sum, up_three)
+    gain_sum, sum_down_w, sum_up_w, *pieces = window(
+        gain_sum, sum_down_w, sum_up_w, *qkv_three, *o_three
+    )
+    qkv_three, o_three = cut(pieces, 2, 2)
+
+    (sum_o_w,) = finish_sum(o_sum, o_three)
+    sum_o_w = to_owners(sum_o_w.astype(jnp.bfloat16), (1 << bits) // shifts)
+    gain_here, shift = gain_sum[0], 1
+    while shift < shifts:
+        gain_here = sum_step(gain_here, shift, "tp")
+        shift *= 2
+    (sum_gate_w,) = finish_sum(gate_sum, gate_three)
     block_out = (residual_here + mlp_out.astype(jnp.float32)).astype(jnp.bfloat16)
     block_out = reorder(place, block_out, bits, inverse=True)
-    grad_attn_in = grad_attn_in.astype(jnp.float32)
-    inputs_here = lax.dynamic_slice_in_dim(rows_all, tp * local_rows, local_rows)
-    inputs_here = inputs_here.astype(jnp.float32)
-    factor_attn = rms_scale(inputs_here)
-    input_grad = grad_residual + norm_back(
-        grad_attn_in * g_attn, inputs_here * factor_attn, factor_attn
-    )
+    input_grad = finish_input(place, grad_attn_in, grad_residual, rows_all, g_attn, bits)
+    sum_q_w, sum_k_w, sum_v_w = finish_sum(qkv_sum, qkv_three, [width_q, width_k, width_k])
     return (
         block_out,
-        reorder(place, input_grad, bits, inverse=True),
+        input_grad,
         gain_here[0],
-        sum_qkv_w[:, :width_q],
-        sum_qkv_w[:, width_q : width_q + width_k],
-        sum_qkv_w[:, width_q + width_k :],
-        sum_o_w,
+        sum_q_w,
+        sum_k_w,
+        sum_v_w,
+        sum_o_w.astype(jnp.float32),
         gain_here[1],
         sum_gate_w,
         sum_up_w,

time: 600 us -> 568 us (0.947)
  waiting for transfers between devices: 179 us -> 163 us
  local copies, waits for them, and re-layouts: 36.8 us -> 26.8 us
    all_gather x1, waiting for transfers between devices: 17.4 us -> 0.01 us  [on_device(): attended_all = lax.all_gather(attended, 'tp', axis=0)]
    ppermute x1, waiting for transfers between devices: 16.6 us -> 4.78 us  [to_owners(): return lax.ppermute(array, ('ctx', 'tp'), moves)]
    ppermute x9 -> x6, waiting for transfers between devices: 4.09 us -> 13.2 us  [tp_shift(): lax.ppermute(array, 'tp', [(i, (i + distance) % size) for i in range(size)])]
    ppermute x0 -> x2, waiting for transfers between devices: none -> 6.51 us  [sum_step(): lax.ppermute(array, axis, [(i, i ^ shift) for i in range(size)])]
    ppermute x9 -> x6, starting transfers between devices: 14.6 us -> 9.43 us  [tp_shift(): lax.ppermute(array, 'tp', [(i, (i + distance) % size) for i in range(size)])]
    ppermute x78 -> x75, waiting for transfers between devices: 140 us -> 137 us  [swap(): lax.ppermute(array, 'ctx', [(i, i ^ 1 << bit) for i in range(1 << bits)])]
    unnamed x146 -> x144, local copies, waits for them, and re-layouts: 15.8 us -> 14.5 us
    ppermute x78 -> x75, starting transfers between devices: 61.6 us -> 61.5 us  [swap(): lax.ppermute(array, 'ctx', [(i, i ^ 1 << bit) for i in range(1 << bits)])]
  transfers between devices with their start and end apart: 94 -> 90, of which waited for: 30 -> 31; matrix products, arithmetic and copies ran while one was open for 6% -> 5% of each run, Pallas kernels for 37% -> 35%
where the time goes in v3:
time: 568 us; the launch traced here: 559 us
  Pallas kernels  261 us (46%)
  waiting for transfers between devices  163 us (29%)
  starting transfers between devices  79.2 us (14%)
  local copies, waits for them, and re-layouts  26.8 us (5%)
  between operations  15.5 us (3%)
  other arithmetic  13.8 us (2%)
    ppermute x75, waiting for transfers between devices, swap(): lax.ppermute(array, 'ctx', [(i, i ^ 1 << bit) for i in range(1 << bits)])  137 us
    ppermute x75, starting transfers between devices, swap(): lax.ppermute(array, 'ctx', [(i, i ^ 1 << bit) for i in range(1 << bits)])  61.5 us
    pallas_call x8, Pallas kernels, gradient_part(): pl.pallas_call(kernel, grid=(width // tile,), out_shape=[jax.ShapeDtypeSt...  44.8 us
    pallas_call x3, Pallas kernels, to_features(): pl.pallas_call(kernel, grid=(count * tiles,), out_shape=jax.ShapeDtypeStr...  34.4 us
    pallas_call x1, Pallas kernels, attend_backward(): pl.pallas_call(functools.partial(backward_kernel, bits, heads), out_shape...  30 us
    pallas_call x8, Pallas kernels, join(): pl.pallas_call(kernel, out_shape=jax.ShapeDtypeStruct(shape, pieces[0].dt...  26.7 us
    pallas_call x1, Pallas kernels, mlp_inner(): pl.pallas_call(functools.partial(mlp_kernel, count), grid=(units // tile,...  20.4 us
    pallas_call x1, Pallas kernels, attend_forward(): pl.pallas_call(functools.partial(forward_kernel, bits, heads), out_shape=...  18.9 us
  transfers between devices with their start and end apart: 90, of which 31 were waited for; matrix products, arithmetic and copies ran while one was open for 5% of the time, Pallas kernels for 35%

profile of v3, /device:TPU:2, one launch (start us, length us, event | category | flops | bytes accessed | tf_op | source)
XLA Modules:
  0.0 558.8 jit_solution(6367474106506340677)
XLA Ops:
  15.3 6.7 %collective-permute-done.3.refs_1_ = bf16[256,768]{1,0:T(8,128)(2,1)S(1)} collective-permute-done((bf16[256,768]{1,0:T(8,128)(2,1)}, bf16[256,768]{1,0:T(8,128)(2,1)S(1)}, u32[]{:S(2)}, u32[]{:S(2)}) %collective-permute-start.3) | collective-permute-done | bytes 393248 | tf_op jit(solution)/shard_map/ppermute | solution.py:62
  24.2 23.4 %collective-permute-done.5.refs_3_ = bf16[128,768]{1,0:T(8,128)(2,1)S(1)} collective-permute-done((bf16[128,768]{1,0:T(8,128)(2,1)S(1)}, bf16[128,768]{1,0:T(8,128)(2,1)S(1)}, u32[]{:S(2)}, u32[]{:S(2)}) %collective-permute-start.5) | collective-permute-done | bytes 196640 | tf_op jit(solution)/shard_map/ppermute | solution.py:62
  64.1 4.0 norm_rows.1
  68.2 5.9 %qkv.1 = (bf16[512,512]{1,0:T(8,128)(2,1)}, bf16[512,256]{1,0:T(8,128)(2,1)}) custom-call(bf16[512,2048]{1,0:T(8,128)(2,1)} %get-tuple-element.201.x_ref.left_ref, bf16[1024,768]{1,0:T(8,128)(2,1)} %join.9.refs_0_.refs_1_, bf16[1024,768]{1,0:T(8,128)(2,1)} %copy-done.4, f32[512,128]{1,0:T(8,128)} %copy.23.refs_2_.refs_5_.cos_ref, ...), custom_call_target="tpu_custom_call" | custom-call | flops 110000000 | bytes 1024 | tf_op jit(solution)/shard_map/qkv/pallas_call | solution.py:405
  77.4 5.3 collective-permute-done.10.refs_1_
  101.7 18.9 %attention_forward.1 = (bf16[512,512]{1,0:T(8,128)(2,1)}, f32[512,512]{1,0:T(8,128)}, f32[8,512]{1,0:T(8,128)}) custom-call(s32[8]{0:T(128)} %slots.3, s32[2]{0:T(128)} %pad_add_fusion.place, bf16[512,512]{1,0:T(8,128)(2,1)} %get-tuple-element.206.q_ref.refs_0_, bf16[4096,256]{1,0:T(8,128)(2,1)} %join.11.kv_ref.refs_1_), custom_call_target="tpu_custom_call" | custom-call | flops 20899999744 | bytes 1024 | tf_op jit(solution)/shard_map/attention_forward/pallas_call | solution.py:517
  120.7 10.8 %collective-permute-done.17.refs_1_ = bf16[256,2048]{1,0:T(8,128)(2,1)S(1)} collective-permute-done((bf16[256,2048]{1,0:T(8,128)(2,1)S(1)}, bf16[256,2048]{1,0:T(8,128)(2,1)S(1)}, u32[]{:S(2)}, u32[]{:S(2)}) %collective-permute-start.17) | collective-permute-done | bytes 1048608 | tf_op jit(solution)/shard_map/ppermute | solution.py:62
  131.5 4.6 join.12.refs_0_.refs_2_
  144.2 20.6 %collective-permute-done.19.refs_1_ = bf16[4,256,512]{2,1,0:T(8,128)(2,1)S(1)} collective-permute-done((bf16[4,256,512]{2,1,0:T(8,128)(2,1)S(1)}, bf16[4,256,512]{2,1,0:T(8,128)(2,1)S(1)}, u32[]{:S(2)}, u32[]{:S(2)}) %collective-permute-start.19) | collective-permute-done | bytes 1048608 | tf_op jit(solution)/shard_map/ppermute | solution.py:62
  169.9 7.1 %collective-permute-done.23.refs_3_ = bf16[128,2048]{1,0:T(8,128)(2,1)S(1)} collective-permute-done((bf16[128,2048]{1,0:T(8,128)(2,1)S(1)}, bf16[128,2048]{1,0:T(8,128)(2,1)S(1)}, u32[]{:S(2)}, u32[]{:S(2)}) %collective-permute-start.23) | collective-permute-done | bytes 524320 | tf_op jit(solution)/shard_map/ppermute | solution.py:62
  177.0 10.6 %collective-permute-done.20.refs_3_ = bf16[4,128,512]{2,1,0:T(8,128)(2,1)} collective-permute-done((bf16[4,128,512]{2,1,0:T(8,128)(2,1)S(1)}, bf16[4,128,512]{2,1,0:T(8,128)(2,1)}, u32[]{:S(2)}, u32[]{:S(2)}) %collective-permute-start.20) | collective-permute-done | bytes 524320 | tf_op jit(solution)/shard_map/ppermute | solution.py:62
  187.6 4.2 join.13.part_ref.refs_0_
  192.0 4.3 join.14.refs_2_.refs_4_
  198.6 6.5 %project_part.1.refs_0_ = f32[512,1024]{1,0:T(8,128)} custom-call(bf16[4,512,512]{2,1,0:T(8,128)(2,1)} %bitcast.45, bf16[4,1024,512]{2,1,0:T(8,128)(2,1)} %join.13.part_ref.refs_0_), custom_call_target="tpu_custom_call" | custom-call | flops 110000000 | bytes 1024 | tf_op jit(solution)/shard_map/project_part/pallas_call | solution.py:725
  207.2 9.7 %project_residual.1 = (bf16[512,2048]{1,0:T(8,128)(2,1)}, f32[128,2048]{1,0:T(8,128)}) custom-call(s32[2]{0:T(128)} %pad_add_fusion.place, bf16[4,512,512]{2,1,0:T(8,128)(2,1)} %bitcast.46, bf16[512,2048]{1,0:T(8,128)(2,1)} %get-tuple-element.224.x_ref.rows_ref, f32[1,2048]{1,0:T(1,128)} %get-tuple-element.399.gain_ref, bf16[4,1024,512]{2,1,0:T(8,128)(2,1)} %copy-done.2, ...), custom_call_target="tpu_custom_call" | custom-call | flops 110000000 | bytes 1024 | tf_op jit(solution)/shard_map/project_residual/pallas_call | solution.py:792
  216.9 5.0 collective-permute-done.27.refs_1_
  225.4 10.3 %collective-permute-done.30.refs_3_ = bf16[128,2048]{1,0:T(8,128)(2,1)S(1)} collective-permute-done((bf16[128,2048]{1,0:T(8,128)(2,1)S(1)}, bf16[128,2048]{1,0:T(8,128)(2,1)S(1)}, u32[]{:S(2)}, u32[]{:S(2)}) %collective-permute-start.30) | collective-permute-done | bytes 524320 | tf_op jit(solution)/shard_map/ppermute | solution.py:62
  237.3 4.2 join.15.refs_4_.refs_1_
  241.6 7.4 %collective-permute-done.32.refs_5_.refs_2_ = bf16[1024,2048]{1,0:T(8,128)(2,1)S(1)} collective-permute-done((bf16[1024,2048]{1,0:T(8,128)(2,1)}, bf16[1024,2048]{1,0:T(8,128)(2,1)S(1)}, u32[]{:S(2)}, u32[]{:S(2)}) %collective-permute-start.32) | collective-permute-done | bytes 4194336 | tf_op jit(solution)/shard_map/ppermute | solution.py:62
  250.9 20.4 %mlp_inner.1 = (bf16[512,2048]{1,0:T(8,128)(2,1)}, bf16[512,2048]{1,0:T(8,128)(2,1)}, bf16[512,2048]{1,0:T(8,128)(2,1)}) custom-call(bf16[512,2048]{1,0:T(8,128)(2,1)} %get-tuple-element.233.x_ref.left_ref, bf16[512,2048]{1,0:T(8,128)(2,1)} %bitcast.42, bf16[1024,2048]{1,0:T(8,128)(2,1)} %join.12.refs_0_.refs_2_, ...), custom_call_target="tpu_custom_call" | custom-call | flops 110000000 | bytes 1024 | tf_op jit(solution)/shard_map/mlp_inner/pallas_call | solution.py:702
  271.3 15.8 %to_features.3 = bf16[512,2048]{1,0:T(8,128)(2,1)} custom-call(bf16[512,2048]{1,0:T(8,128)(2,1)} %get-tuple-element.267.refs_0_.right_ref, bf16[512,2048]{1,0:T(8,128)(2,1)} %get-tuple-element.256.refs_1_.right_ref, bf16[1024,2048]{1,0:T(8,128)(2,1)} %join.12.refs_0_.refs_2_, bf16[1024,2048]{1,0:T(8,128)(2,1)} %collective-permute-done.25.refs_1_.refs_3_, ...), custom_call_target="tpu_custom_call" | custom-call | flops 110000000 | bytes 1024 | tf_op jit(solution)/shard_map/to_features/pallas_call | solution.py:840
  287.3 5.4 gradient_part.8
  293.7 5.6 gradient_part.10
  300.4 5.6 %gradient_part.12 = (bf16[256,2048]{1,0:T(8,128)(2,1)}, bf16[256,2048]{1,0:T(8,128)(2,1)}, bf16[256,2048]{1,0:T(8,128)(2,1)}, bf16[256,2048]{1,0:T(8,128)(2,1)}) custom-call(bf16[512,2048]{1,0:T(8,128)(2,1)} %get-tuple-element.233.x_ref.left_ref, bf16[512,2048]{1,0:T(8,128)(2,1)} %get-tuple-element.267.refs_0_.right_ref), custom_call_target="tpu_custom_call" | custom-call | flops 110000000 | bytes 1024 | tf_op jit(solution)/shard_map/gradient_part/pallas_call | solution.py:986
  307.1 7.1 %gradient_part.9 = (bf16[256,2048]{1,0:T(8,128)(2,1)}, bf16[256,2048]{1,0:T(8,128)(2,1)}, bf16[256,2048]{1,0:T(8,128)(2,1)}, bf16[128,2048]{1,0:T(8,128)(2,1)}, bf16[128,2048]{1,0:T(8,128)(2,1)}) custom-call(bf16[512,2048]{1,0:T(8,128)(2,1)} %bitcast.44, bf16[512,2048]{1,0:T(8,128)(2,1)} %get-tuple-element.245.refs_0_.right_ref, ...), custom_call_target="tpu_custom_call" | custom-call | flops 110000000 | bytes 1024 | tf_op jit(solution)/shard_map/gradient_part/pallas_call | solution.py:986
  316.5 6.7 %gradient_part.11 = (bf16[256,2048]{1,0:T(8,128)(2,1)}, bf16[256,2048]{1,0:T(8,128)(2,1)}, bf16[256,2048]{1,0:T(8,128)(2,1)}, bf16[128,2048]{1,0:T(8,128)(2,1)}, bf16[128,2048]{1,0:T(8,128)(2,1)}) custom-call(bf16[512,2048]{1,0:T(8,128)(2,1)} %get-tuple-element.233.x_ref.left_ref, bf16[512,2048]{1,0:T(8,128)(2,1)} %get-tuple-element.256.refs_1_.right_ref, ...), custom_call_target="tpu_custom_call" | custom-call | flops 110000000 | bytes 1024 | tf_op jit(solution)/shard_map/gradient_part/pallas_call | solution.py:986
  325.3 6.7 %gradient_part.13 = (bf16[256,2048]{1,0:T(8,128)(2,1)}, bf16[256,2048]{1,0:T(8,128)(2,1)}, bf16[256,2048]{1,0:T(8,128)(2,1)}, bf16[128,2048]{1,0:T(8,128)(2,1)}, bf16[128,2048]{1,0:T(8,128)(2,1)}) custom-call(bf16[512,2048]{1,0:T(8,128)(2,1)} %get-tuple-element.233.x_ref.left_ref, bf16[512,2048]{1,0:T(8,128)(2,1)} %get-tuple-element.267.refs_0_.right_ref, ...), custom_call_target="tpu_custom_call" | custom-call | flops 110000000 | bytes 1024 | tf_op jit(solution)/shard_map/gradient_part/pallas_call | solution.py:986
  334.3 10.9 %to_features.4 = bf16[512,2048]{1,0:T(8,128)(2,1)} custom-call(bf16[512,2048]{1,0:T(8,128)(2,1)} %get-tuple-element.245.refs_0_.right_ref, bf16[1024,2048]{1,0:T(8,128)(2,1)} %join.15.refs_4_.refs_1_, bf16[1024,2048]{1,0:T(8,128)(2,1)} %copy-done.1), custom_call_target="tpu_custom_call" | custom-call | flops 110000000 | bytes 1024 | tf_op jit(solution)/shard_map/to_features/pallas_call | solution.py:840
  345.2 3.3 scatter_two.6
  348.6 3.3 scatter_two.7
  358.8 6.3 %to_groups.1 = bf16[4,128,512]{2,1,0:T(8,128)(2,1)} custom-call(s32[2]{0:T(128)} %pad_add_fusion.place, bf16[128,2048]{1,0:T(8,128)(2,1)} %get-tuple-element.294.x_ref.in_ref, bf16[4,1024,512]{2,1,0:T(8,128)(2,1)} %join.13.part_ref.refs_0_, bf16[4,1024,512]{2,1,0:T(8,128)(2,1)} %copy-done.2), custom_call_target="tpu_custom_call" | custom-call | flops 110000000 | bytes 1024 | tf_op jit(solution)/shard_map/to_groups/pallas_call | solution.py:873
  366.3 3.7 collective-permute-start.53
  374.2 6.5 %collective-permute-done.52 = bf16[128,512]{1,0:T(8,128)(2,1)S(1)} collective-permute-done((bf16[128,512]{1,0:T(8,128)(2,1)S(1)}, bf16[128,512]{1,0:T(8,128)(2,1)S(1)}, u32[]{:S(2)}, u32[]{:S(2)}) %collective-permute-start.52) | collective-permute-done | bytes 131104 | tf_op jit(solution)/shard_map/ppermute | solution.py:207
  383.9 30.0 %attention_backward.1 = (bf16[512,512]{1,0:T(8,128)(2,1)}, bf16[2048,256]{1,0:T(8,128)(2,1)}, bf16[2048,256]{1,0:T(8,128)(2,1)}) custom-call(s32[8]{0:T(128)} %slots.3, s32[2]{0:T(128)} %pad_add_fusion.place, bf16[512,512]{1,0:T(8,128)(2,1)} %get-tuple-element.206.q_ref.refs_0_, bf16[4096,256]{1,0:T(8,128)(2,1)} %join.11.kv_ref.refs_1_, ...), custom_call_target="tpu_custom_call" | custom-call | flops 32999999488 | bytes 1024 | tf_op jit(solution)/shard_map/attention_backward/pallas_call | solution.py:625
  424.5 3.6 collective-permute-done.59.lower_ref
  439.1 3.5 collective-permute-done.63.refs_1_
  449.3 7.7 %to_features.5 = bf16[512,2048]{1,0:T(8,128)(2,1)} custom-call(bf16[512,768]{1,0:T(8,128)(2,1)} %grad_qkv.1.refs_0_.right_ref, bf16[1024,768]{1,0:T(8,128)(2,1)} %join.9.refs_0_.refs_1_, bf16[1024,768]{1,0:T(8,128)(2,1)} %copy-done.4), custom_call_target="tpu_custom_call" | custom-call | flops 110000000 | bytes 1024 | tf_op jit(solution)/shard_map/to_features/pallas_call | solution.py:840
  457.0 3.7 gradient_part.14
  462.4 5.3 gradient_out.1
  474.7 4.0 gradient_part.15
  478.7 8.0 %collective-permute-done.69.first_ref = bf16[256,2048]{1,0:T(8,128)(2,1)} collective-permute-done((bf16[256,2048]{1,0:T(8,128)(2,1)}, bf16[256,2048]{1,0:T(8,128)(2,1)}, u32[]{:S(2)}, u32[]{:S(2)}) %collective-permute-start.69) | collective-permute-done | bytes 1048608 | tf_op jit(solution)/shard_map/ppermute | solution.py:62
  492.1 5.0 collective-permute-done.74.lower_ref
  512.1 3.5 finish_sum.5
  515.6 3.5 finish_sum.6
  519.1 3.5 finish_sum.9
  535.2 6.5 %collective-permute-done.82 = f32[2,256]{1,0:T(2,128)S(1)} collective-permute-done((f32[2,256]{1,0:T(2,128)S(1)}, f32[2,256]{1,0:T(2,128)S(1)}, u32[]{:S(2)}, u32[]{:S(2)}) %collective-permute-start.82) | collective-permute-done | bytes 2080 | tf_op jit(solution)/shard_map/ppermute | solution.py:135
  542.3 4.8 collective-permute-done.83
  547.9 3.6 finish_input.1
  (390 shorter events, 170.1 us)
Async XLA Ops:
  7.2 54.3 %all-gather.6.cloned.1.call-start = ((), (), s32[]{:S(2)}) async-start(), calls=%async_computation.3 | async-start | bytes 2621440 | tf_op jit(solution)/shard_map/all_gather | solution.py:1114
  7.9 123.6 %all-gather.8.cloned.1.call-start = ((), (), s32[]{:S(2)}) async-start(), calls=%async_computation.7 | async-start | bytes 3932160 | tf_op jit(solution)/shard_map/all_gather | solution.py:1133
  11.8 49.6 %collective-permute-start.8 = (bf16[256,2048]{1,0:T(8,128)(2,1)}, bf16[256,2048]{1,0:T(8,128)(2,1)S(1)}, u32[]{:S(2)}, u32[]{:S(2)}) collective-permute-start(bf16[256,2048]{1,0:T(8,128)(2,1)} %refs_0_.3), channel_id=1, source_target_pairs={{0,8},{4,12},{8,0},{12,4},{16,24},{20,28},{24,16},{28,20},{1,9},{5... | collective-permute-start | bytes 3145736 | tf_op jit(solution)/shard_map/ppermute | solution.py:62
  13.3 48.1 %collective-permute-start.9 = (bf16[256,2048]{1,0:T(8,128)(2,1)}, bf16[256,2048]{1,0:T(8,128)(2,1)}, u32[]{:S(2)}, u32[]{:S(2)}) collective-permute-start(bf16[256,2048]{1,0:T(8,128)(2,1)} %refs_0_.3), channel_id=1, source_target_pairs={{0,16},{4,20},{8,24},{12,28},{16,0},{20,4},{24,8},{28,12},{1,17},{... | collective-permute-start | bytes 3145736 | tf_op jit(solution)/shard_map/ppermute | solution.py:62
  15.2 41.3 %collective-permute-start = (bf16[1,2,256]{2,1,0:T(2,128)(2,1)S(1)}, bf16[1,2,256]{2,1,0:T(2,128)(2,1)S(1)}, u32[]{:S(2)}, u32[]{:S(2)}) collective-permute-start(bf16[1,2,256]{2,1,0:T(2,128)(2,1)S(1)} %maximum_bitcast_fusion.1), channel_id=1, source_target_pairs={{0,8},{4,12},{8,0},{12,4},{16,24},{20,28},{24,16},{28,20},{1,9},{5... | collective-permute-start | bytes 3080 | tf_op jit(solution)/shard_map/ppermute | solution.py:62
  22.0 25.6 %collective-permute-start.5 = (bf16[128,768]{1,0:T(8,128)(2,1)S(1)}, bf16[128,768]{1,0:T(8,128)(2,1)S(1)}, u32[]{:S(2)}, u32[]{:S(2)}) collective-permute-start(bf16[128,768]{1,0:T(8,128)(2,1)S(1)} %slice.128), channel_id=1, source_target_pairs={{0,16},{4,20},{8,24},{12,28},{16,0},{20,4},{24,8},{28,12},{1,17},{... | collective-permute-start | bytes 589832 | tf_op jit(solution)/shard_map/ppermute | solution.py:62
  23.6 24.0 %collective-permute-start.6 = (bf16[128,768]{1,0:T(8,128)(2,1)S(1)}, bf16[128,768]{1,0:T(8,128)(2,1)S(1)}, u32[]{:S(2)}, u32[]{:S(2)}) collective-permute-start(bf16[128,768]{1,0:T(8,128)(2,1)S(1)} %slice.129), channel_id=1, source_target_pairs={{0,8},{4,12},{8,0},{12,4},{16,24},{20,28},{24,16},{28,20},{1,9},{5... | collective-permute-start | bytes 589832 | tf_op jit(solution)/shard_map/ppermute | solution.py:62
  61.6 126.0 %all-gather.10.cloned.1.call-start = ((), (), s32[]{:S(2)}) async-start(), calls=%async_computation.8 | async-start | bytes 2621440 | tf_op jit(solution)/shard_map/all_gather | solution.py:1148
  92.5 28.2 %collective-permute-start.15 = (bf16[128,2048]{1,0:T(8,128)(2,1)S(1)}, bf16[128,2048]{1,0:T(8,128)(2,1)S(1)}, u32[]{:S(2)}, u32[]{:S(2)}) collective-permute-start(bf16[128,2048]{1,0:T(8,128)(2,1)S(1)} %slice.101), channel_id=1, source_target_pairs={{0,16},{4,20},{8,24},{12,28},{16,0},{20,4},{24,8},{28,12},{1,17},{... | collective-permute-start | bytes 1572872 | tf_op jit(solution)/shard_map/ppermute | solution.py:62
  94.9 25.7 %collective-permute-start.16 = (bf16[128,2048]{1,0:T(8,128)(2,1)S(1)}, bf16[128,2048]{1,0:T(8,128)(2,1)S(1)}, u32[]{:S(2)}, u32[]{:S(2)}) collective-permute-start(bf16[128,2048]{1,0:T(8,128)(2,1)S(1)} %slice.102), channel_id=1, source_target_pairs={{0,8},{4,12},{8,0},{12,4},{16,24},{20,28},{24,16},{28,20},{1,9},{5... | collective-permute-start | bytes 1572872 | tf_op jit(solution)/shard_map/ppermute | solution.py:62
  99.8 31.7 %collective-permute-start.17 = (bf16[256,2048]{1,0:T(8,128)(2,1)S(1)}, bf16[256,2048]{1,0:T(8,128)(2,1)S(1)}, u32[]{:S(2)}, u32[]{:S(2)}) collective-permute-start(bf16[256,2048]{1,0:T(8,128)(2,1)S(1)} %copy-done.20), channel_id=1, source_target_pairs={{0,8},{4,12},{8,0},{12,4},{16,24},{20,28},{24,16},{28,20},{1,9},{5... | collective-permute-start | bytes 3145736 | tf_op jit(solution)/shard_map/ppermute | solution.py:62
  101.0 30.5 %collective-permute-start.18 = (bf16[256,2048]{1,0:T(8,128)(2,1)S(1)}, bf16[256,2048]{1,0:T(8,128)(2,1)}, u32[]{:S(2)}, u32[]{:S(2)}) collective-permute-start(bf16[256,2048]{1,0:T(8,128)(2,1)S(1)} %copy-done.20), channel_id=1, source_target_pairs={{0,16},{4,20},{8,24},{12,28},{16,0},{20,4},{24,8},{28,12},{1,17},{... | collective-permute-start | bytes 3145736 | tf_op jit(solution)/shard_map/ppermute | solution.py:62
  136.1 51.5 %collective-permute-start.25 = (bf16[1024,2048]{1,0:T(8,128)(2,1)}, bf16[1024,2048]{1,0:T(8,128)(2,1)}, u32[]{:S(2)}, u32[]{:S(2)}) collective-permute-start(bf16[1024,2048]{1,0:T(8,128)(2,1)} %join.12.refs_0_.refs_2_), channel_id=1, source_target_pairs={{0,4},{4,0},{8,12},{12,8},{16,20},{20,16},{24,28},{28,24},{1,5},{5... | collective-permute-start | bytes 12582920 | tf_op jit(solution)/shard_map/ppermute | solution.py:62
  136.3 215.8 %reduce-scatter.4.cloned.1.call-start = ((), (), s32[]{:S(2)}) async-start(), calls=%async_computation.4 | async-start | bytes 2621440 | tf_op jit(solution)/shard_map/reduce_scatter | solution.py:1175
  138.8 26.0 %collective-permute-start.19 = (bf16[4,256,512]{2,1,0:T(8,128)(2,1)S(1)}, bf16[4,256,512]{2,1,0:T(8,128)(2,1)S(1)}, u32[]{:S(2)}, u32[]{:S(2)}) collective-permute-start(bf16[4,256,512]{2,1,0:T(8,128)(2,1)S(1)} %reshape.173.refs_0_), channel_id=1, source_target_pairs={{0,8},{4,12},{8,0},{12,4},{16,24},{20,28},{24,16},{28,20},{1,9},{5... | collective-permute-start | bytes 3145736 | tf_op jit(solution)/shard_map/ppermute | solution.py:62
  139.8 26.0 %collective-permute-start.21 = (bf16[4,256,512]{2,1,0:T(8,128)(2,1)S(1)}, bf16[4,256,512]{2,1,0:T(8,128)(2,1)S(1)}, u32[]{:S(2)}, u32[]{:S(2)}) collective-permute-start(bf16[4,256,512]{2,1,0:T(8,128)(2,1)S(1)} %reshape.173.refs_0_), channel_id=1, source_target_pairs={{0,16},{4,20},{8,24},{12,28},{16,0},{20,4},{24,8},{28,12},{1,17},{... | collective-permute-start | bytes 3145736 | tf_op jit(solution)/shard_map/ppermute | solution.py:62
  141.3 35.7 %collective-permute-start.23 = (bf16[128,2048]{1,0:T(8,128)(2,1)S(1)}, bf16[128,2048]{1,0:T(8,128)(2,1)S(1)}, u32[]{:S(2)}, u32[]{:S(2)}) collective-permute-start(bf16[128,2048]{1,0:T(8,128)(2,1)S(1)} %slice.107), channel_id=1, source_target_pairs={{0,16},{4,20},{8,24},{12,28},{16,0},{20,4},{24,8},{28,12},{1,17},{... | collective-permute-start | bytes 1572872 | tf_op jit(solution)/shard_map/ppermute | solution.py:62
  143.0 34.0 %collective-permute-start.24 = (bf16[128,2048]{1,0:T(8,128)(2,1)S(1)}, bf16[128,2048]{1,0:T(8,128)(2,1)}, u32[]{:S(2)}, u32[]{:S(2)}) collective-permute-start(bf16[128,2048]{1,0:T(8,128)(2,1)S(1)} %slice.108), channel_id=1, source_target_pairs={{0,8},{4,12},{8,0},{12,4},{16,24},{20,28},{24,16},{28,20},{1,9},{5... | collective-permute-start | bytes 1572872 | tf_op jit(solution)/shard_map/ppermute | solution.py:62
  164.8 22.8 %collective-permute-start.20 = (bf16[4,128,512]{2,1,0:T(8,128)(2,1)S(1)}, bf16[4,128,512]{2,1,0:T(8,128)(2,1)}, u32[]{:S(2)}, u32[]{:S(2)}) collective-permute-start(bf16[4,128,512]{2,1,0:T(8,128)(2,1)S(1)} %slice.132), channel_id=1, source_target_pairs={{0,16},{4,20},{8,24},{12,28},{16,0},{20,4},{24,8},{28,12},{1,17},{... | collective-permute-start | bytes 1572872 | tf_op jit(solution)/shard_map/ppermute | solution.py:62
  166.8 20.8 %collective-permute-start.22 = (bf16[4,128,512]{2,1,0:T(8,128)(2,1)S(1)}, bf16[4,128,512]{2,1,0:T(8,128)(2,1)}, u32[]{:S(2)}, u32[]{:S(2)}) collective-permute-start(bf16[4,128,512]{2,1,0:T(8,128)(2,1)S(1)} %slice.133), channel_id=1, source_target_pairs={{0,8},{4,12},{8,0},{12,4},{16,24},{20,28},{24,16},{28,20},{1,9},{5... | collective-permute-start | bytes 1572872 | tf_op jit(solution)/shard_map/ppermute | solution.py:62
  196.3 26.5 %collective-permute-start.29 = (bf16[1024,2048]{1,0:T(8,128)(2,1)}, bf16[1024,2048]{1,0:T(8,128)(2,1)}, u32[]{:S(2)}, u32[]{:S(2)}) collective-permute-start(bf16[1024,2048]{1,0:T(8,128)(2,1)} %join.14.refs_2_.refs_4_), channel_id=1, source_target_pairs={{0,4},{4,0},{8,12},{12,8},{16,20},{20,16},{24,28},{28,24},{1,5},{5... | collective-permute-start | bytes 12582920 | tf_op jit(solution)/shard_map/ppermute | solution.py:62
  196.8 25.2 %collective-permute-start.27 = (bf16[256,2048]{1,0:T(8,128)(2,1)S(1)}, bf16[256,2048]{1,0:T(8,128)(2,1)S(1)}, u32[]{:S(2)}, u32[]{:S(2)}) collective-permute-start(bf16[256,2048]{1,0:T(8,128)(2,1)S(1)} %copy-done.21), channel_id=1, source_target_pairs={{0,8},{4,12},{8,0},{12,4},{16,24},{20,28},{24,16},{28,20},{1,9},{5... | collective-permute-start | bytes 3145736 | tf_op jit(solution)/shard_map/ppermute | solution.py:62
  197.9 24.9 %collective-permute-start.28 = (bf16[256,2048]{1,0:T(8,128)(2,1)S(1)}, bf16[256,2048]{1,0:T(8,128)(2,1)S(1)}, u32[]{:S(2)}, u32[]{:S(2)}) collective-permute-start(bf16[256,2048]{1,0:T(8,128)(2,1)S(1)} %copy-done.21), channel_id=1, source_target_pairs={{0,16},{4,20},{8,24},{12,28},{16,0},{20,4},{24,8},{28,12},{1,17},{... | collective-permute-start | bytes 3145736 | tf_op jit(solution)/shard_map/ppermute | solution.py:62
  287.1 158.8 %reduce-scatter.6.cloned.1.call-start = ((), (), s32[]{:S(2)}) async-start(), calls=%async_computation.5 | async-start | bytes 2621440 | tf_op jit(solution)/shard_map/reduce_scatter | solution.py:1209
  300.0 14.2 %collective-permute-start.42 = (bf16[256,2048]{1,0:T(8,128)(2,1)}, bf16[256,2048]{1,0:T(8,128)(2,1)}, u32[]{:S(2)}, u32[]{:S(2)}) collective-permute-start(bf16[256,2048]{1,0:T(8,128)(2,1)} %get-tuple-element.260), channel_id=1, source_target_pairs={{0,4},{4,0},{8,12},{12,8},{16,20},{20,16},{24,28},{28,24},{1,5},{5... | collective-permute-start | bytes 3145736 | tf_op jit(solution)/shard_map/ppermute | solution.py:62
  306.4 16.8 %collective-permute-start.46 = (bf16[256,2048]{1,0:T(8,128)(2,1)}, bf16[256,2048]{1,0:T(8,128)(2,1)S(1)}, u32[]{:S(2)}, u32[]{:S(2)}) collective-permute-start(bf16[256,2048]{1,0:T(8,128)(2,1)} %get-tuple-element.269), channel_id=1, source_target_pairs={{0,4},{4,0},{8,12},{12,8},{16,20},{20,16},{24,28},{28,24},{1,5},{5... | collective-permute-start | bytes 3145736 | tf_op jit(solution)/shard_map/ppermute | solution.py:62
  306.6 17.7 %collective-permute-start.47 = (bf16[256,2048]{1,0:T(8,128)(2,1)}, bf16[256,2048]{1,0:T(8,128)(2,1)S(1)}, u32[]{:S(2)}, u32[]{:S(2)}) collective-permute-start(bf16[256,2048]{1,0:T(8,128)(2,1)} %get-tuple-element.270), channel_id=1, source_target_pairs={{0,4},{4,0},{8,12},{12,8},{16,20},{20,16},{24,28},{28,24},{1,5},{5... | collective-permute-start | bytes 3145736 | tf_op jit(solution)/shard_map/ppermute | solution.py:62
  306.9 18.2 %collective-permute-start.48 = (bf16[256,2048]{1,0:T(8,128)(2,1)}, bf16[256,2048]{1,0:T(8,128)(2,1)}, u32[]{:S(2)}, u32[]{:S(2)}) collective-permute-start(bf16[256,2048]{1,0:T(8,128)(2,1)} %get-tuple-element.271), channel_id=1, source_target_pairs={{0,4},{4,0},{8,12},{12,8},{16,20},{20,16},{24,28},{28,24},{1,5},{5... | collective-permute-start | bytes 3145736 | tf_op jit(solution)/shard_map/ppermute | solution.py:62
  314.2 18.9 %collective-permute-start.37 = (bf16[128,2048]{1,0:T(8,128)(2,1)}, bf16[128,2048]{1,0:T(8,128)(2,1)S(1)}, u32[]{:S(2)}, u32[]{:S(2)}) collective-permute-start(bf16[128,2048]{1,0:T(8,128)(2,1)} %get-tuple-element.252), channel_id=1, source_target_pairs={{0,16},{4,20},{8,24},{12,28},{16,0},{20,4},{24,8},{28,12},{1,17},{... | collective-permute-start | bytes 1572872 | tf_op jit(solution)/shard_map/ppermute | solution.py:62
  315.5 29.7 %collective-permute-start.38 = (bf16[128,2048]{1,0:T(8,128)(2,1)}, bf16[128,2048]{1,0:T(8,128)(2,1)}, u32[]{:S(2)}, u32[]{:S(2)}) collective-permute-start(bf16[128,2048]{1,0:T(8,128)(2,1)} %get-tuple-element.253), channel_id=1, source_target_pairs={{0,8},{4,12},{8,0},{12,4},{16,24},{20,28},{24,16},{28,20},{1,9},{5... | collective-permute-start | bytes 1572872 | tf_op jit(solution)/shard_map/ppermute | solution.py:62
  323.3 25.3 %collective-permute-start.43 = (bf16[128,2048]{1,0:T(8,128)(2,1)}, bf16[128,2048]{1,0:T(8,128)(2,1)}, u32[]{:S(2)}, u32[]{:S(2)}) collective-permute-start(bf16[128,2048]{1,0:T(8,128)(2,1)} %get-tuple-element.263), channel_id=1, source_target_pairs={{0,16},{4,20},{8,24},{12,28},{16,0},{20,4},{24,8},{28,12},{1,17},{... | collective-permute-start | bytes 1572872 | tf_op jit(solution)/shard_map/ppermute | solution.py:62
  324.3 24.2 %collective-permute-start.44 = (bf16[128,2048]{1,0:T(8,128)(2,1)}, bf16[128,2048]{1,0:T(8,128)(2,1)}, u32[]{:S(2)}, u32[]{:S(2)}) collective-permute-start(bf16[128,2048]{1,0:T(8,128)(2,1)} %get-tuple-element.264), channel_id=1, source_target_pairs={{0,8},{4,12},{8,0},{12,4},{16,24},{20,28},{24,16},{28,20},{1,9},{5... | collective-permute-start | bytes 1572872 | tf_op jit(solution)/shard_map/ppermute | solution.py:62
  332.0 19.9 %collective-permute-start.49 = (bf16[128,2048]{1,0:T(8,128)(2,1)}, bf16[128,2048]{1,0:T(8,128)(2,1)S(1)}, u32[]{:S(2)}, u32[]{:S(2)}) collective-permute-start(bf16[128,2048]{1,0:T(8,128)(2,1)} %get-tuple-element.272), channel_id=1, source_target_pairs={{0,16},{4,20},{8,24},{12,28},{16,0},{20,4},{24,8},{28,12},{1,17},{... | collective-permute-start | bytes 1572872 | tf_op jit(solution)/shard_map/ppermute | solution.py:62
  333.1 18.9 %collective-permute-start.50 = (bf16[128,2048]{1,0:T(8,128)(2,1)}, bf16[128,2048]{1,0:T(8,128)(2,1)S(1)}, u32[]{:S(2)}, u32[]{:S(2)}) collective-permute-start(bf16[128,2048]{1,0:T(8,128)(2,1)} %get-tuple-element.273), channel_id=1, source_target_pairs={{0,8},{4,12},{8,0},{12,4},{16,24},{20,28},{24,16},{28,20},{1,9},{5... | collective-permute-start | bytes 1572872 | tf_op jit(solution)/shard_map/ppermute | solution.py:62
  352.9 28.8 %collective-permute-start.54 = (bf16[256,2048]{1,0:T(8,128)(2,1)}, bf16[256,2048]{1,0:T(8,128)(2,1)S(1)}, u32[]{:S(2)}, u32[]{:S(2)}) collective-permute-start(bf16[256,2048]{1,0:T(8,128)(2,1)} %get-tuple-element.279), channel_id=1, source_target_pairs={{0,8},{4,12},{8,0},{12,4},{16,24},{20,28},{24,16},{28,20},{1,9},{5... | collective-permute-start | bytes 3145736 | tf_op jit(solution)/shard_map/ppermute | solution.py:62
  353.9 27.7 %collective-permute-start.55 = (bf16[256,2048]{1,0:T(8,128)(2,1)}, bf16[256,2048]{1,0:T(8,128)(2,1)}, u32[]{:S(2)}, u32[]{:S(2)}) collective-permute-start(bf16[256,2048]{1,0:T(8,128)(2,1)} %get-tuple-element.280), channel_id=1, source_target_pairs={{0,16},{4,20},{8,24},{12,28},{16,0},{20,4},{24,8},{28,12},{1,17},{... | collective-permute-start | bytes 3145736 | tf_op jit(solution)/shard_map/ppermute | solution.py:62
  381.7 166.3 %reduce-scatter.8.cloned.1.call-start = ((), (), s32[]{:S(2)}) async-start(), calls=%async_computation.6 | async-start | bytes 2621440 | tf_op jit(solution)/shard_map/reduce_scatter | solution.py:1225
  381.9 33.9 %collective-permute-start.56 = (bf16[256,2048]{1,0:T(8,128)(2,1)}, bf16[256,2048]{1,0:T(8,128)(2,1)S(1)}, u32[]{:S(2)}, u32[]{:S(2)}) collective-permute-start(bf16[256,2048]{1,0:T(8,128)(2,1)} %get-tuple-element.297), channel_id=1, source_target_pairs={{0,8},{4,12},{8,0},{12,4},{16,24},{20,28},{24,16},{28,20},{1,9},{5... | collective-permute-start | bytes 3145736 | tf_op jit(solution)/shard_map/ppermute | solution.py:62
  382.6 33.2 %collective-permute-start.57 = (bf16[256,2048]{1,0:T(8,128)(2,1)}, bf16[256,2048]{1,0:T(8,128)(2,1)S(1)}, u32[]{:S(2)}, u32[]{:S(2)}) collective-permute-start(bf16[256,2048]{1,0:T(8,128)(2,1)} %get-tuple-element.298), channel_id=1, source_target_pairs={{0,16},{4,20},{8,24},{12,28},{16,0},{20,4},{24,8},{28,12},{1,17},{... | collective-permute-start | bytes 3145736 | tf_op jit(solution)/shard_map/ppermute | solution.py:62
  431.2 14.6 %collective-permute-start.61 = (bf16[512,256]{1,0:T(8,128)(2,1)}, bf16[512,256]{1,0:T(8,128)(2,1)S(1)}, u32[]{:S(2)}, u32[]{:S(2)}) collective-permute-start(bf16[512,256]{1,0:T(8,128)(2,1)} %get-tuple-element.306), channel_id=1, source_target_pairs={{0,8},{4,12},{8,0},{12,4},{16,24},{20,28},{24,16},{28,20},{1,9},{5... | collective-permute-start | bytes 786440 | tf_op jit(solution)/shard_map/ppermute | solution.py:62
  460.7 14.0 %collective-permute-start.67 = (bf16[1024,768]{1,0:T(8,128)(2,1)}, bf16[1024,768]{1,0:T(8,128)(2,1)}, u32[]{:S(2)}, u32[]{:S(2)}) collective-permute-start(bf16[1024,768]{1,0:T(8,128)(2,1)} %gradient_part.14), channel_id=1, source_target_pairs={{0,4},{4,0},{8,12},{12,8},{16,20},{20,16},{24,28},{28,24},{1,5},{5... | collective-permute-start | bytes 4718600 | tf_op jit(solution)/shard_map/ppermute | solution.py:62
  460.8 25.9 %collective-permute-start.69 = (bf16[256,2048]{1,0:T(8,128)(2,1)}, bf16[256,2048]{1,0:T(8,128)(2,1)}, u32[]{:S(2)}, u32[]{:S(2)}) collective-permute-start(bf16[256,2048]{1,0:T(8,128)(2,1)} %get-tuple-element.334), channel_id=1, source_target_pairs={{0,8},{4,12},{8,0},{12,4},{16,24},{20,28},{24,16},{28,20},{1,9},{5... | collective-permute-start | bytes 3145736 | tf_op jit(solution)/shard_map/ppermute | solution.py:62
  461.7 25.5 %collective-permute-start.70 = (bf16[256,2048]{1,0:T(8,128)(2,1)}, bf16[256,2048]{1,0:T(8,128)(2,1)}, u32[]{:S(2)}, u32[]{:S(2)}) collective-permute-start(bf16[256,2048]{1,0:T(8,128)(2,1)} %get-tuple-element.335), channel_id=1, source_target_pairs={{0,16},{4,20},{8,24},{12,28},{16,0},{20,4},{24,8},{28,12},{1,17},{... | collective-permute-start | bytes 3145736 | tf_op jit(solution)/shard_map/ppermute | solution.py:62
  504.0 18.6 %collective-permute-start.77 = (bf16[256,768]{1,0:T(8,128)(2,1)}, bf16[256,768]{1,0:T(8,128)(2,1)S(1)}, u32[]{:S(2)}, u32[]{:S(2)}) collective-permute-start(bf16[256,768]{1,0:T(8,128)(2,1)} %get-tuple-element.368), channel_id=1, source_target_pairs={{0,8},{4,12},{8,0},{12,4},{16,24},{20,28},{24,16},{28,20},{1,9},{5... | collective-permute-start | bytes 1179656 | tf_op jit(solution)/shard_map/ppermute | solution.py:62
  505.2 17.5 %collective-permute-start.78 = (bf16[256,768]{1,0:T(8,128)(2,1)}, bf16[256,768]{1,0:T(8,128)(2,1)S(1)}, u32[]{:S(2)}, u32[]{:S(2)}) collective-permute-start(bf16[256,768]{1,0:T(8,128)(2,1)} %get-tuple-element.369), channel_id=1, source_target_pairs={{0,16},{4,20},{8,24},{12,28},{16,0},{20,4},{24,8},{28,12},{1,17},{... | collective-permute-start | bytes 1179656 | tf_op jit(solution)/shard_map/ppermute | solution.py:62
  507.1 15.5 %collective-permute-start.76 = (f32[1,2,256]{2,0,1:T(1,128)S(1)}, f32[1,2,256]{2,0,1:T(1,128)S(1)}, u32[]{:S(2)}, u32[]{:S(2)}) collective-permute-start(f32[1,2,256]{2,0,1:T(1,128)S(1)} %slice.125), channel_id=1, source_target_pairs={{0,8},{4,12},{8,0},{12,4},{16,24},{20,28},{24,16},{28,20},{1,9},{5... | collective-permute-start | bytes 6152 | tf_op jit(solution)/shard_map/ppermute | solution.py:62
  508.0 14.7 %collective-permute-start.79 = (bf16[256,512]{1,0:T(8,128)(2,1)S(1)}, bf16[256,512]{1,0:T(8,128)(2,1)S(1)}, u32[]{:S(2)}, u32[]{:S(2)}) collective-permute-start(bf16[256,512]{1,0:T(8,128)(2,1)S(1)} %copy-done.68), channel_id=1, source_target_pairs={{0,8},{4,12},{8,0},{12,4},{16,24},{20,28},{24,16},{28,20},{1,9},{5... | collective-permute-start | bytes 786440 | tf_op jit(solution)/shard_map/ppermute | solution.py:62
  528.2 18.9 %collective-permute-start.83 = (bf16[256,512]{1,0:T(8,128)(2,1)S(1)}, bf16[256,512]{1,0:T(8,128)(2,1)S(1)}, u32[]{:S(2)}, u32[]{:S(2)}) collective-permute-start(bf16[256,512]{1,0:T(8,128)(2,1)S(1)} %convert_element_type.47), channel_id=1, source_target_pairs={{0,0},{1,8},{2,16},{3,24},{4,4},{5,12},{6,20},{7,28},{8,1},{9,9},{... | collective-permute-start | bytes 786440 | tf_op jit(solution)/shard_map/ppermute | solution.py:958
  (113 other events, 1037.8 us)
Sparse Core Ops, SparseCore 0:
  9.6 47.1 all-gather.5
  61.7 64.9 all-gather.7
  136.4 46.6 all-gather.9
  287.2 44.5 reduce-scatter.3
  381.8 42.6 reduce-scatter.5
  457.1 44.4 reduce-scatter.7

commit v4 on v3

--- a/solution.py
+++ b/solution.py
@@ -1241,30 +1241,31 @@
     qkv_two = scatter_two(qkv_sum, scatter_one(qkv_sum, bits))
     o_two = scatter_two(o_sum, scatter_one(o_sum, bits))
     gain_sum = scatter_step(gain_sum, order[1], bits)
-    pieces = window(gain_sum, *qkv_two, *o_two, *gate_three, *down_three, *up_three, mlp_out)
-    (gain_sum,), qkv_two, o_two, gate_three, down_three, up_three, (mlp_out,) = cut(
-        pieces, 1, 2, 2, 2, 2, 2, 1
-    )
-
-    qkv_three, o_three = scatter_three(qkv_two, bits), scatter_three(o_two, bits)
     gain_sum = scatter_step(gain_sum, order[0], bits)
     (sum_down_w,) = finish_sum(down_sum, down_three)
-    (sum_up_w,) = finish_sum(up_sum, up_three)
-    gain_sum, sum_down_w, sum_up_w, *pieces = window(
-        gain_sum, sum_down_w, sum_up_w, *qkv_three, *o_three
-    )
-    qkv_three, o_three = cut(pieces, 2, 2)
-
-    (sum_o_w,) = finish_sum(o_sum, o_three)
-    sum_o_w = to_owners(sum_o_w.astype(jnp.bfloat16), (1 << bits) // shifts)
+    pieces = window(gain_sum, *qkv_two, *o_two, *gate_three, *up_three, mlp_out, sum_down_w)
+    (gain_sum,), qkv_two, o_two, gate_three, up_three, (mlp_out, sum_down_w) = cut(
+        pieces, 1, 2, 2, 2, 2, 2
+    )
+    gate_three, up_three = list(gate_three), list(up_three)
+
+    qkv_three, o_three = scatter_three(qkv_two, bits), scatter_three(o_two, bits)
     gain_here, shift = gain_sum[0], 1
     while shift < shifts:
         gain_here = sum_step(gain_here, shift, "tp")
         shift *= 2
+    (sum_up_w,) = finish_sum(up_sum, up_three)
+    input_grad = finish_input(place, grad_attn_in, grad_residual, rows_all, g_attn, bits)
+    gain_here, sum_up_w, input_grad, gate_three[0], *pieces = window(
+        gain_here, sum_up_w, input_grad, gate_three[0], *qkv_three, *o_three
+    )
+    qkv_three, o_three = cut(pieces, 2, 2)
+
+    (sum_o_w,) = finish_sum(o_sum, o_three)
+    sum_o_w = to_owners(sum_o_w.astype(jnp.bfloat16), (1 << bits) // shifts)
     (sum_gate_w,) = finish_sum(gate_sum, gate_three)
     block_out = (residual_here + mlp_out.astype(jnp.float32)).astype(jnp.bfloat16)
     block_out = reorder(place, block_out, bits, inverse=True)
-    input_grad = finish_input(place, grad_attn_in, grad_residual, rows_all, g_attn, bits)
     sum_q_w, sum_k_w, sum_v_w = finish_sum(qkv_sum, qkv_three, [width_q, width_k, width_k])
     return (
         block_out,

time: 568 us -> 561 us (0.988)
  waiting for transfers between devices: 163 us -> 152 us
    unnamed x144 -> x140, local copies, waits for them, and re-layouts: 14.5 us -> 15.7 us
  transfers between devices with their start and end apart: 90 -> 90, of which waited for: 31 -> 29; matrix products, arithmetic and copies ran while one was open for 5% -> 4% of each run, Pallas kernels for 35% -> 36%
where the time goes in v4:
time: 561 us; the launch traced here: 552 us
  Pallas kernels  261 us (47%)
  waiting for transfers between devices  152 us (27%)
  starting transfers between devices  81 us (14%)
  local copies, waits for them, and re-layouts  28.1 us (5%)
  between operations  15.5 us (3%)
  other arithmetic  13.8 us (2%)
    ppermute x75, waiting for transfers between devices, swap(): lax.ppermute(array, 'ctx', [(i, i ^ 1 << bit) for i in range(1 << bits)])  132 us
    ppermute x75, starting transfers between devices, swap(): lax.ppermute(array, 'ctx', [(i, i ^ 1 << bit) for i in range(1 << bits)])  62 us
    pallas_call x8, Pallas kernels, gradient_part(): pl.pallas_call(kernel, grid=(width // tile,), out_shape=[jax.ShapeDtypeSt...  44.9 us
    pallas_call x3, Pallas kernels, to_features(): pl.pallas_call(kernel, grid=(count * tiles,), out_shape=jax.ShapeDtypeStr...  34.4 us
    pallas_call x1, Pallas kernels, attend_backward(): pl.pallas_call(functools.partial(backward_kernel, bits, heads), out_shape...  30 us
    pallas_call x8, Pallas kernels, join(): pl.pallas_call(kernel, out_shape=jax.ShapeDtypeStruct(shape, pieces[0].dt...  26.8 us
    pallas_call x1, Pallas kernels, mlp_inner(): pl.pallas_call(functools.partial(mlp_kernel, count), grid=(units // tile,...  20.4 us
    pallas_call x1, Pallas kernels, attend_forward(): pl.pallas_call(functools.partial(forward_kernel, bits, heads), out_shape=...  18.9 us
  transfers between devices with their start and end apart: 90, of which 29 were waited for; matrix products, arithmetic and copies ran while one was open for 4% of the time, Pallas kernels for 36%

profile of v4, /device:TPU:2, one launch (start us, length us, event | category | flops | bytes accessed | tf_op | source)
XLA Modules:
  0.0 551.9 jit_solution(4130645438809188165)
XLA Ops:
  15.3 6.7 %collective-permute-done.3.refs_1_ = bf16[256,768]{1,0:T(8,128)(2,1)S(1)} collective-permute-done((bf16[256,768]{1,0:T(8,128)(2,1)}, bf16[256,768]{1,0:T(8,128)(2,1)S(1)}, u32[]{:S(2)}, u32[]{:S(2)}) %collective-permute-start.3) | collective-permute-done | bytes 393248 | tf_op jit(solution)/shard_map/ppermute | solution.py:62
  24.2 23.4 %collective-permute-done.5.refs_3_ = bf16[128,768]{1,0:T(8,128)(2,1)S(1)} collective-permute-done((bf16[128,768]{1,0:T(8,128)(2,1)S(1)}, bf16[128,768]{1,0:T(8,128)(2,1)S(1)}, u32[]{:S(2)}, u32[]{:S(2)}) %collective-permute-start.5) | collective-permute-done | bytes 196640 | tf_op jit(solution)/shard_map/ppermute | solution.py:62
  64.2 4.0 norm_rows.1
  68.2 5.9 %qkv.1 = (bf16[512,512]{1,0:T(8,128)(2,1)}, bf16[512,256]{1,0:T(8,128)(2,1)}) custom-call(bf16[512,2048]{1,0:T(8,128)(2,1)} %get-tuple-element.201.x_ref.left_ref, bf16[1024,768]{1,0:T(8,128)(2,1)} %join.9.refs_0_.refs_1_, bf16[1024,768]{1,0:T(8,128)(2,1)} %copy-done.4, f32[512,128]{1,0:T(8,128)} %copy.23.refs_2_.refs_5_.cos_ref, ...), custom_call_target="tpu_custom_call" | custom-call | flops 110000000 | bytes 1024 | tf_op jit(solution)/shard_map/qkv/pallas_call | solution.py:405
  77.5 5.3 collective-permute-done.10.refs_1_
  101.8 18.9 %attention_forward.1 = (bf16[512,512]{1,0:T(8,128)(2,1)}, f32[512,512]{1,0:T(8,128)}, f32[8,512]{1,0:T(8,128)}) custom-call(s32[8]{0:T(128)} %slots.3, s32[2]{0:T(128)} %pad_add_fusion.place, bf16[512,512]{1,0:T(8,128)(2,1)} %get-tuple-element.206.q_ref.refs_0_, bf16[4096,256]{1,0:T(8,128)(2,1)} %join.11.kv_ref.refs_1_), custom_call_target="tpu_custom_call" | custom-call | flops 20899999744 | bytes 1024 | tf_op jit(solution)/shard_map/attention_forward/pallas_call | solution.py:517
  120.7 10.9 %collective-permute-done.17.refs_1_ = bf16[256,2048]{1,0:T(8,128)(2,1)S(1)} collective-permute-done((bf16[256,2048]{1,0:T(8,128)(2,1)S(1)}, bf16[256,2048]{1,0:T(8,128)(2,1)S(1)}, u32[]{:S(2)}, u32[]{:S(2)}) %collective-permute-start.17) | collective-permute-done | bytes 1048608 | tf_op jit(solution)/shard_map/ppermute | solution.py:62
  131.6 4.6 join.12.refs_0_.refs_2_
  144.2 20.6 %collective-permute-done.19.refs_1_ = bf16[4,256,512]{2,1,0:T(8,128)(2,1)S(1)} collective-permute-done((bf16[4,256,512]{2,1,0:T(8,128)(2,1)S(1)}, bf16[4,256,512]{2,1,0:T(8,128)(2,1)S(1)}, u32[]{:S(2)}, u32[]{:S(2)}) %collective-permute-start.19) | collective-permute-done | bytes 1048608 | tf_op jit(solution)/shard_map/ppermute | solution.py:62
  169.9 7.1 %collective-permute-done.23.refs_3_ = bf16[128,2048]{1,0:T(8,128)(2,1)S(1)} collective-permute-done((bf16[128,2048]{1,0:T(8,128)(2,1)S(1)}, bf16[128,2048]{1,0:T(8,128)(2,1)S(1)}, u32[]{:S(2)}, u32[]{:S(2)}) %collective-permute-start.23) | collective-permute-done | bytes 524320 | tf_op jit(solution)/shard_map/ppermute | solution.py:62
  177.0 10.6 %collective-permute-done.20.refs_3_ = bf16[4,128,512]{2,1,0:T(8,128)(2,1)} collective-permute-done((bf16[4,128,512]{2,1,0:T(8,128)(2,1)S(1)}, bf16[4,128,512]{2,1,0:T(8,128)(2,1)}, u32[]{:S(2)}, u32[]{:S(2)}) %collective-permute-start.20) | collective-permute-done | bytes 524320 | tf_op jit(solution)/shard_map/ppermute | solution.py:62
  187.7 4.3 join.13.part_ref.refs_0_
  192.0 4.3 join.14.refs_2_.refs_4_
  198.7 6.5 %project_part.1.refs_0_ = f32[512,1024]{1,0:T(8,128)} custom-call(bf16[4,512,512]{2,1,0:T(8,128)(2,1)} %bitcast.45, bf16[4,1024,512]{2,1,0:T(8,128)(2,1)} %join.13.part_ref.refs_0_), custom_call_target="tpu_custom_call" | custom-call | flops 110000000 | bytes 1024 | tf_op jit(solution)/shard_map/project_part/pallas_call | solution.py:725
  207.3 9.8 %project_residual.1 = (bf16[512,2048]{1,0:T(8,128)(2,1)}, f32[128,2048]{1,0:T(8,128)}) custom-call(s32[2]{0:T(128)} %pad_add_fusion.place, bf16[4,512,512]{2,1,0:T(8,128)(2,1)} %bitcast.46, bf16[512,2048]{1,0:T(8,128)(2,1)} %get-tuple-element.224.x_ref.rows_ref, f32[1,2048]{1,0:T(1,128)} %get-tuple-element.399.gain_ref, bf16[4,1024,512]{2,1,0:T(8,128)(2,1)} %copy-done.2, ...), custom_call_target="tpu_custom_call" | custom-call | flops 110000000 | bytes 1024 | tf_op jit(solution)/shard_map/project_residual/pallas_call | solution.py:792
  217.1 4.9 collective-permute-done.27.refs_1_
  225.5 10.3 %collective-permute-done.30.refs_3_ = bf16[128,2048]{1,0:T(8,128)(2,1)S(1)} collective-permute-done((bf16[128,2048]{1,0:T(8,128)(2,1)S(1)}, bf16[128,2048]{1,0:T(8,128)(2,1)S(1)}, u32[]{:S(2)}, u32[]{:S(2)}) %collective-permute-start.30) | collective-permute-done | bytes 524320 | tf_op jit(solution)/shard_map/ppermute | solution.py:62
  237.3 4.3 join.15.refs_4_.refs_1_
  241.7 7.4 %collective-permute-done.32.refs_5_.refs_2_ = bf16[1024,2048]{1,0:T(8,128)(2,1)S(1)} collective-permute-done((bf16[1024,2048]{1,0:T(8,128)(2,1)}, bf16[1024,2048]{1,0:T(8,128)(2,1)S(1)}, u32[]{:S(2)}, u32[]{:S(2)}) %collective-permute-start.32) | collective-permute-done | bytes 4194336 | tf_op jit(solution)/shard_map/ppermute | solution.py:62
  251.0 20.4 %mlp_inner.1 = (bf16[512,2048]{1,0:T(8,128)(2,1)}, bf16[512,2048]{1,0:T(8,128)(2,1)}, bf16[512,2048]{1,0:T(8,128)(2,1)}) custom-call(bf16[512,2048]{1,0:T(8,128)(2,1)} %get-tuple-element.233.x_ref.left_ref, bf16[512,2048]{1,0:T(8,128)(2,1)} %bitcast.42, bf16[1024,2048]{1,0:T(8,128)(2,1)} %join.12.refs_0_.refs_2_, ...), custom_call_target="tpu_custom_call" | custom-call | flops 110000000 | bytes 1024 | tf_op jit(solution)/shard_map/mlp_inner/pallas_call | solution.py:702
  271.4 15.8 %to_features.3 = bf16[512,2048]{1,0:T(8,128)(2,1)} custom-call(bf16[512,2048]{1,0:T(8,128)(2,1)} %get-tuple-element.267.refs_0_.right_ref, bf16[512,2048]{1,0:T(8,128)(2,1)} %get-tuple-element.256.refs_1_.right_ref, bf16[1024,2048]{1,0:T(8,128)(2,1)} %join.12.refs_0_.refs_2_, bf16[1024,2048]{1,0:T(8,128)(2,1)} %collective-permute-done.25.refs_1_.refs_3_, ...), custom_call_target="tpu_custom_call" | custom-call | flops 110000000 | bytes 1024 | tf_op jit(solution)/shard_map/to_features/pallas_call | solution.py:840
  287.4 5.4 gradient_part.8
  293.8 5.6 %gradient_part.10 = (bf16[256,2048]{1,0:T(8,128)(2,1)}, bf16[256,2048]{1,0:T(8,128)(2,1)}, bf16[256,2048]{1,0:T(8,128)(2,1)}, bf16[256,2048]{1,0:T(8,128)(2,1)}) custom-call(bf16[512,2048]{1,0:T(8,128)(2,1)} %get-tuple-element.233.x_ref.left_ref, bf16[512,2048]{1,0:T(8,128)(2,1)} %get-tuple-element.256.refs_1_.right_ref), custom_call_target="tpu_custom_call" | custom-call | flops 110000000 | bytes 1024 | tf_op jit(solution)/shard_map/gradient_part/pallas_call | solution.py:986
  300.5 5.6 %gradient_part.12 = (bf16[256,2048]{1,0:T(8,128)(2,1)}, bf16[256,2048]{1,0:T(8,128)(2,1)}, bf16[256,2048]{1,0:T(8,128)(2,1)}, bf16[256,2048]{1,0:T(8,128)(2,1)}) custom-call(bf16[512,2048]{1,0:T(8,128)(2,1)} %get-tuple-element.233.x_ref.left_ref, bf16[512,2048]{1,0:T(8,128)(2,1)} %get-tuple-element.267.refs_0_.right_ref), custom_call_target="tpu_custom_call" | custom-call | flops 110000000 | bytes 1024 | tf_op jit(solution)/shard_map/gradient_part/pallas_call | solution.py:986
  307.3 7.1 %gradient_part.9 = (bf16[256,2048]{1,0:T(8,128)(2,1)}, bf16[256,2048]{1,0:T(8,128)(2,1)}, bf16[256,2048]{1,0:T(8,128)(2,1)}, bf16[128,2048]{1,0:T(8,128)(2,1)}, bf16[128,2048]{1,0:T(8,128)(2,1)}) custom-call(bf16[512,2048]{1,0:T(8,128)(2,1)} %bitcast.44, bf16[512,2048]{1,0:T(8,128)(2,1)} %get-tuple-element.245.refs_0_.right_ref, ...), custom_call_target="tpu_custom_call" | custom-call | flops 110000000 | bytes 1024 | tf_op jit(solution)/shard_map/gradient_part/pallas_call | solution.py:986
  316.7 6.8 %gradient_part.11 = (bf16[256,2048]{1,0:T(8,128)(2,1)}, bf16[256,2048]{1,0:T(8,128)(2,1)}, bf16[256,2048]{1,0:T(8,128)(2,1)}, bf16[128,2048]{1,0:T(8,128)(2,1)}, bf16[128,2048]{1,0:T(8,128)(2,1)}) custom-call(bf16[512,2048]{1,0:T(8,128)(2,1)} %get-tuple-element.233.x_ref.left_ref, bf16[512,2048]{1,0:T(8,128)(2,1)} %get-tuple-element.256.refs_1_.right_ref, ...), custom_call_target="tpu_custom_call" | custom-call | flops 110000000 | bytes 1024 | tf_op jit(solution)/shard_map/gradient_part/pallas_call | solution.py:986
  325.6 6.7 %gradient_part.13 = (bf16[256,2048]{1,0:T(8,128)(2,1)}, bf16[256,2048]{1,0:T(8,128)(2,1)}, bf16[256,2048]{1,0:T(8,128)(2,1)}, bf16[128,2048]{1,0:T(8,128)(2,1)}, bf16[128,2048]{1,0:T(8,128)(2,1)}) custom-call(bf16[512,2048]{1,0:T(8,128)(2,1)} %get-tuple-element.233.x_ref.left_ref, bf16[512,2048]{1,0:T(8,128)(2,1)} %get-tuple-element.267.refs_0_.right_ref, ...), custom_call_target="tpu_custom_call" | custom-call | flops 110000000 | bytes 1024 | tf_op jit(solution)/shard_map/gradient_part/pallas_call | solution.py:986
  334.6 10.9 %to_features.4 = bf16[512,2048]{1,0:T(8,128)(2,1)} custom-call(bf16[512,2048]{1,0:T(8,128)(2,1)} %get-tuple-element.245.refs_0_.right_ref, bf16[1024,2048]{1,0:T(8,128)(2,1)} %join.15.refs_4_.refs_1_, bf16[1024,2048]{1,0:T(8,128)(2,1)} %copy-done.1), custom_call_target="tpu_custom_call" | custom-call | flops 110000000 | bytes 1024 | tf_op jit(solution)/shard_map/to_features/pallas_call | solution.py:840
  345.4 3.3 scatter_two.6
  348.8 3.4 scatter_two.7
  359.1 6.3 %to_groups.1 = bf16[4,128,512]{2,1,0:T(8,128)(2,1)} custom-call(s32[2]{0:T(128)} %pad_add_fusion.place, bf16[128,2048]{1,0:T(8,128)(2,1)} %get-tuple-element.294.x_ref.in_ref, bf16[4,1024,512]{2,1,0:T(8,128)(2,1)} %join.13.part_ref.refs_0_, bf16[4,1024,512]{2,1,0:T(8,128)(2,1)} %copy-done.2), custom_call_target="tpu_custom_call" | custom-call | flops 110000000 | bytes 1024 | tf_op jit(solution)/shard_map/to_groups/pallas_call | solution.py:873
  366.6 3.6 collective-permute-start.53
  371.2 3.3 scatter_two.8
  374.5 6.4 %collective-permute-done.52 = bf16[128,512]{1,0:T(8,128)(2,1)S(1)} collective-permute-done((bf16[128,512]{1,0:T(8,128)(2,1)S(1)}, bf16[128,512]{1,0:T(8,128)(2,1)S(1)}, u32[]{:S(2)}, u32[]{:S(2)}) %collective-permute-start.52) | collective-permute-done | bytes 131104 | tf_op jit(solution)/shard_map/ppermute | solution.py:207
  384.1 30.0 %attention_backward.1 = (bf16[512,512]{1,0:T(8,128)(2,1)}, bf16[2048,256]{1,0:T(8,128)(2,1)}, bf16[2048,256]{1,0:T(8,128)(2,1)}) custom-call(s32[8]{0:T(128)} %slots.3, s32[2]{0:T(128)} %pad_add_fusion.place, bf16[512,512]{1,0:T(8,128)(2,1)} %get-tuple-element.206.q_ref.refs_0_, bf16[4096,256]{1,0:T(8,128)(2,1)} %join.11.kv_ref.refs_1_, ...), custom_call_target="tpu_custom_call" | custom-call | flops 32999999488 | bytes 1024 | tf_op jit(solution)/shard_map/attention_backward/pallas_call | solution.py:625
  424.6 3.6 collective-permute-done.59.lower_ref
  439.2 3.4 collective-permute-done.63.refs_1_
  449.3 7.7 %to_features.5 = bf16[512,2048]{1,0:T(8,128)(2,1)} custom-call(bf16[512,768]{1,0:T(8,128)(2,1)} %grad_qkv.1.refs_0_.right_ref, bf16[1024,768]{1,0:T(8,128)(2,1)} %join.9.refs_0_.refs_1_, bf16[1024,768]{1,0:T(8,128)(2,1)} %copy-done.4), custom_call_target="tpu_custom_call" | custom-call | flops 110000000 | bytes 1024 | tf_op jit(solution)/shard_map/to_features/pallas_call | solution.py:840
  457.1 3.7 gradient_part.14
  462.6 5.4 gradient_out.1
  474.9 4.0 gradient_part.15
  478.9 7.8 %collective-permute-done.69.first_ref = bf16[256,2048]{1,0:T(8,128)(2,1)} collective-permute-done((bf16[256,2048]{1,0:T(8,128)(2,1)}, bf16[256,2048]{1,0:T(8,128)(2,1)}, u32[]{:S(2)}, u32[]{:S(2)}) %collective-permute-start.69) | collective-permute-done | bytes 1048608 | tf_op jit(solution)/shard_map/ppermute | solution.py:62
  493.6 3.5 finish_sum.5
  514.4 3.5 finish_sum.6
  518.0 3.6 finish_input.1
  525.6 4.4 collective-permute-start.83
  535.0 3.5 finish_sum.9
  539.1 4.7 collective-permute-done.83
  (386 shorter events, 167.2 us)
Async XLA Ops:
  7.2 54.3 %all-gather.6.cloned.1.call-start = ((), (), s32[]{:S(2)}) async-start(), calls=%async_computation.3 | async-start | bytes 2621440 | tf_op jit(solution)/shard_map/all_gather | solution.py:1114
  7.9 123.6 %all-gather.8.cloned.1.call-start = ((), (), s32[]{:S(2)}) async-start(), calls=%async_computation.7 | async-start | bytes 3932160 | tf_op jit(solution)/shard_map/all_gather | solution.py:1133
  11.8 49.6 %collective-permute-start.8 = (bf16[256,2048]{1,0:T(8,128)(2,1)}, bf16[256,2048]{1,0:T(8,128)(2,1)S(1)}, u32[]{:S(2)}, u32[]{:S(2)}) collective-permute-start(bf16[256,2048]{1,0:T(8,128)(2,1)} %refs_0_.3), channel_id=1, source_target_pairs={{0,8},{4,12},{8,0},{12,4},{16,24},{20,28},{24,16},{28,20},{1,9},{5... | collective-permute-start | bytes 3145736 | tf_op jit(solution)/shard_map/ppermute | solution.py:62
  13.3 48.1 %collective-permute-start.9 = (bf16[256,2048]{1,0:T(8,128)(2,1)}, bf16[256,2048]{1,0:T(8,128)(2,1)}, u32[]{:S(2)}, u32[]{:S(2)}) collective-permute-start(bf16[256,2048]{1,0:T(8,128)(2,1)} %refs_0_.3), channel_id=1, source_target_pairs={{0,16},{4,20},{8,24},{12,28},{16,0},{20,4},{24,8},{28,12},{1,17},{... | collective-permute-start | bytes 3145736 | tf_op jit(solution)/shard_map/ppermute | solution.py:62
  15.2 41.3 %collective-permute-start = (bf16[1,2,256]{2,1,0:T(2,128)(2,1)S(1)}, bf16[1,2,256]{2,1,0:T(2,128)(2,1)S(1)}, u32[]{:S(2)}, u32[]{:S(2)}) collective-permute-start(bf16[1,2,256]{2,1,0:T(2,128)(2,1)S(1)} %maximum_bitcast_fusion.1), channel_id=1, source_target_pairs={{0,8},{4,12},{8,0},{12,4},{16,24},{20,28},{24,16},{28,20},{1,9},{5... | collective-permute-start | bytes 3080 | tf_op jit(solution)/shard_map/ppermute | solution.py:62
  22.0 25.6 %collective-permute-start.5 = (bf16[128,768]{1,0:T(8,128)(2,1)S(1)}, bf16[128,768]{1,0:T(8,128)(2,1)S(1)}, u32[]{:S(2)}, u32[]{:S(2)}) collective-permute-start(bf16[128,768]{1,0:T(8,128)(2,1)S(1)} %slice.128), channel_id=1, source_target_pairs={{0,16},{4,20},{8,24},{12,28},{16,0},{20,4},{24,8},{28,12},{1,17},{... | collective-permute-start | bytes 589832 | tf_op jit(solution)/shard_map/ppermute | solution.py:62
  23.6 24.0 %collective-permute-start.6 = (bf16[128,768]{1,0:T(8,128)(2,1)S(1)}, bf16[128,768]{1,0:T(8,128)(2,1)S(1)}, u32[]{:S(2)}, u32[]{:S(2)}) collective-permute-start(bf16[128,768]{1,0:T(8,128)(2,1)S(1)} %slice.129), channel_id=1, source_target_pairs={{0,8},{4,12},{8,0},{12,4},{16,24},{20,28},{24,16},{28,20},{1,9},{5... | collective-permute-start | bytes 589832 | tf_op jit(solution)/shard_map/ppermute | solution.py:62
  61.6 126.1 %all-gather.10.cloned.1.call-start = ((), (), s32[]{:S(2)}) async-start(), calls=%async_computation.8 | async-start | bytes 2621440 | tf_op jit(solution)/shard_map/all_gather | solution.py:1148
  92.5 28.1 %collective-permute-start.15 = (bf16[128,2048]{1,0:T(8,128)(2,1)S(1)}, bf16[128,2048]{1,0:T(8,128)(2,1)S(1)}, u32[]{:S(2)}, u32[]{:S(2)}) collective-permute-start(bf16[128,2048]{1,0:T(8,128)(2,1)S(1)} %slice.101), channel_id=1, source_target_pairs={{0,16},{4,20},{8,24},{12,28},{16,0},{20,4},{24,8},{28,12},{1,17},{... | collective-permute-start | bytes 1572872 | tf_op jit(solution)/shard_map/ppermute | solution.py:62
  95.0 25.7 %collective-permute-start.16 = (bf16[128,2048]{1,0:T(8,128)(2,1)S(1)}, bf16[128,2048]{1,0:T(8,128)(2,1)S(1)}, u32[]{:S(2)}, u32[]{:S(2)}) collective-permute-start(bf16[128,2048]{1,0:T(8,128)(2,1)S(1)} %slice.102), channel_id=1, source_target_pairs={{0,8},{4,12},{8,0},{12,4},{16,24},{20,28},{24,16},{28,20},{1,9},{5... | collective-permute-start | bytes 1572872 | tf_op jit(solution)/shard_map/ppermute | solution.py:62
  99.9 31.7 %collective-permute-start.17 = (bf16[256,2048]{1,0:T(8,128)(2,1)S(1)}, bf16[256,2048]{1,0:T(8,128)(2,1)S(1)}, u32[]{:S(2)}, u32[]{:S(2)}) collective-permute-start(bf16[256,2048]{1,0:T(8,128)(2,1)S(1)} %copy-done.20), channel_id=1, source_target_pairs={{0,8},{4,12},{8,0},{12,4},{16,24},{20,28},{24,16},{28,20},{1,9},{5... | collective-permute-start | bytes 3145736 | tf_op jit(solution)/shard_map/ppermute | solution.py:62
  101.0 30.5 %collective-permute-start.18 = (bf16[256,2048]{1,0:T(8,128)(2,1)S(1)}, bf16[256,2048]{1,0:T(8,128)(2,1)}, u32[]{:S(2)}, u32[]{:S(2)}) collective-permute-start(bf16[256,2048]{1,0:T(8,128)(2,1)S(1)} %copy-done.20), channel_id=1, source_target_pairs={{0,16},{4,20},{8,24},{12,28},{16,0},{20,4},{24,8},{28,12},{1,17},{... | collective-permute-start | bytes 3145736 | tf_op jit(solution)/shard_map/ppermute | solution.py:62
  136.2 51.5 %collective-permute-start.25 = (bf16[1024,2048]{1,0:T(8,128)(2,1)}, bf16[1024,2048]{1,0:T(8,128)(2,1)}, u32[]{:S(2)}, u32[]{:S(2)}) collective-permute-start(bf16[1024,2048]{1,0:T(8,128)(2,1)} %join.12.refs_0_.refs_2_), channel_id=1, source_target_pairs={{0,4},{4,0},{8,12},{12,8},{16,20},{20,16},{24,28},{28,24},{1,5},{5... | collective-permute-start | bytes 12582920 | tf_op jit(solution)/shard_map/ppermute | solution.py:62
  136.3 215.9 %reduce-scatter.4.cloned.1.call-start = ((), (), s32[]{:S(2)}) async-start(), calls=%async_computation.4 | async-start | bytes 2621440 | tf_op jit(solution)/shard_map/reduce_scatter | solution.py:1175
  138.8 26.0 %collective-permute-start.19 = (bf16[4,256,512]{2,1,0:T(8,128)(2,1)S(1)}, bf16[4,256,512]{2,1,0:T(8,128)(2,1)S(1)}, u32[]{:S(2)}, u32[]{:S(2)}) collective-permute-start(bf16[4,256,512]{2,1,0:T(8,128)(2,1)S(1)} %reshape.173.refs_0_), channel_id=1, source_target_pairs={{0,8},{4,12},{8,0},{12,4},{16,24},{20,28},{24,16},{28,20},{1,9},{5... | collective-permute-start | bytes 3145736 | tf_op jit(solution)/shard_map/ppermute | solution.py:62
  139.8 26.0 %collective-permute-start.21 = (bf16[4,256,512]{2,1,0:T(8,128)(2,1)S(1)}, bf16[4,256,512]{2,1,0:T(8,128)(2,1)S(1)}, u32[]{:S(2)}, u32[]{:S(2)}) collective-permute-start(bf16[4,256,512]{2,1,0:T(8,128)(2,1)S(1)} %reshape.173.refs_0_), channel_id=1, source_target_pairs={{0,16},{4,20},{8,24},{12,28},{16,0},{20,4},{24,8},{28,12},{1,17},{... | collective-permute-start | bytes 3145736 | tf_op jit(solution)/shard_map/ppermute | solution.py:62
  141.3 35.7 %collective-permute-start.23 = (bf16[128,2048]{1,0:T(8,128)(2,1)S(1)}, bf16[128,2048]{1,0:T(8,128)(2,1)S(1)}, u32[]{:S(2)}, u32[]{:S(2)}) collective-permute-start(bf16[128,2048]{1,0:T(8,128)(2,1)S(1)} %slice.107), channel_id=1, source_target_pairs={{0,16},{4,20},{8,24},{12,28},{16,0},{20,4},{24,8},{28,12},{1,17},{... | collective-permute-start | bytes 1572872 | tf_op jit(solution)/shard_map/ppermute | solution.py:62
  143.0 34.0 %collective-permute-start.24 = (bf16[128,2048]{1,0:T(8,128)(2,1)S(1)}, bf16[128,2048]{1,0:T(8,128)(2,1)}, u32[]{:S(2)}, u32[]{:S(2)}) collective-permute-start(bf16[128,2048]{1,0:T(8,128)(2,1)S(1)} %slice.108), channel_id=1, source_target_pairs={{0,8},{4,12},{8,0},{12,4},{16,24},{20,28},{24,16},{28,20},{1,9},{5... | collective-permute-start | bytes 1572872 | tf_op jit(solution)/shard_map/ppermute | solution.py:62
  164.9 22.8 %collective-permute-start.20 = (bf16[4,128,512]{2,1,0:T(8,128)(2,1)S(1)}, bf16[4,128,512]{2,1,0:T(8,128)(2,1)}, u32[]{:S(2)}, u32[]{:S(2)}) collective-permute-start(bf16[4,128,512]{2,1,0:T(8,128)(2,1)S(1)} %slice.132), channel_id=1, source_target_pairs={{0,16},{4,20},{8,24},{12,28},{16,0},{20,4},{24,8},{28,12},{1,17},{... | collective-permute-start | bytes 1572872 | tf_op jit(solution)/shard_map/ppermute | solution.py:62
  166.8 20.8 %collective-permute-start.22 = (bf16[4,128,512]{2,1,0:T(8,128)(2,1)S(1)}, bf16[4,128,512]{2,1,0:T(8,128)(2,1)}, u32[]{:S(2)}, u32[]{:S(2)}) collective-permute-start(bf16[4,128,512]{2,1,0:T(8,128)(2,1)S(1)} %slice.133), channel_id=1, source_target_pairs={{0,8},{4,12},{8,0},{12,4},{16,24},{20,28},{24,16},{28,20},{1,9},{5... | collective-permute-start | bytes 1572872 | tf_op jit(solution)/shard_map/ppermute | solution.py:62
  196.4 26.5 %collective-permute-start.29 = (bf16[1024,2048]{1,0:T(8,128)(2,1)}, bf16[1024,2048]{1,0:T(8,128)(2,1)}, u32[]{:S(2)}, u32[]{:S(2)}) collective-permute-start(bf16[1024,2048]{1,0:T(8,128)(2,1)} %join.14.refs_2_.refs_4_), channel_id=1, source_target_pairs={{0,4},{4,0},{8,12},{12,8},{16,20},{20,16},{24,28},{28,24},{1,5},{5... | collective-permute-start | bytes 12582920 | tf_op jit(solution)/shard_map/ppermute | solution.py:62
  196.9 25.2 %collective-permute-start.27 = (bf16[256,2048]{1,0:T(8,128)(2,1)S(1)}, bf16[256,2048]{1,0:T(8,128)(2,1)S(1)}, u32[]{:S(2)}, u32[]{:S(2)}) collective-permute-start(bf16[256,2048]{1,0:T(8,128)(2,1)S(1)} %copy-done.21), channel_id=1, source_target_pairs={{0,8},{4,12},{8,0},{12,4},{16,24},{20,28},{24,16},{28,20},{1,9},{5... | collective-permute-start | bytes 3145736 | tf_op jit(solution)/shard_map/ppermute | solution.py:62
  198.0 24.9 %collective-permute-start.28 = (bf16[256,2048]{1,0:T(8,128)(2,1)S(1)}, bf16[256,2048]{1,0:T(8,128)(2,1)S(1)}, u32[]{:S(2)}, u32[]{:S(2)}) collective-permute-start(bf16[256,2048]{1,0:T(8,128)(2,1)S(1)} %copy-done.21), channel_id=1, source_target_pairs={{0,16},{4,20},{8,24},{12,28},{16,0},{20,4},{24,8},{28,12},{1,17},{... | collective-permute-start | bytes 3145736 | tf_op jit(solution)/shard_map/ppermute | solution.py:62
  287.2 158.7 %reduce-scatter.6.cloned.1.call-start = ((), (), s32[]{:S(2)}) async-start(), calls=%async_computation.5 | async-start | bytes 2621440 | tf_op jit(solution)/shard_map/reduce_scatter | solution.py:1209
  300.2 14.3 %collective-permute-start.42 = (bf16[256,2048]{1,0:T(8,128)(2,1)}, bf16[256,2048]{1,0:T(8,128)(2,1)}, u32[]{:S(2)}, u32[]{:S(2)}) collective-permute-start(bf16[256,2048]{1,0:T(8,128)(2,1)} %get-tuple-element.260), channel_id=1, source_target_pairs={{0,4},{4,0},{8,12},{12,8},{16,20},{20,16},{24,28},{28,24},{1,5},{5... | collective-permute-start | bytes 3145736 | tf_op jit(solution)/shard_map/ppermute | solution.py:62
  306.6 17.0 %collective-permute-start.46 = (bf16[256,2048]{1,0:T(8,128)(2,1)}, bf16[256,2048]{1,0:T(8,128)(2,1)S(1)}, u32[]{:S(2)}, u32[]{:S(2)}) collective-permute-start(bf16[256,2048]{1,0:T(8,128)(2,1)} %get-tuple-element.269), channel_id=1, source_target_pairs={{0,4},{4,0},{8,12},{12,8},{16,20},{20,16},{24,28},{28,24},{1,5},{5... | collective-permute-start | bytes 3145736 | tf_op jit(solution)/shard_map/ppermute | solution.py:62
  306.7 17.9 %collective-permute-start.47 = (bf16[256,2048]{1,0:T(8,128)(2,1)}, bf16[256,2048]{1,0:T(8,128)(2,1)S(1)}, u32[]{:S(2)}, u32[]{:S(2)}) collective-permute-start(bf16[256,2048]{1,0:T(8,128)(2,1)} %get-tuple-element.270), channel_id=1, source_target_pairs={{0,4},{4,0},{8,12},{12,8},{16,20},{20,16},{24,28},{28,24},{1,5},{5... | collective-permute-start | bytes 3145736 | tf_op jit(solution)/shard_map/ppermute | solution.py:62
  307.1 18.4 %collective-permute-start.48 = (bf16[256,2048]{1,0:T(8,128)(2,1)}, bf16[256,2048]{1,0:T(8,128)(2,1)}, u32[]{:S(2)}, u32[]{:S(2)}) collective-permute-start(bf16[256,2048]{1,0:T(8,128)(2,1)} %get-tuple-element.271), channel_id=1, source_target_pairs={{0,4},{4,0},{8,12},{12,8},{16,20},{20,16},{24,28},{28,24},{1,5},{5... | collective-permute-start | bytes 3145736 | tf_op jit(solution)/shard_map/ppermute | solution.py:62
  314.4 18.9 %collective-permute-start.37 = (bf16[128,2048]{1,0:T(8,128)(2,1)}, bf16[128,2048]{1,0:T(8,128)(2,1)S(1)}, u32[]{:S(2)}, u32[]{:S(2)}) collective-permute-start(bf16[128,2048]{1,0:T(8,128)(2,1)} %get-tuple-element.252), channel_id=1, source_target_pairs={{0,16},{4,20},{8,24},{12,28},{16,0},{20,4},{24,8},{28,12},{1,17},{... | collective-permute-start | bytes 1572872 | tf_op jit(solution)/shard_map/ppermute | solution.py:62
  315.7 29.7 %collective-permute-start.38 = (bf16[128,2048]{1,0:T(8,128)(2,1)}, bf16[128,2048]{1,0:T(8,128)(2,1)}, u32[]{:S(2)}, u32[]{:S(2)}) collective-permute-start(bf16[128,2048]{1,0:T(8,128)(2,1)} %get-tuple-element.253), channel_id=1, source_target_pairs={{0,8},{4,12},{8,0},{12,4},{16,24},{20,28},{24,16},{28,20},{1,9},{5... | collective-permute-start | bytes 1572872 | tf_op jit(solution)/shard_map/ppermute | solution.py:62
  323.6 25.2 %collective-permute-start.43 = (bf16[128,2048]{1,0:T(8,128)(2,1)}, bf16[128,2048]{1,0:T(8,128)(2,1)}, u32[]{:S(2)}, u32[]{:S(2)}) collective-permute-start(bf16[128,2048]{1,0:T(8,128)(2,1)} %get-tuple-element.263), channel_id=1, source_target_pairs={{0,16},{4,20},{8,24},{12,28},{16,0},{20,4},{24,8},{28,12},{1,17},{... | collective-permute-start | bytes 1572872 | tf_op jit(solution)/shard_map/ppermute | solution.py:62
  324.6 24.2 %collective-permute-start.44 = (bf16[128,2048]{1,0:T(8,128)(2,1)}, bf16[128,2048]{1,0:T(8,128)(2,1)}, u32[]{:S(2)}, u32[]{:S(2)}) collective-permute-start(bf16[128,2048]{1,0:T(8,128)(2,1)} %get-tuple-element.264), channel_id=1, source_target_pairs={{0,8},{4,12},{8,0},{12,4},{16,24},{20,28},{24,16},{28,20},{1,9},{5... | collective-permute-start | bytes 1572872 | tf_op jit(solution)/shard_map/ppermute | solution.py:62
  332.3 19.9 %collective-permute-start.49 = (bf16[128,2048]{1,0:T(8,128)(2,1)}, bf16[128,2048]{1,0:T(8,128)(2,1)S(1)}, u32[]{:S(2)}, u32[]{:S(2)}) collective-permute-start(bf16[128,2048]{1,0:T(8,128)(2,1)} %get-tuple-element.272), channel_id=1, source_target_pairs={{0,16},{4,20},{8,24},{12,28},{16,0},{20,4},{24,8},{28,12},{1,17},{... | collective-permute-start | bytes 1572872 | tf_op jit(solution)/shard_map/ppermute | solution.py:62
  333.4 18.8 %collective-permute-start.50 = (bf16[128,2048]{1,0:T(8,128)(2,1)}, bf16[128,2048]{1,0:T(8,128)(2,1)S(1)}, u32[]{:S(2)}, u32[]{:S(2)}) collective-permute-start(bf16[128,2048]{1,0:T(8,128)(2,1)} %get-tuple-element.273), channel_id=1, source_target_pairs={{0,8},{4,12},{8,0},{12,4},{16,24},{20,28},{24,16},{28,20},{1,9},{5... | collective-permute-start | bytes 1572872 | tf_op jit(solution)/shard_map/ppermute | solution.py:62
  353.0 28.8 %collective-permute-start.54 = (bf16[256,2048]{1,0:T(8,128)(2,1)}, bf16[256,2048]{1,0:T(8,128)(2,1)S(1)}, u32[]{:S(2)}, u32[]{:S(2)}) collective-permute-start(bf16[256,2048]{1,0:T(8,128)(2,1)} %get-tuple-element.279), channel_id=1, source_target_pairs={{0,8},{4,12},{8,0},{12,4},{16,24},{20,28},{24,16},{28,20},{1,9},{5... | collective-permute-start | bytes 3145736 | tf_op jit(solution)/shard_map/ppermute | solution.py:62
  354.1 27.7 %collective-permute-start.55 = (bf16[256,2048]{1,0:T(8,128)(2,1)}, bf16[256,2048]{1,0:T(8,128)(2,1)}, u32[]{:S(2)}, u32[]{:S(2)}) collective-permute-start(bf16[256,2048]{1,0:T(8,128)(2,1)} %get-tuple-element.280), channel_id=1, source_target_pairs={{0,16},{4,20},{8,24},{12,28},{16,0},{20,4},{24,8},{28,12},{1,17},{... | collective-permute-start | bytes 3145736 | tf_op jit(solution)/shard_map/ppermute | solution.py:62
  381.8 136.1 %reduce-scatter.8.cloned.1.call-start = ((), (), s32[]{:S(2)}) async-start(), calls=%async_computation.6 | async-start | bytes 2621440 | tf_op jit(solution)/shard_map/reduce_scatter | solution.py:1225
  382.1 33.9 %collective-permute-start.56 = (bf16[256,2048]{1,0:T(8,128)(2,1)}, bf16[256,2048]{1,0:T(8,128)(2,1)S(1)}, u32[]{:S(2)}, u32[]{:S(2)}) collective-permute-start(bf16[256,2048]{1,0:T(8,128)(2,1)} %get-tuple-element.297), channel_id=1, source_target_pairs={{0,8},{4,12},{8,0},{12,4},{16,24},{20,28},{24,16},{28,20},{1,9},{5... | collective-permute-start | bytes 3145736 | tf_op jit(solution)/shard_map/ppermute | solution.py:62
  382.9 33.1 %collective-permute-start.57 = (bf16[256,2048]{1,0:T(8,128)(2,1)}, bf16[256,2048]{1,0:T(8,128)(2,1)S(1)}, u32[]{:S(2)}, u32[]{:S(2)}) collective-permute-start(bf16[256,2048]{1,0:T(8,128)(2,1)} %get-tuple-element.298), channel_id=1, source_target_pairs={{0,16},{4,20},{8,24},{12,28},{16,0},{20,4},{24,8},{28,12},{1,17},{... | collective-permute-start | bytes 3145736 | tf_op jit(solution)/shard_map/ppermute | solution.py:62
  431.4 14.5 %collective-permute-start.61 = (bf16[512,256]{1,0:T(8,128)(2,1)}, bf16[512,256]{1,0:T(8,128)(2,1)S(1)}, u32[]{:S(2)}, u32[]{:S(2)}) collective-permute-start(bf16[512,256]{1,0:T(8,128)(2,1)} %get-tuple-element.306), channel_id=1, source_target_pairs={{0,8},{4,12},{8,0},{12,4},{16,24},{20,28},{24,16},{28,20},{1,9},{5... | collective-permute-start | bytes 786440 | tf_op jit(solution)/shard_map/ppermute | solution.py:62
  460.8 14.2 %collective-permute-start.67 = (bf16[1024,768]{1,0:T(8,128)(2,1)}, bf16[1024,768]{1,0:T(8,128)(2,1)}, u32[]{:S(2)}, u32[]{:S(2)}) collective-permute-start(bf16[1024,768]{1,0:T(8,128)(2,1)} %gradient_part.14), channel_id=1, source_target_pairs={{0,4},{4,0},{8,12},{12,8},{16,20},{20,16},{24,28},{28,24},{1,5},{5... | collective-permute-start | bytes 4718600 | tf_op jit(solution)/shard_map/ppermute | solution.py:62
  460.8 25.9 %collective-permute-start.69 = (bf16[256,2048]{1,0:T(8,128)(2,1)}, bf16[256,2048]{1,0:T(8,128)(2,1)}, u32[]{:S(2)}, u32[]{:S(2)}) collective-permute-start(bf16[256,2048]{1,0:T(8,128)(2,1)} %get-tuple-element.334), channel_id=1, source_target_pairs={{0,8},{4,12},{8,0},{12,4},{16,24},{20,28},{24,16},{28,20},{1,9},{5... | collective-permute-start | bytes 3145736 | tf_op jit(solution)/shard_map/ppermute | solution.py:62
  461.8 25.5 %collective-permute-start.70 = (bf16[256,2048]{1,0:T(8,128)(2,1)}, bf16[256,2048]{1,0:T(8,128)(2,1)}, u32[]{:S(2)}, u32[]{:S(2)}) collective-permute-start(bf16[256,2048]{1,0:T(8,128)(2,1)} %get-tuple-element.335), channel_id=1, source_target_pairs={{0,16},{4,20},{8,24},{12,28},{16,0},{20,4},{24,8},{28,12},{1,17},{... | collective-permute-start | bytes 3145736 | tf_op jit(solution)/shard_map/ppermute | solution.py:62
  504.8 16.8 %collective-permute-start.79 = (bf16[256,768]{1,0:T(8,128)(2,1)}, bf16[256,768]{1,0:T(8,128)(2,1)S(1)}, u32[]{:S(2)}, u32[]{:S(2)}) collective-permute-start(bf16[256,768]{1,0:T(8,128)(2,1)} %get-tuple-element.367), channel_id=1, source_target_pairs={{0,8},{4,12},{8,0},{12,4},{16,24},{20,28},{24,16},{28,20},{1,9},{5... | collective-permute-start | bytes 1179656 | tf_op jit(solution)/shard_map/ppermute | solution.py:62
  505.9 15.7 %collective-permute-start.80 = (bf16[256,768]{1,0:T(8,128)(2,1)}, bf16[256,768]{1,0:T(8,128)(2,1)S(1)}, u32[]{:S(2)}, u32[]{:S(2)}) collective-permute-start(bf16[256,768]{1,0:T(8,128)(2,1)} %get-tuple-element.368), channel_id=1, source_target_pairs={{0,16},{4,20},{8,24},{12,28},{16,0},{20,4},{24,8},{28,12},{1,17},{... | collective-permute-start | bytes 1179656 | tf_op jit(solution)/shard_map/ppermute | solution.py:62
  506.9 14.6 %collective-permute-start.81 = (bf16[256,512]{1,0:T(8,128)(2,1)}, bf16[256,512]{1,0:T(8,128)(2,1)S(1)}, u32[]{:S(2)}, u32[]{:S(2)}) collective-permute-start(bf16[256,512]{1,0:T(8,128)(2,1)} %get-tuple-element.369), channel_id=1, source_target_pairs={{0,8},{4,12},{8,0},{12,4},{16,24},{20,28},{24,16},{28,20},{1,9},{5... | collective-permute-start | bytes 786440 | tf_op jit(solution)/shard_map/ppermute | solution.py:62
  507.6 14.0 %collective-permute-start.82 = (bf16[256,512]{1,0:T(8,128)(2,1)}, bf16[256,512]{1,0:T(8,128)(2,1)S(1)}, u32[]{:S(2)}, u32[]{:S(2)}) collective-permute-start(bf16[256,512]{1,0:T(8,128)(2,1)} %get-tuple-element.370), channel_id=1, source_target_pairs={{0,16},{4,20},{8,24},{12,28},{16,0},{20,4},{24,8},{28,12},{1,17},{... | collective-permute-start | bytes 786440 | tf_op jit(solution)/shard_map/ppermute | solution.py:62
  525.6 18.2 %collective-permute-start.83 = (bf16[256,512]{1,0:T(8,128)(2,1)S(1)}, bf16[256,512]{1,0:T(8,128)(2,1)S(1)}, u32[]{:S(2)}, u32[]{:S(2)}) collective-permute-start(bf16[256,512]{1,0:T(8,128)(2,1)S(1)} %convert_element_type.47), channel_id=1, source_target_pairs={{0,0},{1,8},{2,16},{3,24},{4,4},{5,12},{6,20},{7,28},{8,1},{9,9},{... | collective-permute-start | bytes 786440 | tf_op jit(solution)/shard_map/ppermute | solution.py:958
  (111 other events, 980.8 us)
Sparse Core Ops, SparseCore 0:
  9.6 47.1 all-gather.5
  61.7 64.9 all-gather.7
  136.4 46.6 all-gather.9
  287.3 44.5 reduce-scatter.3
  382.0 42.6 reduce-scatter.5
  457.2 44.4 reduce-scatter.7

commit v5 on v4

--- a/solution.py
+++ b/solution.py
@@ -84,27 +84,37 @@
 def join(pieces, axis=0):
     shape = list(pieces[0].shape)
     shape[axis] = sum(piece.shape[axis] for piece in pieces)
+    count = len(pieces)
 
     def kernel(*refs):
-        in_refs, out_ref, sems = refs[: len(pieces)], refs[len(pieces)], refs[-1]
-        copies, start = [], 0
+        in_refs, out_ref, buffer, in_sems, out_sems = refs[:count], *refs[count:]
+        brought, sent, start = [], [], 0
         for index, in_ref in enumerate(in_refs):
             size = in_ref.shape[axis]
-            place = pl.ds(start, size)
-            target = out_ref.at[(slice(None),) * axis + (place,)]
-            copies.append(pltpu.make_async_copy(in_ref, target, sems.at[index]))
+            here = (slice(None),) * axis + (pl.ds(start, size),)
+            brought.append(pltpu.make_async_copy(in_ref, buffer.at[here], in_sems.at[index]))
+            sent.append(
+                pltpu.make_async_copy(buffer.at[here], out_ref.at[here], out_sems.at[index])
+            )
             start += size
-        for copy in copies:
+        for copy in brought:
             copy.start()
-        for copy in copies:
+        for bring, send in zip(brought, sent):
+            bring.wait()
+            send.start()
+        for copy in sent:
             copy.wait()
 
     return pl.pallas_call(
         kernel,
         out_shape=jax.ShapeDtypeStruct(shape, pieces[0].dtype),
-        in_specs=[unread] * len(pieces),
-        out_specs=in_vmem,
-        scratch_shapes=[pltpu.SemaphoreType.DMA((len(pieces),))],
+        in_specs=[unread] * count,
+        out_specs=unread,
+        scratch_shapes=[
+            pltpu.VMEM(tuple(shape), pieces[0].dtype),
+            pltpu.SemaphoreType.DMA((count,)),
+            pltpu.SemaphoreType.DMA((count,)),
+        ],
         compiler_params=kernel_params(),
         cost_estimate=cost(0.1),
         name="join",
@@ -1158,11 +1168,13 @@
     o_two, up_two, gate_w = cut(pieces, 2, 2, count)
 
     down_one = gather_one(w_down, bits)
-    up_w = gather_end(w_up, up_one, up_two, bits)
     o_w = gather_end(wo_groups, o_one, o_two, bits, 1)
     mlp_in, residual_here = project_residual(place, attended_all, rows_all, g_mlp, o_w)
-    mlp_in, residual_here, *pieces = window(mlp_in, residual_here, *down_one, *up_w)
-    down_one, up_w = cut(pieces, 2, count)
+    mlp_in, residual_here, *pieces = window(
+        mlp_in, residual_here, *down_one, *up_one, *up_two
+    )
+    down_one, up_one, up_two = cut(pieces, 2, 2, 2)
+    up_w = gather_end(w_up, up_one, up_two, bits)
     down_two = gather_two(down_one, bits)
     down_w = gather_end(w_down, down_one, down_two, bits)
     factor_mlp = rms_scale(residual_here)

time: 561 us -> 554 us (0.988)
  transfers between devices with their start and end apart: 90 -> 90, of which waited for: 29 -> 29; matrix products, arithmetic and copies ran while one was open for 4% -> 4% of each run, Pallas kernels for 36% -> 37%
where the time goes in v5:
time: 554 us; the launch traced here: 545 us
  Pallas kernels  257 us (46%)
  waiting for transfers between devices  150 us (27%)
  starting transfers between devices  80.6 us (15%)
  local copies, waits for them, and re-layouts  28.1 us (5%)
  between operations  15.5 us (3%)
  other arithmetic  13.8 us (2%)
    ppermute x75, waiting for transfers between devices, swap(): lax.ppermute(array, 'ctx', [(i, i ^ 1 << bit) for i in range(1 << bits)])  130 us
    ppermute x75, starting transfers between devices, swap(): lax.ppermute(array, 'ctx', [(i, i ^ 1 << bit) for i in range(1 << bits)])  61.6 us
    pallas_call x8, Pallas kernels, gradient_part(): pl.pallas_call(kernel, grid=(width // tile,), out_shape=[jax.ShapeDtypeSt...  44.9 us
    pallas_call x3, Pallas kernels, to_features(): pl.pallas_call(kernel, grid=(count * tiles,), out_shape=jax.ShapeDtypeStr...  34.4 us
    pallas_call x1, Pallas kernels, attend_backward(): pl.pallas_call(functools.partial(backward_kernel, bits, heads), out_shape...  30 us
    pallas_call x8, Pallas kernels, join(): pl.pallas_call(kernel, out_shape=jax.ShapeDtypeStruct(shape, pieces[0].dt...  22.5 us
    pallas_call x1, Pallas kernels, mlp_inner(): pl.pallas_call(functools.partial(mlp_kernel, count), grid=(units // tile,...  20.4 us
    pallas_call x1, Pallas kernels, attend_forward(): pl.pallas_call(functools.partial(forward_kernel, bits, heads), out_shape=...  18.9 us
  transfers between devices with their start and end apart: 90, of which 29 were waited for; matrix products, arithmetic and copies ran while one was open for 4% of the time, Pallas kernels for 37%

profile of v5, /device:TPU:2, one launch (start us, length us, event | category | flops | bytes accessed | tf_op | source)
XLA Modules:
  0.0 544.9 jit_solution(6597456585613024260)
XLA Ops:
  15.3 6.7 %collective-permute-done.3.refs_1_ = bf16[256,768]{1,0:T(8,128)(2,1)S(1)} collective-permute-done((bf16[256,768]{1,0:T(8,128)(2,1)}, bf16[256,768]{1,0:T(8,128)(2,1)S(1)}, u32[]{:S(2)}, u32[]{:S(2)}) %collective-permute-start.3) | collective-permute-done | bytes 393248 | tf_op jit(solution)/shard_map/ppermute | solution.py:62
  24.2 23.4 %collective-permute-done.5.refs_3_ = bf16[128,768]{1,0:T(8,128)(2,1)S(1)} collective-permute-done((bf16[128,768]{1,0:T(8,128)(2,1)S(1)}, bf16[128,768]{1,0:T(8,128)(2,1)S(1)}, u32[]{:S(2)}, u32[]{:S(2)}) %collective-permute-start.5) | collective-permute-done | bytes 196640 | tf_op jit(solution)/shard_map/ppermute | solution.py:62
  63.9 4.0 norm_rows.1
  67.9 5.9 %qkv.1 = (bf16[512,512]{1,0:T(8,128)(2,1)}, bf16[512,256]{1,0:T(8,128)(2,1)}) custom-call(bf16[512,2048]{1,0:T(8,128)(2,1)} %get-tuple-element.203.x_ref.left_ref, bf16[1024,768]{1,0:T(8,128)(2,1)} %join.9.refs_0_.refs_1_, bf16[1024,768]{1,0:T(8,128)(2,1)} %copy-done.4, f32[512,128]{1,0:T(8,128)} %copy.23.refs_2_.refs_5_.cos_ref, ...), custom_call_target="tpu_custom_call" | custom-call | flops 110000000 | bytes 1024 | tf_op jit(solution)/shard_map/qkv/pallas_call | solution.py:415
  77.2 5.3 collective-permute-done.10.refs_1_
  101.0 18.9 %attention_forward.1 = (bf16[512,512]{1,0:T(8,128)(2,1)}, f32[512,512]{1,0:T(8,128)}, f32[8,512]{1,0:T(8,128)}) custom-call(s32[8]{0:T(128)} %slots.3, s32[2]{0:T(128)} %pad_add_fusion.place, bf16[512,512]{1,0:T(8,128)(2,1)} %get-tuple-element.208.q_ref.refs_0_, bf16[4096,256]{1,0:T(8,128)(2,1)} %join.11.kv_ref.refs_1_), custom_call_target="tpu_custom_call" | custom-call | flops 20899999744 | bytes 1024 | tf_op jit(solution)/shard_map/attention_forward/pallas_call | solution.py:527
  119.9 11.2 %collective-permute-done.17.refs_1_ = bf16[256,2048]{1,0:T(8,128)(2,1)S(1)} collective-permute-done((bf16[256,2048]{1,0:T(8,128)(2,1)S(1)}, bf16[256,2048]{1,0:T(8,128)(2,1)S(1)}, u32[]{:S(2)}, u32[]{:S(2)}) %collective-permute-start.17) | collective-permute-done | bytes 1048608 | tf_op jit(solution)/shard_map/ppermute | solution.py:62
  131.1 3.7 join.12.refs_0_.refs_2_
  142.8 20.6 %collective-permute-done.19.refs_1_ = bf16[4,256,512]{2,1,0:T(8,128)(2,1)S(1)} collective-permute-done((bf16[4,256,512]{2,1,0:T(8,128)(2,1)S(1)}, bf16[4,256,512]{2,1,0:T(8,128)(2,1)S(1)}, u32[]{:S(2)}, u32[]{:S(2)}) %collective-permute-start.19) | collective-permute-done | bytes 1048608 | tf_op jit(solution)/shard_map/ppermute | solution.py:62
  168.6 7.1 %collective-permute-done.23.refs_3_ = bf16[128,2048]{1,0:T(8,128)(2,1)S(1)} collective-permute-done((bf16[128,2048]{1,0:T(8,128)(2,1)S(1)}, bf16[128,2048]{1,0:T(8,128)(2,1)S(1)}, u32[]{:S(2)}, u32[]{:S(2)}) %collective-permute-start.23) | collective-permute-done | bytes 524320 | tf_op jit(solution)/shard_map/ppermute | solution.py:62
  175.7 10.6 %collective-permute-done.20.refs_3_ = bf16[4,128,512]{2,1,0:T(8,128)(2,1)} collective-permute-done((bf16[4,128,512]{2,1,0:T(8,128)(2,1)S(1)}, bf16[4,128,512]{2,1,0:T(8,128)(2,1)}, u32[]{:S(2)}, u32[]{:S(2)}) %collective-permute-start.20) | collective-permute-done | bytes 524320 | tf_op jit(solution)/shard_map/ppermute | solution.py:62
  186.3 3.5 join.13.part_ref.refs_0_
  191.8 6.5 %project_part.1.refs_0_ = f32[512,1024]{1,0:T(8,128)} custom-call(bf16[4,512,512]{2,1,0:T(8,128)(2,1)} %bitcast.45, bf16[4,1024,512]{2,1,0:T(8,128)(2,1)} %join.13.part_ref.refs_0_), custom_call_target="tpu_custom_call" | custom-call | flops 110000000 | bytes 1024 | tf_op jit(solution)/shard_map/project_part/pallas_call | solution.py:735
  200.4 9.7 %project_residual.1 = (bf16[512,2048]{1,0:T(8,128)(2,1)}, f32[128,2048]{1,0:T(8,128)}) custom-call(s32[2]{0:T(128)} %pad_add_fusion.place, bf16[4,512,512]{2,1,0:T(8,128)(2,1)} %bitcast.46, bf16[512,2048]{1,0:T(8,128)(2,1)} %get-tuple-element.226.x_ref.rows_ref, f32[1,2048]{1,0:T(1,128)} %get-tuple-element.403.gain_ref, bf16[4,1024,512]{2,1,0:T(8,128)(2,1)} %copy-done.2, ...), custom_call_target="tpu_custom_call" | custom-call | flops 110000000 | bytes 1024 | tf_op jit(solution)/shard_map/project_residual/pallas_call | solution.py:802
  210.2 5.3 collective-permute-done.27.refs_1_
  218.9 3.4 join.14.refs_2_.refs_4_
  222.4 7.2 %collective-permute-done.30.refs_3_ = bf16[128,2048]{1,0:T(8,128)(2,1)S(1)} collective-permute-done((bf16[128,2048]{1,0:T(8,128)(2,1)S(1)}, bf16[128,2048]{1,0:T(8,128)(2,1)S(1)}, u32[]{:S(2)}, u32[]{:S(2)}) %collective-permute-start.30) | collective-permute-done | bytes 524320 | tf_op jit(solution)/shard_map/ppermute | solution.py:62
  231.2 3.4 join.15.refs_4_.refs_1_
  234.6 7.3 %collective-permute-done.32.refs_5_.refs_2_ = bf16[1024,2048]{1,0:T(8,128)(2,1)S(1)} collective-permute-done((bf16[1024,2048]{1,0:T(8,128)(2,1)}, bf16[1024,2048]{1,0:T(8,128)(2,1)S(1)}, u32[]{:S(2)}, u32[]{:S(2)}) %collective-permute-start.32) | collective-permute-done | bytes 4194336 | tf_op jit(solution)/shard_map/ppermute | solution.py:62
  244.0 20.4 %mlp_inner.1 = (bf16[512,2048]{1,0:T(8,128)(2,1)}, bf16[512,2048]{1,0:T(8,128)(2,1)}, bf16[512,2048]{1,0:T(8,128)(2,1)}) custom-call(bf16[512,2048]{1,0:T(8,128)(2,1)} %get-tuple-element.235.x_ref.left_ref, bf16[512,2048]{1,0:T(8,128)(2,1)} %bitcast.42, bf16[1024,2048]{1,0:T(8,128)(2,1)} %join.12.refs_0_.refs_2_, ...), custom_call_target="tpu_custom_call" | custom-call | flops 110000000 | bytes 1024 | tf_op jit(solution)/shard_map/mlp_inner/pallas_call | solution.py:712
  264.4 15.8 %to_features.3 = bf16[512,2048]{1,0:T(8,128)(2,1)} custom-call(bf16[512,2048]{1,0:T(8,128)(2,1)} %get-tuple-element.271.refs_0_.right_ref, bf16[512,2048]{1,0:T(8,128)(2,1)} %get-tuple-element.260.refs_1_.right_ref, bf16[1024,2048]{1,0:T(8,128)(2,1)} %join.12.refs_0_.refs_2_, bf16[1024,2048]{1,0:T(8,128)(2,1)} %collective-permute-done.25.refs_1_.refs_3_, ...), custom_call_target="tpu_custom_call" | custom-call | flops 110000000 | bytes 1024 | tf_op jit(solution)/shard_map/to_features/pallas_call | solution.py:850
  280.4 5.4 gradient_part.8
  286.8 5.6 %gradient_part.10 = (bf16[256,2048]{1,0:T(8,128)(2,1)}, bf16[256,2048]{1,0:T(8,128)(2,1)}, bf16[256,2048]{1,0:T(8,128)(2,1)}, bf16[256,2048]{1,0:T(8,128)(2,1)}) custom-call(bf16[512,2048]{1,0:T(8,128)(2,1)} %get-tuple-element.235.x_ref.left_ref, bf16[512,2048]{1,0:T(8,128)(2,1)} %get-tuple-element.260.refs_1_.right_ref), custom_call_target="tpu_custom_call" | custom-call | flops 110000000 | bytes 1024 | tf_op jit(solution)/shard_map/gradient_part/pallas_call | solution.py:996
  293.5 5.6 %gradient_part.12 = (bf16[256,2048]{1,0:T(8,128)(2,1)}, bf16[256,2048]{1,0:T(8,128)(2,1)}, bf16[256,2048]{1,0:T(8,128)(2,1)}, bf16[256,2048]{1,0:T(8,128)(2,1)}) custom-call(bf16[512,2048]{1,0:T(8,128)(2,1)} %get-tuple-element.235.x_ref.left_ref, bf16[512,2048]{1,0:T(8,128)(2,1)} %get-tuple-element.271.refs_0_.right_ref), custom_call_target="tpu_custom_call" | custom-call | flops 110000000 | bytes 1024 | tf_op jit(solution)/shard_map/gradient_part/pallas_call | solution.py:996
  300.2 7.1 %gradient_part.9 = (bf16[256,2048]{1,0:T(8,128)(2,1)}, bf16[256,2048]{1,0:T(8,128)(2,1)}, bf16[256,2048]{1,0:T(8,128)(2,1)}, bf16[128,2048]{1,0:T(8,128)(2,1)}, bf16[128,2048]{1,0:T(8,128)(2,1)}) custom-call(bf16[512,2048]{1,0:T(8,128)(2,1)} %bitcast.44, bf16[512,2048]{1,0:T(8,128)(2,1)} %get-tuple-element.249.refs_0_.right_ref, ...), custom_call_target="tpu_custom_call" | custom-call | flops 110000000 | bytes 1024 | tf_op jit(solution)/shard_map/gradient_part/pallas_call | solution.py:996
  309.7 6.8 %gradient_part.11 = (bf16[256,2048]{1,0:T(8,128)(2,1)}, bf16[256,2048]{1,0:T(8,128)(2,1)}, bf16[256,2048]{1,0:T(8,128)(2,1)}, bf16[128,2048]{1,0:T(8,128)(2,1)}, bf16[128,2048]{1,0:T(8,128)(2,1)}) custom-call(bf16[512,2048]{1,0:T(8,128)(2,1)} %get-tuple-element.235.x_ref.left_ref, bf16[512,2048]{1,0:T(8,128)(2,1)} %get-tuple-element.260.refs_1_.right_ref, ...), custom_call_target="tpu_custom_call" | custom-call | flops 110000000 | bytes 1024 | tf_op jit(solution)/shard_map/gradient_part/pallas_call | solution.py:996
  318.5 6.7 %gradient_part.13 = (bf16[256,2048]{1,0:T(8,128)(2,1)}, bf16[256,2048]{1,0:T(8,128)(2,1)}, bf16[256,2048]{1,0:T(8,128)(2,1)}, bf16[128,2048]{1,0:T(8,128)(2,1)}, bf16[128,2048]{1,0:T(8,128)(2,1)}) custom-call(bf16[512,2048]{1,0:T(8,128)(2,1)} %get-tuple-element.235.x_ref.left_ref, bf16[512,2048]{1,0:T(8,128)(2,1)} %get-tuple-element.271.refs_0_.right_ref, ...), custom_call_target="tpu_custom_call" | custom-call | flops 110000000 | bytes 1024 | tf_op jit(solution)/shard_map/gradient_part/pallas_call | solution.py:996
  327.5 10.9 %to_features.4 = bf16[512,2048]{1,0:T(8,128)(2,1)} custom-call(bf16[512,2048]{1,0:T(8,128)(2,1)} %get-tuple-element.249.refs_0_.right_ref, bf16[1024,2048]{1,0:T(8,128)(2,1)} %join.15.refs_4_.refs_1_, bf16[1024,2048]{1,0:T(8,128)(2,1)} %copy-done.1), custom_call_target="tpu_custom_call" | custom-call | flops 110000000 | bytes 1024 | tf_op jit(solution)/shard_map/to_features/pallas_call | solution.py:850
  338.4 3.3 scatter_two.6
  341.8 3.4 scatter_two.7
  352.0 6.3 %to_groups.1 = bf16[4,128,512]{2,1,0:T(8,128)(2,1)} custom-call(s32[2]{0:T(128)} %pad_add_fusion.place, bf16[128,2048]{1,0:T(8,128)(2,1)} %get-tuple-element.298.x_ref.in_ref, bf16[4,1024,512]{2,1,0:T(8,128)(2,1)} %join.13.part_ref.refs_0_, bf16[4,1024,512]{2,1,0:T(8,128)(2,1)} %copy-done.2), custom_call_target="tpu_custom_call" | custom-call | flops 110000000 | bytes 1024 | tf_op jit(solution)/shard_map/to_groups/pallas_call | solution.py:883
  359.5 3.7 collective-permute-start.53
  364.1 3.3 scatter_two.8
  367.5 6.4 %collective-permute-done.52 = bf16[128,512]{1,0:T(8,128)(2,1)S(1)} collective-permute-done((bf16[128,512]{1,0:T(8,128)(2,1)S(1)}, bf16[128,512]{1,0:T(8,128)(2,1)S(1)}, u32[]{:S(2)}, u32[]{:S(2)}) %collective-permute-start.52) | collective-permute-done | bytes 131104 | tf_op jit(solution)/shard_map/ppermute | solution.py:217
  377.0 30.0 %attention_backward.1 = (bf16[512,512]{1,0:T(8,128)(2,1)}, bf16[2048,256]{1,0:T(8,128)(2,1)}, bf16[2048,256]{1,0:T(8,128)(2,1)}) custom-call(s32[8]{0:T(128)} %slots.3, s32[2]{0:T(128)} %pad_add_fusion.place, bf16[512,512]{1,0:T(8,128)(2,1)} %get-tuple-element.208.q_ref.refs_0_, bf16[4096,256]{1,0:T(8,128)(2,1)} %join.11.kv_ref.refs_1_, ...), custom_call_target="tpu_custom_call" | custom-call | flops 32999999488 | bytes 1024 | tf_op jit(solution)/shard_map/attention_backward/pallas_call | solution.py:635
  417.6 3.6 collective-permute-done.59.lower_ref
  432.2 3.5 collective-permute-done.63.refs_1_
  442.3 7.7 %to_features.5 = bf16[512,2048]{1,0:T(8,128)(2,1)} custom-call(bf16[512,768]{1,0:T(8,128)(2,1)} %grad_qkv.1.refs_0_.right_ref, bf16[1024,768]{1,0:T(8,128)(2,1)} %join.9.refs_0_.refs_1_, bf16[1024,768]{1,0:T(8,128)(2,1)} %copy-done.4), custom_call_target="tpu_custom_call" | custom-call | flops 110000000 | bytes 1024 | tf_op jit(solution)/shard_map/to_features/pallas_call | solution.py:850
  450.1 3.7 gradient_part.14
  455.5 5.4 gradient_out.1
  467.9 4.0 gradient_part.15
  471.9 7.8 %collective-permute-done.69.first_ref = bf16[256,2048]{1,0:T(8,128)(2,1)} collective-permute-done((bf16[256,2048]{1,0:T(8,128)(2,1)}, bf16[256,2048]{1,0:T(8,128)(2,1)}, u32[]{:S(2)}, u32[]{:S(2)}) %collective-permute-start.69) | collective-permute-done | bytes 1048608 | tf_op jit(solution)/shard_map/ppermute | solution.py:62
  486.6 3.5 finish_sum.5
  507.4 3.5 finish_sum.6
  510.9 3.6 finish_input.1
  518.5 4.4 collective-permute-start.83
  528.0 3.5 finish_sum.9
  532.0 4.7 collective-permute-done.83
  (386 shorter events, 165.9 us)
Async XLA Ops:
  7.2 54.0 %all-gather.6.cloned.1.call-start = ((), (), s32[]{:S(2)}) async-start(), calls=%async_computation.3 | async-start | bytes 2621440 | tf_op jit(solution)/shard_map/all_gather | solution.py:1124
  7.9 123.2 %all-gather.8.cloned.1.call-start = ((), (), s32[]{:S(2)}) async-start(), calls=%async_computation.7 | async-start | bytes 3932160 | tf_op jit(solution)/shard_map/all_gather | solution.py:1143
  9.8 13.8 %collective-permute-start.4 = (bf16[256,768]{1,0:T(8,128)(2,1)}, bf16[256,768]{1,0:T(8,128)(2,1)S(1)}, u32[]{:S(2)}, u32[]{:S(2)}) collective-permute-start(bf16[256,768]{1,0:T(8,128)(2,1)} %join.8.refs_0_), channel_id=1, source_target_pairs={{0,16},{4,20},{8,24},{12,28},{16,0},{20,4},{24,8},{28,12},{1,17},{... | collective-permute-start | bytes 1179656 | tf_op jit(solution)/shard_map/ppermute | solution.py:62
  11.8 49.3 %collective-permute-start.8 = (bf16[256,2048]{1,0:T(8,128)(2,1)}, bf16[256,2048]{1,0:T(8,128)(2,1)S(1)}, u32[]{:S(2)}, u32[]{:S(2)}) collective-permute-start(bf16[256,2048]{1,0:T(8,128)(2,1)} %refs_0_.3), channel_id=1, source_target_pairs={{0,8},{4,12},{8,0},{12,4},{16,24},{20,28},{24,16},{28,20},{1,9},{5... | collective-permute-start | bytes 3145736 | tf_op jit(solution)/shard_map/ppermute | solution.py:62
  13.3 47.8 %collective-permute-start.9 = (bf16[256,2048]{1,0:T(8,128)(2,1)}, bf16[256,2048]{1,0:T(8,128)(2,1)}, u32[]{:S(2)}, u32[]{:S(2)}) collective-permute-start(bf16[256,2048]{1,0:T(8,128)(2,1)} %refs_0_.3), channel_id=1, source_target_pairs={{0,16},{4,20},{8,24},{12,28},{16,0},{20,4},{24,8},{28,12},{1,17},{... | collective-permute-start | bytes 3145736 | tf_op jit(solution)/shard_map/ppermute | solution.py:62
  15.2 41.0 %collective-permute-start = (bf16[1,2,256]{2,1,0:T(2,128)(2,1)S(1)}, bf16[1,2,256]{2,1,0:T(2,128)(2,1)S(1)}, u32[]{:S(2)}, u32[]{:S(2)}) collective-permute-start(bf16[1,2,256]{2,1,0:T(2,128)(2,1)S(1)} %maximum_bitcast_fusion.1), channel_id=1, source_target_pairs={{0,8},{4,12},{8,0},{12,4},{16,24},{20,28},{24,16},{28,20},{1,9},{5... | collective-permute-start | bytes 3080 | tf_op jit(solution)/shard_map/ppermute | solution.py:62
  22.0 25.6 %collective-permute-start.5 = (bf16[128,768]{1,0:T(8,128)(2,1)S(1)}, bf16[128,768]{1,0:T(8,128)(2,1)S(1)}, u32[]{:S(2)}, u32[]{:S(2)}) collective-permute-start(bf16[128,768]{1,0:T(8,128)(2,1)S(1)} %slice.128), channel_id=1, source_target_pairs={{0,16},{4,20},{8,24},{12,28},{16,0},{20,4},{24,8},{28,12},{1,17},{... | collective-permute-start | bytes 589832 | tf_op jit(solution)/shard_map/ppermute | solution.py:62
  23.6 24.0 %collective-permute-start.6 = (bf16[128,768]{1,0:T(8,128)(2,1)S(1)}, bf16[128,768]{1,0:T(8,128)(2,1)S(1)}, u32[]{:S(2)}, u32[]{:S(2)}) collective-permute-start(bf16[128,768]{1,0:T(8,128)(2,1)S(1)} %slice.129), channel_id=1, source_target_pairs={{0,8},{4,12},{8,0},{12,4},{16,24},{20,28},{24,16},{28,20},{1,9},{5... | collective-permute-start | bytes 589832 | tf_op jit(solution)/shard_map/ppermute | solution.py:62
  61.3 125.0 %all-gather.10.cloned.1.call-start = ((), (), s32[]{:S(2)}) async-start(), calls=%async_computation.8 | async-start | bytes 2621440 | tf_op jit(solution)/shard_map/all_gather | solution.py:1158
  92.1 27.8 %collective-permute-start.15 = (bf16[128,2048]{1,0:T(8,128)(2,1)S(1)}, bf16[128,2048]{1,0:T(8,128)(2,1)S(1)}, u32[]{:S(2)}, u32[]{:S(2)}) collective-permute-start(bf16[128,2048]{1,0:T(8,128)(2,1)S(1)} %slice.101), channel_id=1, source_target_pairs={{0,16},{4,20},{8,24},{12,28},{16,0},{20,4},{24,8},{28,12},{1,17},{... | collective-permute-start | bytes 1572872 | tf_op jit(solution)/shard_map/ppermute | solution.py:62
  94.5 25.4 %collective-permute-start.16 = (bf16[128,2048]{1,0:T(8,128)(2,1)S(1)}, bf16[128,2048]{1,0:T(8,128)(2,1)S(1)}, u32[]{:S(2)}, u32[]{:S(2)}) collective-permute-start(bf16[128,2048]{1,0:T(8,128)(2,1)S(1)} %slice.102), channel_id=1, source_target_pairs={{0,8},{4,12},{8,0},{12,4},{16,24},{20,28},{24,16},{28,20},{1,9},{5... | collective-permute-start | bytes 1572872 | tf_op jit(solution)/shard_map/ppermute | solution.py:62
  99.0 32.0 %collective-permute-start.17 = (bf16[256,2048]{1,0:T(8,128)(2,1)S(1)}, bf16[256,2048]{1,0:T(8,128)(2,1)S(1)}, u32[]{:S(2)}, u32[]{:S(2)}) collective-permute-start(bf16[256,2048]{1,0:T(8,128)(2,1)S(1)} %copy-done.20), channel_id=1, source_target_pairs={{0,8},{4,12},{8,0},{12,4},{16,24},{20,28},{24,16},{28,20},{1,9},{5... | collective-permute-start | bytes 3145736 | tf_op jit(solution)/shard_map/ppermute | solution.py:62
  100.2 30.8 %collective-permute-start.18 = (bf16[256,2048]{1,0:T(8,128)(2,1)S(1)}, bf16[256,2048]{1,0:T(8,128)(2,1)}, u32[]{:S(2)}, u32[]{:S(2)}) collective-permute-start(bf16[256,2048]{1,0:T(8,128)(2,1)S(1)} %copy-done.20), channel_id=1, source_target_pairs={{0,16},{4,20},{8,24},{12,28},{16,0},{20,4},{24,8},{28,12},{1,17},{... | collective-permute-start | bytes 3145736 | tf_op jit(solution)/shard_map/ppermute | solution.py:62
  134.8 51.5 %collective-permute-start.25 = (bf16[1024,2048]{1,0:T(8,128)(2,1)}, bf16[1024,2048]{1,0:T(8,128)(2,1)}, u32[]{:S(2)}, u32[]{:S(2)}) collective-permute-start(bf16[1024,2048]{1,0:T(8,128)(2,1)} %join.12.refs_0_.refs_2_), channel_id=1, source_target_pairs={{0,4},{4,0},{8,12},{12,8},{16,20},{20,16},{24,28},{28,24},{1,5},{5... | collective-permute-start | bytes 12582920 | tf_op jit(solution)/shard_map/ppermute | solution.py:62
  134.9 210.2 %reduce-scatter.4.cloned.1.call-start = ((), (), s32[]{:S(2)}) async-start(), calls=%async_computation.4 | async-start | bytes 2621440 | tf_op jit(solution)/shard_map/reduce_scatter | solution.py:1187
  137.5 26.0 %collective-permute-start.19 = (bf16[4,256,512]{2,1,0:T(8,128)(2,1)S(1)}, bf16[4,256,512]{2,1,0:T(8,128)(2,1)S(1)}, u32[]{:S(2)}, u32[]{:S(2)}) collective-permute-start(bf16[4,256,512]{2,1,0:T(8,128)(2,1)S(1)} %reshape.173.refs_0_), channel_id=1, source_target_pairs={{0,8},{4,12},{8,0},{12,4},{16,24},{20,28},{24,16},{28,20},{1,9},{5... | collective-permute-start | bytes 3145736 | tf_op jit(solution)/shard_map/ppermute | solution.py:62
  138.4 26.0 %collective-permute-start.21 = (bf16[4,256,512]{2,1,0:T(8,128)(2,1)S(1)}, bf16[4,256,512]{2,1,0:T(8,128)(2,1)S(1)}, u32[]{:S(2)}, u32[]{:S(2)}) collective-permute-start(bf16[4,256,512]{2,1,0:T(8,128)(2,1)S(1)} %reshape.173.refs_0_), channel_id=1, source_target_pairs={{0,16},{4,20},{8,24},{12,28},{16,0},{20,4},{24,8},{28,12},{1,17},{... | collective-permute-start | bytes 3145736 | tf_op jit(solution)/shard_map/ppermute | solution.py:62
  139.9 35.7 %collective-permute-start.23 = (bf16[128,2048]{1,0:T(8,128)(2,1)S(1)}, bf16[128,2048]{1,0:T(8,128)(2,1)S(1)}, u32[]{:S(2)}, u32[]{:S(2)}) collective-permute-start(bf16[128,2048]{1,0:T(8,128)(2,1)S(1)} %slice.107), channel_id=1, source_target_pairs={{0,16},{4,20},{8,24},{12,28},{16,0},{20,4},{24,8},{28,12},{1,17},{... | collective-permute-start | bytes 1572872 | tf_op jit(solution)/shard_map/ppermute | solution.py:62
  141.7 34.0 %collective-permute-start.24 = (bf16[128,2048]{1,0:T(8,128)(2,1)S(1)}, bf16[128,2048]{1,0:T(8,128)(2,1)}, u32[]{:S(2)}, u32[]{:S(2)}) collective-permute-start(bf16[128,2048]{1,0:T(8,128)(2,1)S(1)} %slice.108), channel_id=1, source_target_pairs={{0,8},{4,12},{8,0},{12,4},{16,24},{20,28},{24,16},{28,20},{1,9},{5... | collective-permute-start | bytes 1572872 | tf_op jit(solution)/shard_map/ppermute | solution.py:62
  163.5 22.8 %collective-permute-start.20 = (bf16[4,128,512]{2,1,0:T(8,128)(2,1)S(1)}, bf16[4,128,512]{2,1,0:T(8,128)(2,1)}, u32[]{:S(2)}, u32[]{:S(2)}) collective-permute-start(bf16[4,128,512]{2,1,0:T(8,128)(2,1)S(1)} %slice.132), channel_id=1, source_target_pairs={{0,16},{4,20},{8,24},{12,28},{16,0},{20,4},{24,8},{28,12},{1,17},{... | collective-permute-start | bytes 1572872 | tf_op jit(solution)/shard_map/ppermute | solution.py:62
  165.5 20.8 %collective-permute-start.22 = (bf16[4,128,512]{2,1,0:T(8,128)(2,1)S(1)}, bf16[4,128,512]{2,1,0:T(8,128)(2,1)}, u32[]{:S(2)}, u32[]{:S(2)}) collective-permute-start(bf16[4,128,512]{2,1,0:T(8,128)(2,1)S(1)} %slice.133), channel_id=1, source_target_pairs={{0,8},{4,12},{8,0},{12,4},{16,24},{20,28},{24,16},{28,20},{1,9},{5... | collective-permute-start | bytes 1572872 | tf_op jit(solution)/shard_map/ppermute | solution.py:62
  189.9 25.6 %collective-permute-start.27 = (bf16[256,2048]{1,0:T(8,128)(2,1)S(1)}, bf16[256,2048]{1,0:T(8,128)(2,1)S(1)}, u32[]{:S(2)}, u32[]{:S(2)}) collective-permute-start(bf16[256,2048]{1,0:T(8,128)(2,1)S(1)} %copy-done.21), channel_id=1, source_target_pairs={{0,8},{4,12},{8,0},{12,4},{16,24},{20,28},{24,16},{28,20},{1,9},{5... | collective-permute-start | bytes 3145736 | tf_op jit(solution)/shard_map/ppermute | solution.py:62
  191.1 25.2 %collective-permute-start.28 = (bf16[256,2048]{1,0:T(8,128)(2,1)S(1)}, bf16[256,2048]{1,0:T(8,128)(2,1)S(1)}, u32[]{:S(2)}, u32[]{:S(2)}) collective-permute-start(bf16[256,2048]{1,0:T(8,128)(2,1)S(1)} %copy-done.21), channel_id=1, source_target_pairs={{0,16},{4,20},{8,24},{12,28},{16,0},{20,4},{24,8},{28,12},{1,17},{... | collective-permute-start | bytes 3145736 | tf_op jit(solution)/shard_map/ppermute | solution.py:62
  280.2 158.8 %reduce-scatter.6.cloned.1.call-start = ((), (), s32[]{:S(2)}) async-start(), calls=%async_computation.5 | async-start | bytes 2621440 | tf_op jit(solution)/shard_map/reduce_scatter | solution.py:1221
  293.1 14.3 %collective-permute-start.42 = (bf16[256,2048]{1,0:T(8,128)(2,1)}, bf16[256,2048]{1,0:T(8,128)(2,1)}, u32[]{:S(2)}, u32[]{:S(2)}) collective-permute-start(bf16[256,2048]{1,0:T(8,128)(2,1)} %get-tuple-element.264), channel_id=1, source_target_pairs={{0,4},{4,0},{8,12},{12,8},{16,20},{20,16},{24,28},{28,24},{1,5},{5... | collective-permute-start | bytes 3145736 | tf_op jit(solution)/shard_map/ppermute | solution.py:62
  299.5 17.0 %collective-permute-start.46 = (bf16[256,2048]{1,0:T(8,128)(2,1)}, bf16[256,2048]{1,0:T(8,128)(2,1)S(1)}, u32[]{:S(2)}, u32[]{:S(2)}) collective-permute-start(bf16[256,2048]{1,0:T(8,128)(2,1)} %get-tuple-element.273), channel_id=1, source_target_pairs={{0,4},{4,0},{8,12},{12,8},{16,20},{20,16},{24,28},{28,24},{1,5},{5... | collective-permute-start | bytes 3145736 | tf_op jit(solution)/shard_map/ppermute | solution.py:62
  299.7 17.9 %collective-permute-start.47 = (bf16[256,2048]{1,0:T(8,128)(2,1)}, bf16[256,2048]{1,0:T(8,128)(2,1)S(1)}, u32[]{:S(2)}, u32[]{:S(2)}) collective-permute-start(bf16[256,2048]{1,0:T(8,128)(2,1)} %get-tuple-element.274), channel_id=1, source_target_pairs={{0,4},{4,0},{8,12},{12,8},{16,20},{20,16},{24,28},{28,24},{1,5},{5... | collective-permute-start | bytes 3145736 | tf_op jit(solution)/shard_map/ppermute | solution.py:62
  300.1 18.4 %collective-permute-start.48 = (bf16[256,2048]{1,0:T(8,128)(2,1)}, bf16[256,2048]{1,0:T(8,128)(2,1)}, u32[]{:S(2)}, u32[]{:S(2)}) collective-permute-start(bf16[256,2048]{1,0:T(8,128)(2,1)} %get-tuple-element.275), channel_id=1, source_target_pairs={{0,4},{4,0},{8,12},{12,8},{16,20},{20,16},{24,28},{28,24},{1,5},{5... | collective-permute-start | bytes 3145736 | tf_op jit(solution)/shard_map/ppermute | solution.py:62
  307.4 18.9 %collective-permute-start.37 = (bf16[128,2048]{1,0:T(8,128)(2,1)}, bf16[128,2048]{1,0:T(8,128)(2,1)S(1)}, u32[]{:S(2)}, u32[]{:S(2)}) collective-permute-start(bf16[128,2048]{1,0:T(8,128)(2,1)} %get-tuple-element.256), channel_id=1, source_target_pairs={{0,16},{4,20},{8,24},{12,28},{16,0},{20,4},{24,8},{28,12},{1,17},{... | collective-permute-start | bytes 1572872 | tf_op jit(solution)/shard_map/ppermute | solution.py:62
  308.7 29.7 %collective-permute-start.38 = (bf16[128,2048]{1,0:T(8,128)(2,1)}, bf16[128,2048]{1,0:T(8,128)(2,1)}, u32[]{:S(2)}, u32[]{:S(2)}) collective-permute-start(bf16[128,2048]{1,0:T(8,128)(2,1)} %get-tuple-element.257), channel_id=1, source_target_pairs={{0,8},{4,12},{8,0},{12,4},{16,24},{20,28},{24,16},{28,20},{1,9},{5... | collective-permute-start | bytes 1572872 | tf_op jit(solution)/shard_map/ppermute | solution.py:62
  316.5 25.2 %collective-permute-start.43 = (bf16[128,2048]{1,0:T(8,128)(2,1)}, bf16[128,2048]{1,0:T(8,128)(2,1)}, u32[]{:S(2)}, u32[]{:S(2)}) collective-permute-start(bf16[128,2048]{1,0:T(8,128)(2,1)} %get-tuple-element.267), channel_id=1, source_target_pairs={{0,16},{4,20},{8,24},{12,28},{16,0},{20,4},{24,8},{28,12},{1,17},{... | collective-permute-start | bytes 1572872 | tf_op jit(solution)/shard_map/ppermute | solution.py:62
  317.6 24.2 %collective-permute-start.44 = (bf16[128,2048]{1,0:T(8,128)(2,1)}, bf16[128,2048]{1,0:T(8,128)(2,1)}, u32[]{:S(2)}, u32[]{:S(2)}) collective-permute-start(bf16[128,2048]{1,0:T(8,128)(2,1)} %get-tuple-element.268), channel_id=1, source_target_pairs={{0,8},{4,12},{8,0},{12,4},{16,24},{20,28},{24,16},{28,20},{1,9},{5... | collective-permute-start | bytes 1572872 | tf_op jit(solution)/shard_map/ppermute | solution.py:62
  325.2 19.9 %collective-permute-start.49 = (bf16[128,2048]{1,0:T(8,128)(2,1)}, bf16[128,2048]{1,0:T(8,128)(2,1)S(1)}, u32[]{:S(2)}, u32[]{:S(2)}) collective-permute-start(bf16[128,2048]{1,0:T(8,128)(2,1)} %get-tuple-element.276), channel_id=1, source_target_pairs={{0,16},{4,20},{8,24},{12,28},{16,0},{20,4},{24,8},{28,12},{1,17},{... | collective-permute-start | bytes 1572872 | tf_op jit(solution)/shard_map/ppermute | solution.py:62
  326.3 18.8 %collective-permute-start.50 = (bf16[128,2048]{1,0:T(8,128)(2,1)}, bf16[128,2048]{1,0:T(8,128)(2,1)S(1)}, u32[]{:S(2)}, u32[]{:S(2)}) collective-permute-start(bf16[128,2048]{1,0:T(8,128)(2,1)} %get-tuple-element.277), channel_id=1, source_target_pairs={{0,8},{4,12},{8,0},{12,4},{16,24},{20,28},{24,16},{28,20},{1,9},{5... | collective-permute-start | bytes 1572872 | tf_op jit(solution)/shard_map/ppermute | solution.py:62
  346.0 28.8 %collective-permute-start.54 = (bf16[256,2048]{1,0:T(8,128)(2,1)}, bf16[256,2048]{1,0:T(8,128)(2,1)S(1)}, u32[]{:S(2)}, u32[]{:S(2)}) collective-permute-start(bf16[256,2048]{1,0:T(8,128)(2,1)} %get-tuple-element.283), channel_id=1, source_target_pairs={{0,8},{4,12},{8,0},{12,4},{16,24},{20,28},{24,16},{28,20},{1,9},{5... | collective-permute-start | bytes 3145736 | tf_op jit(solution)/shard_map/ppermute | solution.py:62
  347.1 27.7 %collective-permute-start.55 = (bf16[256,2048]{1,0:T(8,128)(2,1)}, bf16[256,2048]{1,0:T(8,128)(2,1)}, u32[]{:S(2)}, u32[]{:S(2)}) collective-permute-start(bf16[256,2048]{1,0:T(8,128)(2,1)} %get-tuple-element.284), channel_id=1, source_target_pairs={{0,16},{4,20},{8,24},{12,28},{16,0},{20,4},{24,8},{28,12},{1,17},{... | collective-permute-start | bytes 3145736 | tf_op jit(solution)/shard_map/ppermute | solution.py:62
  374.8 136.1 %reduce-scatter.8.cloned.1.call-start = ((), (), s32[]{:S(2)}) async-start(), calls=%async_computation.6 | async-start | bytes 2621440 | tf_op jit(solution)/shard_map/reduce_scatter | solution.py:1237
  375.1 33.9 %collective-permute-start.56 = (bf16[256,2048]{1,0:T(8,128)(2,1)}, bf16[256,2048]{1,0:T(8,128)(2,1)S(1)}, u32[]{:S(2)}, u32[]{:S(2)}) collective-permute-start(bf16[256,2048]{1,0:T(8,128)(2,1)} %get-tuple-element.301), channel_id=1, source_target_pairs={{0,8},{4,12},{8,0},{12,4},{16,24},{20,28},{24,16},{28,20},{1,9},{5... | collective-permute-start | bytes 3145736 | tf_op jit(solution)/shard_map/ppermute | solution.py:62
  375.8 33.1 %collective-permute-start.57 = (bf16[256,2048]{1,0:T(8,128)(2,1)}, bf16[256,2048]{1,0:T(8,128)(2,1)S(1)}, u32[]{:S(2)}, u32[]{:S(2)}) collective-permute-start(bf16[256,2048]{1,0:T(8,128)(2,1)} %get-tuple-element.302), channel_id=1, source_target_pairs={{0,16},{4,20},{8,24},{12,28},{16,0},{20,4},{24,8},{28,12},{1,17},{... | collective-permute-start | bytes 3145736 | tf_op jit(solution)/shard_map/ppermute | solution.py:62
  424.3 14.5 %collective-permute-start.61 = (bf16[512,256]{1,0:T(8,128)(2,1)}, bf16[512,256]{1,0:T(8,128)(2,1)S(1)}, u32[]{:S(2)}, u32[]{:S(2)}) collective-permute-start(bf16[512,256]{1,0:T(8,128)(2,1)} %get-tuple-element.310), channel_id=1, source_target_pairs={{0,8},{4,12},{8,0},{12,4},{16,24},{20,28},{24,16},{28,20},{1,9},{5... | collective-permute-start | bytes 786440 | tf_op jit(solution)/shard_map/ppermute | solution.py:62
  453.8 14.1 %collective-permute-start.67 = (bf16[1024,768]{1,0:T(8,128)(2,1)}, bf16[1024,768]{1,0:T(8,128)(2,1)}, u32[]{:S(2)}, u32[]{:S(2)}) collective-permute-start(bf16[1024,768]{1,0:T(8,128)(2,1)} %gradient_part.14), channel_id=1, source_target_pairs={{0,4},{4,0},{8,12},{12,8},{16,20},{20,16},{24,28},{28,24},{1,5},{5... | collective-permute-start | bytes 4718600 | tf_op jit(solution)/shard_map/ppermute | solution.py:62
  453.8 25.9 %collective-permute-start.69 = (bf16[256,2048]{1,0:T(8,128)(2,1)}, bf16[256,2048]{1,0:T(8,128)(2,1)}, u32[]{:S(2)}, u32[]{:S(2)}) collective-permute-start(bf16[256,2048]{1,0:T(8,128)(2,1)} %get-tuple-element.338), channel_id=1, source_target_pairs={{0,8},{4,12},{8,0},{12,4},{16,24},{20,28},{24,16},{28,20},{1,9},{5... | collective-permute-start | bytes 3145736 | tf_op jit(solution)/shard_map/ppermute | solution.py:62
  454.7 25.5 %collective-permute-start.70 = (bf16[256,2048]{1,0:T(8,128)(2,1)}, bf16[256,2048]{1,0:T(8,128)(2,1)}, u32[]{:S(2)}, u32[]{:S(2)}) collective-permute-start(bf16[256,2048]{1,0:T(8,128)(2,1)} %get-tuple-element.339), channel_id=1, source_target_pairs={{0,16},{4,20},{8,24},{12,28},{16,0},{20,4},{24,8},{28,12},{1,17},{... | collective-permute-start | bytes 3145736 | tf_op jit(solution)/shard_map/ppermute | solution.py:62
  497.7 16.8 %collective-permute-start.79 = (bf16[256,768]{1,0:T(8,128)(2,1)}, bf16[256,768]{1,0:T(8,128)(2,1)S(1)}, u32[]{:S(2)}, u32[]{:S(2)}) collective-permute-start(bf16[256,768]{1,0:T(8,128)(2,1)} %get-tuple-element.371), channel_id=1, source_target_pairs={{0,8},{4,12},{8,0},{12,4},{16,24},{20,28},{24,16},{28,20},{1,9},{5... | collective-permute-start | bytes 1179656 | tf_op jit(solution)/shard_map/ppermute | solution.py:62
  498.9 15.7 %collective-permute-start.80 = (bf16[256,768]{1,0:T(8,128)(2,1)}, bf16[256,768]{1,0:T(8,128)(2,1)S(1)}, u32[]{:S(2)}, u32[]{:S(2)}) collective-permute-start(bf16[256,768]{1,0:T(8,128)(2,1)} %get-tuple-element.372), channel_id=1, source_target_pairs={{0,16},{4,20},{8,24},{12,28},{16,0},{20,4},{24,8},{28,12},{1,17},{... | collective-permute-start | bytes 1179656 | tf_op jit(solution)/shard_map/ppermute | solution.py:62
  499.9 14.7 %collective-permute-start.81 = (bf16[256,512]{1,0:T(8,128)(2,1)}, bf16[256,512]{1,0:T(8,128)(2,1)S(1)}, u32[]{:S(2)}, u32[]{:S(2)}) collective-permute-start(bf16[256,512]{1,0:T(8,128)(2,1)} %get-tuple-element.373), channel_id=1, source_target_pairs={{0,8},{4,12},{8,0},{12,4},{16,24},{20,28},{24,16},{28,20},{1,9},{5... | collective-permute-start | bytes 786440 | tf_op jit(solution)/shard_map/ppermute | solution.py:62
  500.6 14.0 %collective-permute-start.82 = (bf16[256,512]{1,0:T(8,128)(2,1)}, bf16[256,512]{1,0:T(8,128)(2,1)S(1)}, u32[]{:S(2)}, u32[]{:S(2)}) collective-permute-start(bf16[256,512]{1,0:T(8,128)(2,1)} %get-tuple-element.374), channel_id=1, source_target_pairs={{0,16},{4,20},{8,24},{12,28},{16,0},{20,4},{24,8},{28,12},{1,17},{... | collective-permute-start | bytes 786440 | tf_op jit(solution)/shard_map/ppermute | solution.py:62
  518.5 18.2 %collective-permute-start.83 = (bf16[256,512]{1,0:T(8,128)(2,1)S(1)}, bf16[256,512]{1,0:T(8,128)(2,1)S(1)}, u32[]{:S(2)}, u32[]{:S(2)}) collective-permute-start(bf16[256,512]{1,0:T(8,128)(2,1)S(1)} %convert_element_type.47), channel_id=1, source_target_pairs={{0,0},{1,8},{2,16},{3,24},{4,4},{5,12},{6,20},{7,28},{8,1},{9,9},{... | collective-permute-start | bytes 786440 | tf_op jit(solution)/shard_map/ppermute | solution.py:968
  (111 other events, 956.5 us)
Sparse Core Ops, SparseCore 0:
  9.6 47.1 all-gather.5
  61.4 64.9 all-gather.7
  135.1 46.6 all-gather.9
  280.3 44.5 reduce-scatter.3
  374.9 42.6 reduce-scatter.5
  450.2 44.4 reduce-scatter.7
